TPU v7x, 32 devices: a whole 2x2x4 slice. The times are simulated.
32 devices in a mesh: section: 2 (over core), dp: 16 (over z, y, x).
Axes of the slice: x: 2, y: 2, z: 4, core: 2. Of those that a mesh axis runs over, the one named last changes fastest.
Arguments:
- pixels: bfloat16 [8, 2048, 768], P(None, 'dp'), may hold values from -4 to 4
- codes_top: int32 [8, 256, 32], P(None, 'dp'), may hold values from 0 to 511
- codes_bottom: int32 [8, 512, 64], P(None, 'dp'), may hold values from 0 to 511
- valid_rows: int32 [8, 8], replicated, may hold values from 64 to 256
- dead_codes: int32 [2, 8], replicated, may hold values from 0 to 511, as said below
- dead_source: int32 [2, 8], replicated, may hold values from 0 to 262143, as said below
- w_conv: float32 [3, 1152, 64], replicated, may hold values from -0.1875 to 0.1875
- w_res_out: float32 [3, 64, 128], replicated, may hold values from -0.75 to 0.75
- w_from_code: float32 [5, 64, 128], replicated, may hold values from -0.75 to 0.75
- w_to_code: float32 [2, 128, 64], replicated, may hold values from -0.5 to 0.5
- w_pixel: float32 [2, 48, 128], replicated, may hold values from -0.5 to 0.5
- w_down: float32 [4, 128, 128], replicated, may hold values from -0.25 to 0.25
- m_conv: float32 [3, 1152, 64], replicated, may hold values from -9.536743e-07 to 9.536743e-07
- m_res_out: float32 [3, 64, 128], replicated, may hold values from -9.536743e-07 to 9.536743e-07
- m_from_code: float32 [5, 64, 128], replicated, may hold values from -9.536743e-07 to 9.536743e-07
- m_to_code: float32 [2, 128, 64], replicated, may hold values from -9.536743e-07 to 9.536743e-07
- m_pixel: float32 [2, 48, 128], replicated, may hold values from -9.536743e-07 to 9.536743e-07
- m_down: float32 [4, 128, 128], replicated, may hold values from -9.536743e-07 to 9.536743e-07
- v_conv: float32 [3, 1152, 64], replicated, may hold values from 2.625168e-15 to 1.0500672e-14
- v_res_out: float32 [3, 64, 128], replicated, may hold values from 2.625168e-15 to 1.0500672e-14
- v_from_code: float32 [5, 64, 128], replicated, may hold values from 2.625168e-15 to 1.0500672e-14
- v_to_code: float32 [2, 128, 64], replicated, may hold values from 2.625168e-15 to 1.0500672e-14
- v_pixel: float32 [2, 48, 128], replicated, may hold values from 2.625168e-15 to 1.0500672e-14
- v_down: float32 [4, 128, 128], replicated, may hold values from 2.625168e-15 to 1.0500672e-14
- codebook: float32 [2, 512, 64], replicated, may hold values from -5 to 5
- ema_count: float32 [2, 512], replicated, may hold values from 5 to 50
- ema_sum: float32 [2, 512, 64], replicated, may hold values from -60 to 60
Outputs:
- grad_norm: float32 [], replicated
- loss_pair: float32 [2], replicated
- new_conv: float32 [3, 1152, 64], replicated
- new_res_out: float32 [3, 64, 128], replicated
- new_from_code: float32 [5, 64, 128], replicated
- new_to_code: float32 [2, 128, 64], replicated
- new_pixel: float32 [2, 48, 128], replicated
- new_down: float32 [4, 128, 128], replicated
- mom_conv: float32 [3, 1152, 64], replicated
- mom_res_out: float32 [3, 64, 128], replicated
- mom_from_code: float32 [5, 64, 128], replicated
- mom_to_code: float32 [2, 128, 64], replicated
- mom_pixel: float32 [2, 48, 128], replicated
- mom_down: float32 [4, 128, 128], replicated
- sec_conv: float32 [3, 1152, 64], replicated
- sec_res_out: float32 [3, 64, 128], replicated
- sec_from_code: float32 [5, 64, 128], replicated
- sec_to_code: float32 [2, 128, 64], replicated
- sec_pixel: float32 [2, 48, 128], replicated
- sec_down: float32 [4, 128, 128], replicated
- low_conv: bfloat16 [3, 1152, 64], replicated
- low_res_out: bfloat16 [3, 64, 128], replicated
- low_from_code: bfloat16 [5, 64, 128], replicated
- low_to_code: bfloat16 [2, 128, 64], replicated
- low_pixel: bfloat16 [2, 48, 128], replicated
- low_down: bfloat16 [4, 128, 128], replicated
- new_book: float32 [2, 512, 64], replicated
- new_count: float32 [2, 512], replicated
- new_sum: float32 [2, 512, 64], replicated
Inputs may be any that keep to these rules, and one draw needn't show every extreme that they name: `dead_codes`: each row holds 8 different codes of one level, row 0 the top level and row 1 the bottom. `dead_source`: row 0 indexes top positions in (micro-batch, row, column) order, below 8 * 8 * (32) squared, one of them 0; row 1 bottom positions, below 8 * 8 * (64) squared, one of them the last.
All inputs are finite; a program needn't handle non-finite values.
Results may differ from a plain program's by a relative error of at most 0.001.
The roundings to bfloat16 on the way count: a program that leaves them out, or rounds other values in their place, can miss the bound.
Values may be sent and summed in bfloat16 or wider, within the bound.
A program may use at most 576 MiB of HBM per device.

v0:
```python
import jax
import jax.numpy as jnp
from jax import lax
from jax.sharding import PartitionSpec as P

STEP = 10


COMMIT_WEIGHT = 0.25
CODE_DECAY = 0.9
CLIP_NORM = 0.001
LEARN_RATE = 0.03
MOMENT_ONE = 0.9
MOMENT_TWO = 0.999
WEIGHT_DECAY = 0.01
ADAM_EPSILON = 1e-08
HIGHEST = lax.Precision.HIGHEST


def with_halo(block, sides, width):
    for axis, dim in sides:
        count = lax.axis_size(axis)
        forward = [(i, i + 1) for i in range(count - 1)]
        backward = [(target, source) for source, target in forward]
        low = lax.ppermute(
            lax.slice_in_dim(block, block.shape[dim] - width, None, axis=dim), axis, forward
        )
        high = lax.ppermute(lax.slice_in_dim(block, 0, width, axis=dim), axis, backward)
        block = jnp.concatenate([low, block, high], axis=dim)
    return block


def from_behind(x, axis, by):
    devices = lax.axis_size(axis)
    pairs = [(i, i + by) for i in range(devices) if 0 <= i + by < devices]
    return lax.ppermute(x, axis, pairs)


def matmul(x, w):
    return jnp.dot(x, w, preferred_element_type=jnp.float32)


def weight_grad(x, grad):
    return lax.dot_general(
        x, grad, (((0, 1), (0, 1)), ((), ())), preferred_element_type=jnp.float32
    )


def silu_slope(preact):
    sigmoid = jax.nn.sigmoid(preact)
    return sigmoid * (1.0 + preact * (1.0 - sigmoid))


def patchify(picture):
    num_rows = picture.shape[0] // 4
    num_cols = picture.shape[1] // 12
    return (
        picture.reshape(num_rows, 4, num_cols, 4, 3)
        .transpose(0, 2, 1, 3, 4)
        .reshape(num_rows, num_cols, 48)
    )


def to_blocks(x):
    num_rows, num_cols, channels = x.shape
    return (
        x.reshape(num_rows // 2, 2, num_cols // 2, 2, channels)
        .transpose(0, 2, 1, 3, 4)
        .reshape(num_rows // 2, num_cols // 2, 4 * channels)
    )


def from_blocks(x, channels):
    num_rows, num_cols = (x.shape[0], x.shape[1])
    return (
        x.reshape(num_rows, num_cols, 2, 2, channels)
        .transpose(0, 2, 1, 3, 4)
        .reshape(2 * num_rows, 2 * num_cols, channels)
    )


def nine_taps(padded):
    height = padded.shape[0] - 2
    across = padded.shape[1]
    widened = jnp.pad(padded, ((0, 0), (1, 1), (0, 0)))
    return jnp.concatenate(
        [widened[i : i + height, j : j + across] for i in range(3) for j in range(3)], axis=2
    )


def flipped(kernel):
    inner = kernel.shape[0] // 9
    return (
        jnp.flip(kernel.reshape(9, inner, kernel.shape[1]), 0)
        .transpose(0, 2, 1)
        .reshape(9 * kernel.shape[1], inner)
    )


def fence_rows(padded, edge_keep):
    height = padded.shape[0]
    row_ids = jnp.arange(height)
    scaling = jnp.where(
        row_ids == 0, edge_keep[0], jnp.where(row_ids == height - 1, edge_keep[1], 1.0)
    )
    return padded * scaling.astype(padded.dtype)[:, None, None]


def top_rows(x, edge_keep):
    return fence_rows(with_halo(x, (("dp", 0),), 1), edge_keep)


def bottom_rows(x, edge_keep):
    return fence_rows(with_halo(x, (("dp", 0),), 1), edge_keep)


def top_grads(x, edge_keep):
    return fence_rows(with_halo(x, (("dp", 0),), 1), edge_keep)


def bottom_grads(x, edge_keep):
    return fence_rows(with_halo(x, (("dp", 0),), 1), edge_keep)


def sectioned(flag, work):
    return lax.cond(flag, work, lambda: jax.tree.map(jnp.zeros_like, work()))


def block_front(padded, resid, kernel, w_out):
    patches = nine_taps(padded)
    preact = matmul(patches, kernel)
    hidden = jax.nn.silu(preact).astype(jnp.bfloat16)
    return (patches, preact, hidden, resid + matmul(hidden, w_out))


def block_back_first(grad_out, preact, hidden, w_out):
    grad_low = grad_out.astype(jnp.bfloat16)
    grad_pre = (matmul(grad_low, w_out.T) * silu_slope(preact)).astype(jnp.bfloat16)
    return (grad_pre, weight_grad(hidden, grad_low))


def block_back_second(grad_out, patches, grad_pre, padded, kernel):
    return (grad_out + matmul(nine_taps(padded), flipped(kernel)), weight_grad(patches, grad_pre))


def adamw(weight, grad, first, second):
    first = MOMENT_ONE * first + (1.0 - MOMENT_ONE) * grad
    second = MOMENT_TWO * second + (1.0 - MOMENT_TWO) * grad * grad
    update = (
        first
        / (1.0 - MOMENT_ONE**STEP)
        / (jnp.sqrt(second / (1.0 - MOMENT_TWO**STEP)) + ADAM_EPSILON)
    )
    return (weight - LEARN_RATE * (update + WEIGHT_DECAY * weight), first, second)


def body(
    pixels,
    codes_top,
    codes_bottom,
    valid_rows,
    dead_codes,
    dead_source,
    w_conv,
    w_res_out,
    w_from_code,
    w_to_code,
    w_pixel,
    w_down,
    m_conv,
    m_res_out,
    m_from_code,
    m_to_code,
    m_pixel,
    m_down,
    v_conv,
    v_res_out,
    v_from_code,
    v_to_code,
    v_pixel,
    v_down,
    codebook,
    ema_count,
    ema_sum,
):
    narrow = jnp.bfloat16
    single = jnp.float32
    weights = (w_conv, w_res_out, w_from_code, w_to_code, w_pixel, w_down)
    kernels, outputs, from_code, to_code, pixel_maps, down_maps = [
        w.astype(narrow) for w in weights
    ]
    batches, pixel_rows, row_lanes = pixels.shape
    image_width = row_lanes // 3
    channels = pixel_maps.shape[2]
    embed_dim = from_code.shape[1]
    book_size = codebook.shape[1]
    per_image = image_width // pixel_rows
    section_id = lax.axis_index("section")
    dp_index = lax.axis_index("dp")
    devices_dp = lax.axis_size("dp")
    row_block = dp_index % per_image
    image_id = dp_index // per_image
    on_top = section_id == 0
    on_bottom = section_id == 1
    edge_keep = ((row_block != 0).astype(single), (row_block != per_image - 1).astype(single))
    valid_count = 3.0 * image_width * jnp.sum(valid_rows).astype(single)
    loss_slope = 2.0 / valid_count
    up_flat = from_code[1:].transpose(1, 0, 2).reshape(embed_dim, 4 * channels)
    down_flat = down_maps.reshape(4 * channels, channels)
    out_map = pixel_maps[1].T

    def level_stats(latent, code_ids, level_id, batch_id):
        num_rows, num_cols = code_ids.shape
        onehot = (code_ids.reshape(-1)[:, None] == jnp.arange(book_size)[None, :]).astype(single)
        flat_latent = latent.reshape(-1, embed_dim)
        slot_ids = jnp.arange(num_rows * num_cols)
        positions = (
            batch_id * devices_dp * num_rows * num_cols
            + (dp_index * num_rows + slot_ids // num_cols) * num_cols
            + slot_ids % num_cols
        )
        dead_match = (dead_source[level_id][:, None] == positions[None, :]).astype(single)
        code_sums = lax.dot_general(
            onehot, flat_latent, (((0,), (0,)), ((), ())), precision=HIGHEST
        )
        return (
            jnp.sum(onehot, axis=0),
            code_sums,
            jnp.dot(dead_match, flat_latent, precision=HIGHEST),
        )

    def forward_batch(batch_id):
        picture = pixels[batch_id]
        row_ids = row_block * pixel_rows + jnp.arange(pixel_rows)
        limit = lax.dynamic_index_in_dim(valid_rows[batch_id], image_id, keepdims=False)
        pixel_mask = patchify(
            jnp.broadcast_to((row_ids < limit).astype(single)[:, None], (pixel_rows, row_lanes))
        )

        def stem_work():
            patches = patchify(picture)
            preact = matmul(patches, pixel_maps[0])
            return (patches, preact, jax.nn.silu(preact).astype(narrow))

        patches, stem_pre, stem = sectioned(on_top, stem_work)
        top_in = sectioned(on_top, lambda: matmul(to_blocks(stem), down_flat))
        padded_top = top_rows(top_in.astype(narrow), edge_keep)

        def top_work():
            block_out = block_front(padded_top, top_in, kernels[0], outputs[0])
            top_low = block_out[3].astype(narrow)
            latent = matmul(top_low, to_code[0])
            nearest = jnp.take(codebook[0], codes_top[batch_id], axis=0)
            return (
                block_out[:3],
                top_low,
                latent,
                nearest,
                COMMIT_WEIGHT * jnp.sum((latent - nearest) ** 2),
            )

        top_block, top_low, top_latent, top_near, top_commit = sectioned(on_top, top_work)
        quant_top = top_near.astype(narrow)
        stem_recv, quant_recv = from_behind((stem, quant_top), "section", 1)

        def up_work():
            upward = from_blocks(matmul(quant_recv, up_flat), channels)
            return (upward, stem_recv.astype(single) + upward)

        upward, bottom_in = sectioned(on_bottom, up_work)
        padded_bottom = bottom_rows(bottom_in.astype(narrow), edge_keep)

        def bottom_work():
            block_out = block_front(padded_bottom, bottom_in, kernels[1], outputs[1])
            bottom_low = block_out[3].astype(narrow)
            latent = matmul(bottom_low, to_code[1])
            nearest = jnp.take(codebook[1], codes_bottom[batch_id], axis=0)
            quantized = nearest.astype(narrow)
            decode_in = matmul(quantized, from_code[0]) + upward
            return (
                block_out[:3],
                bottom_low,
                latent,
                nearest,
                quantized,
                decode_in,
                COMMIT_WEIGHT * jnp.sum((latent - nearest) ** 2),
            )

        (
            bottom_block,
            bottom_low,
            bottom_latent,
            bottom_near,
            quant_bottom,
            decode_in,
            bottom_commit,
        ) = sectioned(on_bottom, bottom_work)
        padded_decode = bottom_rows(decode_in.astype(narrow), edge_keep)

        def decode_work():
            block_out = block_front(padded_decode, decode_in, kernels[2], outputs[2])
            decode_low = block_out[3].astype(narrow)
            residue = matmul(decode_low, out_map) - patchify(picture).astype(single)
            return (block_out[:3], decode_low, residue, jnp.sum(pixel_mask * residue * residue))

        decode_block, decode_low, residue, squared = sectioned(on_bottom, decode_work)
        top_stats = sectioned(
            on_top, lambda: level_stats(top_latent, codes_top[batch_id], 0, batch_id)
        )
        bottom_stats = sectioned(
            on_bottom, lambda: level_stats(bottom_latent, codes_bottom[batch_id], 1, batch_id)
        )
        saved = dict(
            pixel_mask=pixel_mask,
            patches=patches,
            stem_pre=stem_pre,
            stem=stem,
            top_block=top_block,
            top_low=top_low,
            top_latent=top_latent,
            top_near=top_near,
            quant_recv=quant_recv,
            bottom_block=bottom_block,
            bottom_low=bottom_low,
            bottom_latent=bottom_latent,
            bottom_near=bottom_near,
            quant_bottom=quant_bottom,
            decode_block=decode_block,
            decode_low=decode_low,
            residue=residue,
        )
        return (saved, top_commit + bottom_commit + squared, top_stats, bottom_stats)

    records = [forward_batch(batch_id) for batch_id in range(batches)]
    statistics = [
        jnp.zeros((2, book_size), single),
        jnp.zeros((2, book_size, embed_dim), single),
        jnp.zeros((2, dead_codes.shape[1], embed_dim), single),
    ]
    numerator = jnp.zeros((), single)
    for record in records:
        numerator = numerator + record[1]
        for member in range(3):
            statistics[member] = statistics[member] + jnp.stack(
                [record[2][member], record[3][member]]
            )
    summed_stats = lax.psum(
        (statistics[0], statistics[1], statistics[2], numerator), ("section", "dp")
    )
    gradients = [jnp.zeros_like(w) for w in weights]
    for batch_id in reversed(range(batches)):
        backward_saved = records[batch_id][0]

        def decode_back():
            grad_rebuilt = (
                loss_slope * backward_saved["pixel_mask"] * backward_saved["residue"]
            ).astype(narrow)
            grad_decoded = matmul(grad_rebuilt, pixel_maps[1])
            grad_pre, grad_res = block_back_first(
                grad_decoded,
                backward_saved["decode_block"][1],
                backward_saved["decode_block"][2],
                outputs[2],
            )
            return (
                weight_grad(grad_rebuilt, backward_saved["decode_low"]),
                grad_decoded,
                grad_pre,
                grad_res,
            )

        grad_pixel_out, grad_decoded, grad_pre_decode, grad_res_decode = sectioned(
            on_bottom, decode_back
        )
        padded_grad = bottom_grads(grad_pre_decode, edge_keep)

        def bottom_back():
            grad_in, grad_kernel = block_back_second(
                grad_decoded,
                backward_saved["decode_block"][0],
                grad_pre_decode,
                padded_grad,
                kernels[2],
            )
            grad_low = grad_in.astype(narrow)
            grad_quant = matmul(grad_low, from_code[0].T)
            grad_latent = (
                grad_quant
                + loss_slope
                * COMMIT_WEIGHT
                * (backward_saved["bottom_latent"] - backward_saved["bottom_near"])
            ).astype(narrow)
            grad_bottom = matmul(grad_latent, to_code[1].T)
            grad_pre, grad_res = block_back_first(
                grad_bottom,
                backward_saved["bottom_block"][1],
                backward_saved["bottom_block"][2],
                outputs[1],
            )
            return (
                grad_in,
                grad_kernel,
                weight_grad(backward_saved["quant_bottom"], grad_low),
                weight_grad(backward_saved["bottom_low"], grad_latent),
                grad_bottom,
                grad_pre,
                grad_res,
            )

        (
            grad_in_decode,
            grad_kernel_decode,
            grad_from_zero,
            grad_to_bottom,
            grad_bottom,
            grad_pre_bottom,
            grad_res_bottom,
        ) = sectioned(on_bottom, bottom_back)
        padded_grad_bottom = bottom_grads(grad_pre_bottom, edge_keep)

        def up_back():
            grad_in, grad_kernel = block_back_second(
                grad_bottom,
                backward_saved["bottom_block"][0],
                grad_pre_bottom,
                padded_grad_bottom,
                kernels[1],
            )
            grad_up = to_blocks((grad_in_decode + grad_in).astype(narrow))
            return (
                grad_kernel,
                weight_grad(backward_saved["quant_recv"], grad_up),
                matmul(grad_up, up_flat.T).astype(narrow),
                grad_in.astype(narrow),
            )

        grad_kernel_bottom, grad_up_maps, grad_quant_top, grad_stem = sectioned(on_bottom, up_back)
        stem_back, quant_back = from_behind((grad_stem, grad_quant_top), "section", -1)
        grad_stem_bottom = sectioned(
            on_top,
            lambda: weight_grad(
                backward_saved["patches"],
                (stem_back.astype(single) * silu_slope(backward_saved["stem_pre"])).astype(narrow),
            ),
        )

        def top_back():
            grad_latent = (
                quant_back.astype(single)
                + loss_slope
                * COMMIT_WEIGHT
                * (backward_saved["top_latent"] - backward_saved["top_near"])
            ).astype(narrow)
            grad_top = matmul(grad_latent, to_code[0].T)
            grad_pre, grad_res = block_back_first(
                grad_top, backward_saved["top_block"][1], backward_saved["top_block"][2], outputs[0]
            )
            return (
                weight_grad(backward_saved["top_low"], grad_latent),
                grad_top,
                grad_pre,
                grad_res,
            )

        grad_to_top, grad_top, grad_pre_top, grad_res_top = sectioned(on_top, top_back)
        padded_grad_top = top_grads(grad_pre_top, edge_keep)

        def stem_back_top():
            grad_in, grad_kernel = block_back_second(
                grad_top, backward_saved["top_block"][0], grad_pre_top, padded_grad_top, kernels[0]
            )
            grad_low = grad_in.astype(narrow)
            grad_stem_top = from_blocks(matmul(grad_low, down_flat.T), channels)
            grad_pre = (grad_stem_top * silu_slope(backward_saved["stem_pre"])).astype(narrow)
            return (
                grad_kernel,
                weight_grad(to_blocks(backward_saved["stem"]), grad_low),
                weight_grad(backward_saved["patches"], grad_pre),
            )

        grad_kernel_top, grad_down, grad_stem_pixel = sectioned(on_top, stem_back_top)
        batch_terms = (
            jnp.stack([grad_kernel_top, grad_kernel_bottom, grad_kernel_decode]),
            jnp.stack([grad_res_top, grad_res_bottom, grad_res_decode]),
            jnp.concatenate(
                [
                    grad_from_zero[None],
                    grad_up_maps.reshape(embed_dim, 4, channels).transpose(1, 0, 2),
                ],
                axis=0,
            ),
            jnp.stack([grad_to_top, grad_to_bottom]),
            jnp.stack([grad_stem_pixel + grad_stem_bottom, grad_pixel_out]),
            grad_down.reshape(4, channels, channels),
        )
        gradients = [g + t for g, t in zip(gradients, batch_terms)]
    totals = lax.psum(
        (gradients[0], gradients[1], gradients[2], gradients[3], gradients[4], gradients[5]),
        ("section", "dp"),
    )
    grad_norm = jnp.sqrt(sum((jnp.sum(g * g) for g in totals)))
    factor = CLIP_NORM / jnp.maximum(grad_norm, CLIP_NORM)
    firsts = (m_conv, m_res_out, m_from_code, m_to_code, m_pixel, m_down)
    seconds = (v_conv, v_res_out, v_from_code, v_to_code, v_pixel, v_down)
    results = [adamw(w, g * factor, m, v) for w, g, m, v in zip(weights, totals, firsts, seconds)]
    code_used, code_sums, dead_rows, numer_total = summed_stats
    counts_next = CODE_DECAY * ema_count + (1.0 - CODE_DECAY) * code_used
    sums_next = CODE_DECAY * ema_sum + (1.0 - CODE_DECAY) * code_sums
    dead_match = (jnp.arange(book_size)[None, :, None] == dead_codes[:, None, :]).astype(single)
    dead_taken = jnp.sum(dead_match, axis=2)
    replaced = jnp.einsum("lkr,lre->lke", dead_match, dead_rows, precision=HIGHEST)
    new_sum = jnp.where(dead_taken[:, :, None] > 0, replaced, sums_next)
    new_count = jnp.where(dead_taken > 0, 1.0, counts_next)
    new_book = new_sum / new_count[:, :, None]
    loss_pair = jnp.stack([numer_total, valid_count])
    return (
        grad_norm,
        loss_pair,
        results[0][0],
        results[1][0],
        results[2][0],
        results[3][0],
        results[4][0],
        results[5][0],
        results[0][1],
        results[1][1],
        results[2][1],
        results[3][1],
        results[4][1],
        results[5][1],
        results[0][2],
        results[1][2],
        results[2][2],
        results[3][2],
        results[4][2],
        results[5][2],
        results[0][0].astype(narrow),
        results[1][0].astype(narrow),
        results[2][0].astype(narrow),
        results[3][0].astype(narrow),
        results[4][0].astype(narrow),
        results[5][0].astype(narrow),
        new_book,
        new_count,
        new_sum,
    )


def solution(mesh):
    return jax.shard_map(
        body,
        mesh=mesh,
        in_specs=(
            P(None, "dp", None),
            P(None, "dp", None),
            P(None, "dp", None),
            P(),
            P(),
            P(),
            P(),
            P(),
            P(),
            P(),
            P(),
            P(),
            P(),
            P(),
            P(),
            P(),
            P(),
            P(),
            P(),
            P(),
            P(),
            P(),
            P(),
            P(),
            P(),
            P(),
            P(),
        ),
        out_specs=(
            P(),
            P(),
            P(),
            P(),
            P(),
            P(),
            P(),
            P(),
            P(),
            P(),
            P(),
            P(),
            P(),
            P(),
            P(),
            P(),
            P(),
            P(),
            P(),
            P(),
            P(),
            P(),
            P(),
            P(),
            P(),
            P(),
            P(),
            P(),
            P(),
        ),
        check_vma=False,
    )
```

profile of v0, /device:TPU:0, one launch (start us, length us, event | category | flops | bytes accessed | tf_op | source)
XLA Modules:
  0.0 2505.1 jit_solution(11665116361557554113)
XLA Ops:
  11.2 26.8 %conditional.112 = (bf16[32,64,48]{1,0,2:T(8,128)(2,1)}, f32[32,64,128]{2,1,0:T(8,128)S(1)}, bf16[32,64,128]{2,1,0:T(8,128)(2,1)}) conditional(s32[]{:T(128)} %convert_element_type.1236, () %tuple.1156, (bf16[1,128,768]{1,2,0:T(8,128)(2,1)}, bf16[2,48,128]{2,1,0:T(8,128)(2,1)S(1)}) %tuple.1157), branch_computations={%region_1.2_spmd, %region_2.3_spmd} | conditional | flops 26476544 | bytes 2568216 | solution.py:126
  11.2 15.3 reshape_squeeze.16
  26.5 9.2 copy.718
  50.9 26.8 %conditional.123 = (bf16[32,64,48]{1,0,2:T(8,128)(2,1)}, f32[32,64,128]{2,1,0:T(8,128)S(1)}, bf16[32,64,128]{2,1,0:T(8,128)(2,1)}) conditional(s32[]{:T(128)} %convert_element_type.1236, () %tuple.1178, (bf16[1,128,768]{1,2,0:T(8,128)(2,1)}, bf16[2,48,128]{2,1,0:T(8,128)(2,1)S(1)}) %tuple.1179), branch_computations={%region_26.29_spmd, %region_27.30_spmd} | conditional | flops 26476544 | bytes 2568216 | solution.py:126
  50.9 15.2 reshape_squeeze.18
  66.2 9.2 copy.731
  80.6 26.8 %conditional.134 = (bf16[32,64,48]{1,0,2:T(8,128)(2,1)}, f32[32,64,128]{2,1,0:T(8,128)S(1)}, bf16[32,64,128]{2,1,0:T(8,128)(2,1)}) conditional(s32[]{:T(128)} %convert_element_type.1236, () %tuple.1200, (bf16[1,128,768]{1,2,0:T(8,128)(2,1)}, bf16[2,48,128]{2,1,0:T(8,128)(2,1)S(1)}) %tuple.1201), branch_computations={%region_51.54_spmd, %region_52.55_spmd} | conditional | flops 26476544 | bytes 2568216 | solution.py:126
  80.6 15.3 reshape_squeeze.20
  95.9 9.2 copy.744
  124.5 26.0 %conditional.145 = (bf16[32,64,48]{1,0,2:T(8,128)(2,1)}, f32[32,64,128]{2,1,0:T(8,128)S(1)}, bf16[32,64,128]{2,1,0:T(8,128)(2,1)S(1)}) conditional(s32[]{:T(128)} %convert_element_type.1236, () %tuple.1222, (bf16[1,128,768]{1,2,0:T(8,128)(2,1)}, bf16[2,48,128]{2,1,0:T(8,128)(2,1)S(1)}) %tuple.1223), branch_computations={%region_76.79_spmd, %region_77.80_spmd} | conditional | flops 26476544 | bytes 2568216 | solution.py:126
  124.6 15.2 reshape_squeeze.22
  139.8 9.2 copy.757
  155.8 26.8 %conditional.156 = (bf16[32,64,48]{1,0,2:T(8,128)(2,1)}, f32[32,64,128]{2,1,0:T(8,128)S(1)}, bf16[32,64,128]{2,1,0:T(8,128)(2,1)}) conditional(s32[]{:T(128)} %convert_element_type.1236, () %tuple.1244, (bf16[1,128,768]{1,2,0:T(8,128)(2,1)}, bf16[2,48,128]{2,1,0:T(8,128)(2,1)S(1)}) %tuple.1245), branch_computations={%region_101.104_spmd, %region_102.105_spmd} | conditional | flops 26476544 | bytes 2568216 | solution.py:126
  155.8 15.2 reshape_squeeze.24
  171.0 9.2 copy.770
  189.2 27.2 %conditional.167 = (bf16[32,64,48]{1,0,2:T(8,128)(2,1)}, f32[32,64,128]{2,1,0:T(8,128)S(1)}, bf16[32,64,128]{2,1,0:T(8,128)(2,1)}) conditional(s32[]{:T(128)} %convert_element_type.1236, () %tuple.1266, (bf16[1,128,768]{1,2,0:T(8,128)(2,1)}, bf16[2,48,128]{2,1,0:T(8,128)(2,1)S(1)}) %tuple.1267), branch_computations={%region_126.129_spmd, %region_127.130_spmd} | conditional | flops 26476544 | bytes 2568216 | solution.py:126
  189.7 15.2 reshape_squeeze.26
  204.9 9.2 copy.783
  222.1 26.7 %conditional.178 = (bf16[32,64,48]{1,0,2:T(8,128)(2,1)}, f32[32,64,128]{2,1,0:T(8,128)S(1)}, bf16[32,64,128]{2,1,0:T(8,128)(2,1)}) conditional(s32[]{:T(128)} %convert_element_type.1236, () %tuple.1288, (bf16[1,128,768]{1,2,0:T(8,128)(2,1)}, bf16[2,48,128]{2,1,0:T(8,128)(2,1)S(1)}) %tuple.1289), branch_computations={%region_151.154_spmd, %region_152.155_spmd} | conditional | flops 26476544 | bytes 2568216 | solution.py:126
  222.1 15.2 reshape_squeeze.28
  237.4 9.2 copy.796
  254.6 26.9 %conditional.189 = (bf16[32,64,48]{1,0,2:T(8,128)(2,1)}, f32[32,64,128]{2,1,0:T(8,128)S(1)}, bf16[32,64,128]{2,1,0:T(8,128)(2,1)}) conditional(s32[]{:T(128)} %convert_element_type.1236, () %tuple.1310, (bf16[1,128,768]{1,2,0:T(8,128)(2,1)}, bf16[2,48,128]{2,1,0:T(8,128)(2,1)S(1)}) %tuple.1311), branch_computations={%region_176.179_spmd, %region_177.180_spmd} | conditional | flops 26476544 | bytes 2568216 | solution.py:126
  254.6 15.3 reshape_squeeze.30
  270.0 9.2 copy.809
  349.5 6.9 collective-permute-start.105
  358.1 17.1 conditional.114
  376.0 17.8 conditional.125
  394.5 17.8 conditional.136
  413.1 20.2 conditional.147
  434.1 20.4 conditional.158
  455.3 20.9 conditional.169
  477.9 21.1 conditional.180
  506.1 21.0 conditional.191
  570.7 8.4 collective-permute-start.78
  584.8 8.5 collective-permute-start.62
  600.4 8.7 collective-permute-start.77
  616.6 8.8 collective-permute-start.107
  664.8 8.2 conditional.116
  684.1 10.3 conditional.127
  706.0 9.3 conditional.138
  727.8 10.4 conditional.149
  749.8 9.1 conditional.160
  771.4 10.2 conditional.171
  793.2 9.2 conditional.182
  805.3 6.9 collective-permute-start.21
  815.5 10.3 conditional.193
  912.5 6.9 collective-permute-start.96
  964.0 6.9 collective-permute-start.23
  1114.9 6.4 collective-permute-start.70
  1169.6 888.7 %collective-permute-done.12 = bf16[16,32,64]{2,1,0:T(8,128)(2,1)} collective-permute-done((bf16[16,32,64]{2,1,0:T(8,128)(2,1)}, bf16[16,32,64]{2,1,0:T(8,128)(2,1)}, u32[]{:S(2)}, u32[]{:S(2)}) %collective-permute-start.12) | collective-permute-done | bytes 65568 | tf_op jit(solution)/shard_map/ppermute | solution.py:36
  2065.6 15.3 collective-permute-done.27
  2095.6 10.4 collective-permute-done.57
  2120.7 14.1 collective-permute-done.87
  2215.4 6.9 collective-permute-start.118
  2223.1 10.9 conditional.122
  2234.6 12.0 conditional.133
  2247.4 13.9 conditional.144
  2262.2 14.3 conditional.155
  2277.3 11.2 conditional.166
  2289.2 11.7 conditional.177
  2301.6 11.0 conditional.188
  2316.1 11.7 conditional.199
  2359.5 48.9 %all-reduce.48 = (f32[2,48,128]{2,1,0:T(8,128)S(1)}, f32[1]{0:T(128)}, f32[2,8,64]{2,1,0:T(8,128)S(1)}, f32[2,512]{1,0:T(2,128)S(1)}) all-reduce(f32[2,48,128]{2,1,0:T(8,128)S(1)} %fusion.879, f32[1]{0:T(128)} %bitcast.949, f32[2,8,64]{2,1,0:T(8,128)S(1)} %copy-done.341, ...), channel_id=1, replica_groups=mesh['section'=2,'dp'=16] {'section','dp'}, use_global_device_ids=true, to_apply=%region_225.228 | all-reduce | flops 14337 | bytes 114696 | tf_op jit(solution)/shard_map/psum | solution.py:498
  2410.2 65.2 %all-reduce.52.cloned.1.call-done = (f32[3,1152,64]{1,2,0:T(8,128)}, f32[3,64,128]{2,1,0:T(8,128)}, f32[5,64,128]{2,1,0:T(8,128)}, f32[2,128,64]{1,2,0:T(8,128)}...) async-done(((f32[3,1152,64]{1,2,0:T(8,128)}, f32[3,64,128]{2,1,0:T(8,128)}, f32[5,64,128]{2,1,0:T(8,128)}, f32[2,128,64]{1,2,0:T(8,128)}, f32[4,128,128]{2,1,0:T(8,128)}, ...) | async-done | bytes 1736720 | tf_op jit(solution)/shard_map/psum | solution.py:498
  (1954 shorter events, 1363.6 us)
Async XLA Ops:
  7.2 2468.1 %all-reduce.52.cloned.1.call-start = ((), (), s32[]{:S(2)}) async-start(), calls=%async_computation | async-start | bytes 3473408 | tf_op jit(solution)/shard_map/psum | solution.py:498
  38.0 520.6 %collective-permute-start.3 = (bf16[32,64,128]{2,1,0:T(8,128)(2,1)}, bf16[32,64,128]{2,1,0:T(8,128)(2,1)}, u32[]{:S(2)}, u32[]{:S(2)}) collective-permute-start(bf16[32,64,128]{2,1,0:T(8,128)(2,1)} %get-tuple-element.3055), channel_id=1, source_target_pairs={{0,16},{1,17},{2,18},{3,19},{4,20},{5,21},{6,22},{7,23},{8,24},{9,... | collective-permute-start | bytes 1572872 | tf_op jit(solution)/shard_map/ppermute | solution.py:36
  42.8 255.4 %collective-permute-start.1 = (bf16[1,32,128]{2,1,0:T(8,128)(2,1)}, bf16[1,32,128]{2,1,0:T(8,128)(2,1)S(1)}, u32[]{:S(2)}, u32[]{:S(2)}) collective-permute-start(bf16[1,32,128]{2,1,0:T(8,128)(2,1)} %get-tuple-element.6260), channel_id=1, source_target_pairs={{1,0},{2,1},{3,2},{4,3},{5,4},{6,5},{7,6},{8,7},{9,8},{10,9},{11,1... | collective-permute-start | bytes 24584 | tf_op jit(solution)/shard_map/ppermute | solution.py:28
  44.1 255.4 %collective-permute-start = (bf16[1,32,128]{2,1,0:T(8,128)(2,1)}, bf16[1,32,128]{2,1,0:T(8,128)(2,1)}, u32[]{:S(2)}, u32[]{:S(2)}) collective-permute-start(bf16[1,32,128]{2,1,0:T(8,128)(2,1)} %get-tuple-element.6259), channel_id=1, source_target_pairs={{0,1},{1,2},{2,3},{3,4},{4,5},{5,6},{6,7},{7,8},{8,9},{9,10},{10,1... | collective-permute-start | bytes 24584 | tf_op jit(solution)/shard_map/ppermute | solution.py:25
  77.7 486.9 %collective-permute-start.18 = (bf16[32,64,128]{2,1,0:T(8,128)(2,1)}, bf16[32,64,128]{2,1,0:T(8,128)(2,1)}, u32[]{:S(2)}, u32[]{:S(2)}) collective-permute-start(bf16[32,64,128]{2,1,0:T(8,128)(2,1)} %get-tuple-element.3090), channel_id=1, source_target_pairs={{0,16},{1,17},{2,18},{3,19},{4,20},{5,21},{6,22},{7,23},{8,24},{9,... | collective-permute-start | bytes 1572872 | tf_op jit(solution)/shard_map/ppermute | solution.py:36
  107.5 471.7 %collective-permute-start.33 = (bf16[32,64,128]{2,1,0:T(8,128)(2,1)}, bf16[32,64,128]{2,1,0:T(8,128)(2,1)}, u32[]{:S(2)}, u32[]{:S(2)}) collective-permute-start(bf16[32,64,128]{2,1,0:T(8,128)(2,1)} %get-tuple-element.3125), channel_id=1, source_target_pairs={{0,16},{1,17},{2,18},{3,19},{4,20},{5,21},{6,22},{7,23},{8,24},{9,... | collective-permute-start | bytes 1572872 | tf_op jit(solution)/shard_map/ppermute | solution.py:36
  348.2 152.5 %collective-permute-start.106 = (bf16[1,32,128]{2,1,0:T(8,128)(2,1)}, bf16[1,32,128]{2,1,0:T(8,128)(2,1)S(1)}, u32[]{:S(2)}, u32[]{:S(2)}) collective-permute-start(bf16[1,32,128]{2,1,0:T(8,128)(2,1)} %get-tuple-element.6232), channel_id=1, source_target_pairs={{1,0},{2,1},{3,2},{4,3},{5,4},{6,5},{7,6},{8,7},{9,8},{10,9},{11,1... | collective-permute-start | bytes 24584 | tf_op jit(solution)/shard_map/ppermute | solution.py:28
  349.5 153.3 %collective-permute-start.105 = (bf16[1,32,128]{2,1,0:T(8,128)(2,1)}, bf16[1,32,128]{2,1,0:T(8,128)(2,1)}, u32[]{:S(2)}, u32[]{:S(2)}) collective-permute-start(bf16[1,32,128]{2,1,0:T(8,128)(2,1)} %get-tuple-element.6231), channel_id=1, source_target_pairs={{0,1},{1,2},{2,3},{3,4},{4,5},{5,6},{6,7},{7,8},{8,9},{9,10},{10,1... | collective-permute-start | bytes 24584 | tf_op jit(solution)/shard_map/ppermute | solution.py:25
  500.7 93.2 %collective-permute-start.48 = (bf16[32,64,128]{2,1,0:T(8,128)(2,1)S(1)}, bf16[32,64,128]{2,1,0:T(8,128)(2,1)}, u32[]{:S(2)}, u32[]{:S(2)}) collective-permute-start(bf16[32,64,128]{2,1,0:T(8,128)(2,1)S(1)} %get-tuple-element.3160), channel_id=1, source_target_pairs={{0,16},{1,17},{2,18},{3,19},{4,20},{5,21},{6,22},{7,23},{8,24},{9,... | collective-permute-start | bytes 1572872 | tf_op jit(solution)/shard_map/ppermute | solution.py:36
  502.8 53.6 %collective-permute-start.2 = (bf16[16,32,64]{2,1,0:T(8,128)(2,1)}, bf16[16,32,64]{2,1,0:T(8,128)(2,1)}, u32[]{:S(2)}, u32[]{:S(2)}) collective-permute-start(bf16[16,32,64]{2,1,0:T(8,128)(2,1)} %convert_element_type.1250), channel_id=1, source_target_pairs={{0,16},{1,17},{2,18},{3,19},{4,20},{5,21},{6,22},{7,23},{8,24},{9,... | collective-permute-start | bytes 196616 | tf_op jit(solution)/shard_map/ppermute | solution.py:36
  556.4 52.6 %collective-permute-start.63 = (bf16[32,64,128]{2,1,0:T(8,128)(2,1)}, bf16[32,64,128]{2,1,0:T(8,128)(2,1)}, u32[]{:S(2)}, u32[]{:S(2)}) collective-permute-start(bf16[32,64,128]{2,1,0:T(8,128)(2,1)} %get-tuple-element.3195), channel_id=1, source_target_pairs={{0,16},{1,17},{2,18},{3,19},{4,20},{5,21},{6,22},{7,23},{8,24},{9,... | collective-permute-start | bytes 1572872 | tf_op jit(solution)/shard_map/ppermute | solution.py:36
  570.7 54.7 %collective-permute-start.78 = (bf16[32,64,128]{2,1,0:T(8,128)(2,1)}, bf16[32,64,128]{2,1,0:T(8,128)(2,1)}, u32[]{:S(2)}, u32[]{:S(2)}) collective-permute-start(bf16[32,64,128]{2,1,0:T(8,128)(2,1)} %get-tuple-element.3230), channel_id=1, source_target_pairs={{0,16},{1,17},{2,18},{3,19},{4,20},{5,21},{6,22},{7,23},{8,24},{9,... | collective-permute-start | bytes 1572872 | tf_op jit(solution)/shard_map/ppermute | solution.py:36
  579.1 57.8 %collective-permute-start.93 = (bf16[32,64,128]{2,1,0:T(8,128)(2,1)}, bf16[32,64,128]{2,1,0:T(8,128)(2,1)}, u32[]{:S(2)}, u32[]{:S(2)}) collective-permute-start(bf16[32,64,128]{2,1,0:T(8,128)(2,1)} %get-tuple-element.3265), channel_id=1, source_target_pairs={{0,16},{1,17},{2,18},{3,19},{4,20},{5,21},{6,22},{7,23},{8,24},{9,... | collective-permute-start | bytes 1572872 | tf_op jit(solution)/shard_map/ppermute | solution.py:36
  593.9 56.3 %collective-permute-start.108 = (bf16[32,64,128]{2,1,0:T(8,128)(2,1)}, bf16[32,64,128]{2,1,0:T(8,128)(2,1)}, u32[]{:S(2)}, u32[]{:S(2)}) collective-permute-start(bf16[32,64,128]{2,1,0:T(8,128)(2,1)} %get-tuple-element.3300), channel_id=1, source_target_pairs={{0,16},{1,17},{2,18},{3,19},{4,20},{5,21},{6,22},{7,23},{8,24},{9,... | collective-permute-start | bytes 1572872 | tf_op jit(solution)/shard_map/ppermute | solution.py:36
  637.0 37.6 %collective-permute-start.20 = (bf16[1,64,128]{2,1,0:T(8,128)(2,1)}, bf16[1,64,128]{2,1,0:T(8,128)(2,1)S(1)}, u32[]{:S(2)}, u32[]{:S(2)}) collective-permute-start(bf16[1,64,128]{2,1,0:T(8,128)(2,1)} %get-tuple-element.6220), channel_id=1, source_target_pairs={{1,0},{2,1},{3,2},{4,3},{5,4},{6,5},{7,6},{8,7},{9,8},{10,9},{11,1... | collective-permute-start | bytes 49160 | tf_op jit(solution)/shard_map/ppermute | solution.py:28
  643.9 37.0 %collective-permute-start.19 = (bf16[1,64,128]{2,1,0:T(8,128)(2,1)}, bf16[1,64,128]{2,1,0:T(8,128)(2,1)S(1)}, u32[]{:S(2)}, u32[]{:S(2)}) collective-permute-start(bf16[1,64,128]{2,1,0:T(8,128)(2,1)} %get-tuple-element.6219), channel_id=1, source_target_pairs={{0,1},{1,2},{2,3},{3,4},{4,5},{5,6},{6,7},{7,8},{8,9},{9,10},{10,1... | collective-permute-start | bytes 49160 | tf_op jit(solution)/shard_map/ppermute | solution.py:25
  650.2 46.2 %collective-permute-start.35 = (bf16[1,64,128]{2,1,0:T(8,128)(2,1)}, bf16[1,64,128]{2,1,0:T(8,128)(2,1)S(1)}, u32[]{:S(2)}, u32[]{:S(2)}) collective-permute-start(bf16[1,64,128]{2,1,0:T(8,128)(2,1)} %get-tuple-element.6212), channel_id=1, source_target_pairs={{1,0},{2,1},{3,2},{4,3},{5,4},{6,5},{7,6},{8,7},{9,8},{10,9},{11,1... | collective-permute-start | bytes 49160 | tf_op jit(solution)/shard_map/ppermute | solution.py:28
  655.2 47.6 %collective-permute-start.34 = (bf16[1,64,128]{2,1,0:T(8,128)(2,1)S(1)}, bf16[1,64,128]{2,1,0:T(8,128)(2,1)S(1)}, u32[]{:S(2)}, u32[]{:S(2)}) collective-permute-start(bf16[1,64,128]{2,1,0:T(8,128)(2,1)S(1)} %copy-done.366), channel_id=1, source_target_pairs={{0,1},{1,2},{2,3},{3,4},{4,5},{5,6},{6,7},{7,8},{8,9},{9,10},{10,1... | collective-permute-start | bytes 49160 | tf_op jit(solution)/shard_map/ppermute | solution.py:25
  661.6 56.7 %collective-permute-start.50 = (bf16[1,64,128]{2,1,0:T(8,128)(2,1)S(1)}, bf16[1,64,128]{2,1,0:T(8,128)(2,1)S(1)}, u32[]{:S(2)}, u32[]{:S(2)}) collective-permute-start(bf16[1,64,128]{2,1,0:T(8,128)(2,1)S(1)} %get-tuple-element.6204), channel_id=1, source_target_pairs={{1,0},{2,1},{3,2},{4,3},{5,4},{6,5},{7,6},{8,7},{9,8},{10,9},{11,1... | collective-permute-start | bytes 49160 | tf_op jit(solution)/shard_map/ppermute | solution.py:28
  674.6 50.0 %collective-permute-start.49 = (bf16[1,64,128]{2,1,0:T(8,128)(2,1)}, bf16[1,64,128]{2,1,0:T(8,128)(2,1)S(1)}, u32[]{:S(2)}, u32[]{:S(2)}) collective-permute-start(bf16[1,64,128]{2,1,0:T(8,128)(2,1)} %get-tuple-element.6203), channel_id=1, source_target_pairs={{0,1},{1,2},{2,3},{3,4},{4,5},{5,6},{6,7},{7,8},{8,9},{9,10},{10,1... | collective-permute-start | bytes 49160 | tf_op jit(solution)/shard_map/ppermute | solution.py:25
  680.9 59.3 %collective-permute-start.65 = (bf16[1,64,128]{2,1,0:T(8,128)(2,1)}, bf16[1,64,128]{2,1,0:T(8,128)(2,1)S(1)}, u32[]{:S(2)}, u32[]{:S(2)}) collective-permute-start(bf16[1,64,128]{2,1,0:T(8,128)(2,1)} %get-tuple-element.6196), channel_id=1, source_target_pairs={{1,0},{2,1},{3,2},{4,3},{5,4},{6,5},{7,6},{8,7},{9,8},{10,9},{11,1... | collective-permute-start | bytes 49160 | tf_op jit(solution)/shard_map/ppermute | solution.py:28
  696.4 50.1 %collective-permute-start.64 = (bf16[1,64,128]{2,1,0:T(8,128)(2,1)}, bf16[1,64,128]{2,1,0:T(8,128)(2,1)S(1)}, u32[]{:S(2)}, u32[]{:S(2)}) collective-permute-start(bf16[1,64,128]{2,1,0:T(8,128)(2,1)} %get-tuple-element.6195), channel_id=1, source_target_pairs={{0,1},{1,2},{2,3},{3,4},{4,5},{5,6},{6,7},{7,8},{8,9},{9,10},{10,1... | collective-permute-start | bytes 49160 | tf_op jit(solution)/shard_map/ppermute | solution.py:25
  702.8 59.0 %collective-permute-start.80 = (bf16[1,64,128]{2,1,0:T(8,128)(2,1)}, bf16[1,64,128]{2,1,0:T(8,128)(2,1)S(1)}, u32[]{:S(2)}, u32[]{:S(2)}) collective-permute-start(bf16[1,64,128]{2,1,0:T(8,128)(2,1)} %get-tuple-element.6188), channel_id=1, source_target_pairs={{1,0},{2,1},{3,2},{4,3},{5,4},{6,5},{7,6},{8,7},{9,8},{10,9},{11,1... | collective-permute-start | bytes 49160 | tf_op jit(solution)/shard_map/ppermute | solution.py:28
  718.3 49.9 %collective-permute-start.79 = (bf16[1,64,128]{2,1,0:T(8,128)(2,1)S(1)}, bf16[1,64,128]{2,1,0:T(8,128)(2,1)S(1)}, u32[]{:S(2)}, u32[]{:S(2)}) collective-permute-start(bf16[1,64,128]{2,1,0:T(8,128)(2,1)S(1)} %copy-done.365), channel_id=1, source_target_pairs={{0,1},{1,2},{2,3},{3,4},{4,5},{5,6},{6,7},{7,8},{8,9},{9,10},{10,1... | collective-permute-start | bytes 49160 | tf_op jit(solution)/shard_map/ppermute | solution.py:25
  724.6 59.0 %collective-permute-start.95 = (bf16[1,64,128]{2,1,0:T(8,128)(2,1)S(1)}, bf16[1,64,128]{2,1,0:T(8,128)(2,1)S(1)}, u32[]{:S(2)}, u32[]{:S(2)}) collective-permute-start(bf16[1,64,128]{2,1,0:T(8,128)(2,1)S(1)} %copy-done.364), channel_id=1, source_target_pairs={{1,0},{2,1},{3,2},{4,3},{5,4},{6,5},{7,6},{8,7},{9,8},{10,9},{11,1... | collective-permute-start | bytes 49160 | tf_op jit(solution)/shard_map/ppermute | solution.py:28
  740.2 49.8 %collective-permute-start.94 = (bf16[1,64,128]{2,1,0:T(8,128)(2,1)S(1)}, bf16[1,64,128]{2,1,0:T(8,128)(2,1)S(1)}, u32[]{:S(2)}, u32[]{:S(2)}) collective-permute-start(bf16[1,64,128]{2,1,0:T(8,128)(2,1)S(1)} %copy-done.363), channel_id=1, source_target_pairs={{0,1},{1,2},{2,3},{3,4},{4,5},{5,6},{6,7},{7,8},{8,9},{9,10},{10,1... | collective-permute-start | bytes 49160 | tf_op jit(solution)/shard_map/ppermute | solution.py:25
  746.5 58.8 %collective-permute-start.110 = (bf16[1,64,128]{2,1,0:T(8,128)(2,1)S(1)}, bf16[1,64,128]{2,1,0:T(8,128)(2,1)S(1)}, u32[]{:S(2)}, u32[]{:S(2)}) collective-permute-start(bf16[1,64,128]{2,1,0:T(8,128)(2,1)S(1)} %get-tuple-element.6172), channel_id=1, source_target_pairs={{1,0},{2,1},{3,2},{4,3},{5,4},{6,5},{7,6},{8,7},{9,8},{10,9},{11,1... | collective-permute-start | bytes 49160 | tf_op jit(solution)/shard_map/ppermute | solution.py:28
  761.8 50.4 %collective-permute-start.109 = (bf16[1,64,128]{2,1,0:T(8,128)(2,1)S(1)}, bf16[1,64,128]{2,1,0:T(8,128)(2,1)S(1)}, u32[]{:S(2)}, u32[]{:S(2)}) collective-permute-start(bf16[1,64,128]{2,1,0:T(8,128)(2,1)S(1)} %get-tuple-element.6171), channel_id=1, source_target_pairs={{0,1},{1,2},{2,3},{3,4},{4,5},{5,6},{6,7},{7,8},{8,9},{9,10},{10,1... | collective-permute-start | bytes 49160 | tf_op jit(solution)/shard_map/ppermute | solution.py:25
  768.2 77.0 %collective-permute-start.7 = (bf16[1,64,128]{2,1,0:T(8,128)(2,1)}, bf16[1,64,128]{2,1,0:T(8,128)(2,1)S(1)}, u32[]{:S(2)}, u32[]{:S(2)}) collective-permute-start(bf16[1,64,128]{2,1,0:T(8,128)(2,1)} %get-tuple-element.6226), channel_id=1, source_target_pairs={{1,0},{2,1},{3,2},{4,3},{5,4},{6,5},{7,6},{8,7},{9,8},{10,9},{11,1... | collective-permute-start | bytes 49160 | tf_op jit(solution)/shard_map/ppermute | solution.py:28
  783.6 68.0 %collective-permute-start.6 = (bf16[1,64,128]{2,1,0:T(8,128)(2,1)}, bf16[1,64,128]{2,1,0:T(8,128)(2,1)S(1)}, u32[]{:S(2)}, u32[]{:S(2)}) collective-permute-start(bf16[1,64,128]{2,1,0:T(8,128)(2,1)} %get-tuple-element.6225), channel_id=1, source_target_pairs={{0,1},{1,2},{2,3},{3,4},{4,5},{5,6},{6,7},{7,8},{8,9},{9,10},{10,1... | collective-permute-start | bytes 49160 | tf_op jit(solution)/shard_map/ppermute | solution.py:25
  790.0 71.2 %collective-permute-start.22 = (bf16[1,64,128]{2,1,0:T(8,128)(2,1)}, bf16[1,64,128]{2,1,0:T(8,128)(2,1)}, u32[]{:S(2)}, u32[]{:S(2)}) collective-permute-start(bf16[1,64,128]{2,1,0:T(8,128)(2,1)} %get-tuple-element.6218), channel_id=1, source_target_pairs={{1,0},{2,1},{3,2},{4,3},{5,4},{6,5},{7,6},{8,7},{9,8},{10,9},{11,1... | collective-permute-start | bytes 49160 | tf_op jit(solution)/shard_map/ppermute | solution.py:28
  805.3 62.2 %collective-permute-start.21 = (bf16[1,64,128]{2,1,0:T(8,128)(2,1)}, bf16[1,64,128]{2,1,0:T(8,128)(2,1)}, u32[]{:S(2)}, u32[]{:S(2)}) collective-permute-start(bf16[1,64,128]{2,1,0:T(8,128)(2,1)} %get-tuple-element.6217), channel_id=1, source_target_pairs={{0,1},{1,2},{2,3},{3,4},{4,5},{5,6},{6,7},{7,8},{8,9},{9,10},{10,1... | collective-permute-start | bytes 49160 | tf_op jit(solution)/shard_map/ppermute | solution.py:25
  812.2 66.2 %collective-permute-start.37 = (bf16[1,64,128]{2,1,0:T(8,128)(2,1)}, bf16[1,64,128]{2,1,0:T(8,128)(2,1)}, u32[]{:S(2)}, u32[]{:S(2)}) collective-permute-start(bf16[1,64,128]{2,1,0:T(8,128)(2,1)} %get-tuple-element.6210), channel_id=1, source_target_pairs={{1,0},{2,1},{3,2},{4,3},{5,4},{6,5},{7,6},{8,7},{9,8},{10,9},{11,1... | collective-permute-start | bytes 49160 | tf_op jit(solution)/shard_map/ppermute | solution.py:28
  845.2 39.0 %collective-permute-start.36 = (bf16[1,64,128]{2,1,0:T(8,128)(2,1)}, bf16[1,64,128]{2,1,0:T(8,128)(2,1)}, u32[]{:S(2)}, u32[]{:S(2)}) collective-permute-start(bf16[1,64,128]{2,1,0:T(8,128)(2,1)} %get-tuple-element.6209), channel_id=1, source_target_pairs={{0,1},{1,2},{2,3},{3,4},{4,5},{5,6},{6,7},{7,8},{8,9},{9,10},{10,1... | collective-permute-start | bytes 49160 | tf_op jit(solution)/shard_map/ppermute | solution.py:25
  851.6 43.6 %collective-permute-start.52 = (bf16[1,64,128]{2,1,0:T(8,128)(2,1)}, bf16[1,64,128]{2,1,0:T(8,128)(2,1)S(1)}, u32[]{:S(2)}, u32[]{:S(2)}) collective-permute-start(bf16[1,64,128]{2,1,0:T(8,128)(2,1)} %get-tuple-element.6202), channel_id=1, source_target_pairs={{1,0},{2,1},{3,2},{4,3},{5,4},{6,5},{7,6},{8,7},{9,8},{10,9},{11,1... | collective-permute-start | bytes 49160 | tf_op jit(solution)/shard_map/ppermute | solution.py:28
  861.2 40.4 %collective-permute-start.51 = (bf16[1,64,128]{2,1,0:T(8,128)(2,1)}, bf16[1,64,128]{2,1,0:T(8,128)(2,1)}, u32[]{:S(2)}, u32[]{:S(2)}) collective-permute-start(bf16[1,64,128]{2,1,0:T(8,128)(2,1)} %get-tuple-element.6201), channel_id=1, source_target_pairs={{0,1},{1,2},{2,3},{3,4},{4,5},{5,6},{6,7},{7,8},{8,9},{9,10},{10,1... | collective-permute-start | bytes 49160 | tf_op jit(solution)/shard_map/ppermute | solution.py:25
  867.5 45.0 %collective-permute-start.67 = (bf16[1,64,128]{2,1,0:T(8,128)(2,1)}, bf16[1,64,128]{2,1,0:T(8,128)(2,1)S(1)}, u32[]{:S(2)}, u32[]{:S(2)}) collective-permute-start(bf16[1,64,128]{2,1,0:T(8,128)(2,1)} %get-tuple-element.6194), channel_id=1, source_target_pairs={{1,0},{2,1},{3,2},{4,3},{5,4},{6,5},{7,6},{8,7},{9,8},{10,9},{11,1... | collective-permute-start | bytes 49160 | tf_op jit(solution)/shard_map/ppermute | solution.py:28
  878.4 41.1 %collective-permute-start.66 = (bf16[1,64,128]{2,1,0:T(8,128)(2,1)}, bf16[1,64,128]{2,1,0:T(8,128)(2,1)S(1)}, u32[]{:S(2)}, u32[]{:S(2)}) collective-permute-start(bf16[1,64,128]{2,1,0:T(8,128)(2,1)} %get-tuple-element.6193), channel_id=1, source_target_pairs={{0,1},{1,2},{2,3},{3,4},{4,5},{5,6},{6,7},{7,8},{8,9},{9,10},{10,1... | collective-permute-start | bytes 49160 | tf_op jit(solution)/shard_map/ppermute | solution.py:25
  884.2 46.1 %collective-permute-start.82 = (bf16[1,64,128]{2,1,0:T(8,128)(2,1)}, bf16[1,64,128]{2,1,0:T(8,128)(2,1)S(1)}, u32[]{:S(2)}, u32[]{:S(2)}) collective-permute-start(bf16[1,64,128]{2,1,0:T(8,128)(2,1)} %get-tuple-element.6186), channel_id=1, source_target_pairs={{1,0},{2,1},{3,2},{4,3},{5,4},{6,5},{7,6},{8,7},{9,8},{10,9},{11,1... | collective-permute-start | bytes 49160 | tf_op jit(solution)/shard_map/ppermute | solution.py:28
  895.2 40.9 %collective-permute-start.81 = (bf16[1,64,128]{2,1,0:T(8,128)(2,1)S(1)}, bf16[1,64,128]{2,1,0:T(8,128)(2,1)S(1)}, u32[]{:S(2)}, u32[]{:S(2)}) collective-permute-start(bf16[1,64,128]{2,1,0:T(8,128)(2,1)S(1)} %copy-done.362), channel_id=1, source_target_pairs={{0,1},{1,2},{2,3},{3,4},{4,5},{5,6},{6,7},{7,8},{8,9},{9,10},{10,1... | collective-permute-start | bytes 49160 | tf_op jit(solution)/shard_map/ppermute | solution.py:25
  901.5 45.3 %collective-permute-start.97 = (bf16[1,64,128]{2,1,0:T(8,128)(2,1)}, bf16[1,64,128]{2,1,0:T(8,128)(2,1)S(1)}, u32[]{:S(2)}, u32[]{:S(2)}) collective-permute-start(bf16[1,64,128]{2,1,0:T(8,128)(2,1)} %get-tuple-element.6178), channel_id=1, source_target_pairs={{1,0},{2,1},{3,2},{4,3},{5,4},{6,5},{7,6},{8,7},{9,8},{10,9},{11,1... | collective-permute-start | bytes 49160 | tf_op jit(solution)/shard_map/ppermute | solution.py:28
  912.5 40.7 %collective-permute-start.96 = (bf16[1,64,128]{2,1,0:T(8,128)(2,1)}, bf16[1,64,128]{2,1,0:T(8,128)(2,1)}, u32[]{:S(2)}, u32[]{:S(2)}) collective-permute-start(bf16[1,64,128]{2,1,0:T(8,128)(2,1)} %get-tuple-element.6177), channel_id=1, source_target_pairs={{0,1},{1,2},{2,3},{3,4},{4,5},{5,6},{6,7},{7,8},{8,9},{9,10},{10,1... | collective-permute-start | bytes 49160 | tf_op jit(solution)/shard_map/ppermute | solution.py:25
  919.5 44.6 %collective-permute-start.112 = (bf16[1,64,128]{2,1,0:T(8,128)(2,1)}, bf16[1,64,128]{2,1,0:T(8,128)(2,1)S(1)}, u32[]{:S(2)}, u32[]{:S(2)}) collective-permute-start(bf16[1,64,128]{2,1,0:T(8,128)(2,1)} %get-tuple-element.6170), channel_id=1, source_target_pairs={{1,0},{2,1},{3,2},{4,3},{5,4},{6,5},{7,6},{8,7},{9,8},{10,9},{11,1... | collective-permute-start | bytes 49160 | tf_op jit(solution)/shard_map/ppermute | solution.py:28
  930.3 40.7 %collective-permute-start.111 = (bf16[1,64,128]{2,1,0:T(8,128)(2,1)S(1)}, bf16[1,64,128]{2,1,0:T(8,128)(2,1)S(1)}, u32[]{:S(2)}, u32[]{:S(2)}) collective-permute-start(bf16[1,64,128]{2,1,0:T(8,128)(2,1)S(1)} %copy-done.361), channel_id=1, source_target_pairs={{0,1},{1,2},{2,3},{3,4},{4,5},{5,6},{6,7},{7,8},{8,9},{9,10},{10,1... | collective-permute-start | bytes 49160 | tf_op jit(solution)/shard_map/ppermute | solution.py:25
  936.1 45.8 %collective-permute-start.9 = (bf16[1,64,64]{2,1,0:T(8,128)(2,1)}, bf16[1,64,64]{2,1,0:T(8,128)(2,1)S(1)}, u32[]{:S(2)}, u32[]{:S(2)}) collective-permute-start(bf16[1,64,64]{2,1,0:T(8,128)(2,1)} %get-tuple-element.6224), channel_id=1, source_target_pairs={{1,0},{2,1},{3,2},{4,3},{5,4},{6,5},{7,6},{8,7},{9,8},{10,9},{11,1... | collective-permute-start | bytes 24584 | tf_op jit(solution)/shard_map/ppermute | solution.py:28
  946.9 41.4 %collective-permute-start.8 = (bf16[1,64,64]{2,1,0:T(8,128)(2,1)}, bf16[1,64,64]{2,1,0:T(8,128)(2,1)S(1)}, u32[]{:S(2)}, u32[]{:S(2)}) collective-permute-start(bf16[1,64,64]{2,1,0:T(8,128)(2,1)} %get-tuple-element.6223), channel_id=1, source_target_pairs={{0,1},{1,2},{2,3},{3,4},{4,5},{5,6},{6,7},{7,8},{8,9},{9,10},{10,1... | collective-permute-start | bytes 24584 | tf_op jit(solution)/shard_map/ppermute | solution.py:25
  953.2 41.4 %collective-permute-start.24 = (bf16[1,64,64]{2,1,0:T(8,128)(2,1)}, bf16[1,64,64]{2,1,0:T(8,128)(2,1)}, u32[]{:S(2)}, u32[]{:S(2)}) collective-permute-start(bf16[1,64,64]{2,1,0:T(8,128)(2,1)} %get-tuple-element.6216), channel_id=1, source_target_pairs={{1,0},{2,1},{3,2},{4,3},{5,4},{6,5},{7,6},{8,7},{9,8},{10,9},{11,1... | collective-permute-start | bytes 24584 | tf_op jit(solution)/shard_map/ppermute | solution.py:28
  971.0 37.2 %collective-permute-start.39 = (bf16[1,64,64]{2,1,0:T(8,128)(2,1)}, bf16[1,64,64]{2,1,0:T(8,128)(2,1)}, u32[]{:S(2)}, u32[]{:S(2)}) collective-permute-start(bf16[1,64,64]{2,1,0:T(8,128)(2,1)} %get-tuple-element.6208), channel_id=1, source_target_pairs={{1,0},{2,1},{3,2},{4,3},{5,4},{6,5},{7,6},{8,7},{9,8},{10,9},{11,1... | collective-permute-start | bytes 24584 | tf_op jit(solution)/shard_map/ppermute | solution.py:28
  1014.6 37.9 %collective-permute-start.84 = (bf16[1,64,64]{2,1,0:T(8,128)(2,1)}, bf16[1,64,64]{2,1,0:T(8,128)(2,1)}, u32[]{:S(2)}, u32[]{:S(2)}) collective-permute-start(bf16[1,64,64]{2,1,0:T(8,128)(2,1)} %get-tuple-element.6184), channel_id=1, source_target_pairs={{1,0},{2,1},{3,2},{4,3},{5,4},{6,5},{7,6},{8,7},{9,8},{10,9},{11,1... | collective-permute-start | bytes 24584 | tf_op jit(solution)/shard_map/ppermute | solution.py:28
  1029.0 38.2 %collective-permute-start.99 = (bf16[1,64,64]{2,1,0:T(8,128)(2,1)}, bf16[1,64,64]{2,1,0:T(8,128)(2,1)}, u32[]{:S(2)}, u32[]{:S(2)}) collective-permute-start(bf16[1,64,64]{2,1,0:T(8,128)(2,1)} %get-tuple-element.6176), channel_id=1, source_target_pairs={{1,0},{2,1},{3,2},{4,3},{5,4},{6,5},{7,6},{8,7},{9,8},{10,9},{11,1... | collective-permute-start | bytes 24584 | tf_op jit(solution)/shard_map/ppermute | solution.py:28
  1043.8 39.1 %collective-permute-start.114 = (bf16[1,64,64]{2,1,0:T(8,128)(2,1)}, bf16[1,64,64]{2,1,0:T(8,128)(2,1)}, u32[]{:S(2)}, u32[]{:S(2)}) collective-permute-start(bf16[1,64,64]{2,1,0:T(8,128)(2,1)} %get-tuple-element.6168), channel_id=1, source_target_pairs={{1,0},{2,1},{3,2},{4,3},{5,4},{6,5},{7,6},{8,7},{9,8},{10,9},{11,1... | collective-permute-start | bytes 24584 | tf_op jit(solution)/shard_map/ppermute | solution.py:28
  1151.4 906.9 %collective-permute-start.12 = (bf16[16,32,64]{2,1,0:T(8,128)(2,1)}, bf16[16,32,64]{2,1,0:T(8,128)(2,1)}, u32[]{:S(2)}, u32[]{:S(2)}) collective-permute-start(bf16[16,32,64]{2,1,0:T(8,128)(2,1)} %copy-done.293), channel_id=1, source_target_pairs={{16,0},{17,1},{18,2},{19,3},{20,4},{21,5},{22,6},{23,7},{24,8},{25... | collective-permute-start | bytes 196616 | tf_op jit(solution)/shard_map/ppermute | solution.py:36
  1155.0 925.9 %collective-permute-start.27 = (bf16[16,32,64]{2,1,0:T(8,128)(2,1)}, bf16[16,32,64]{2,1,0:T(8,128)(2,1)}, u32[]{:S(2)}, u32[]{:S(2)}) collective-permute-start(bf16[16,32,64]{2,1,0:T(8,128)(2,1)} %copy-done.294), channel_id=1, source_target_pairs={{16,0},{17,1},{18,2},{19,3},{20,4},{21,5},{22,6},{23,7},{24,8},{25... | collective-permute-start | bytes 196616 | tf_op jit(solution)/shard_map/ppermute | solution.py:36
  1156.3 931.9 %collective-permute-start.42 = (bf16[16,32,64]{2,1,0:T(8,128)(2,1)}, bf16[16,32,64]{2,1,0:T(8,128)(2,1)}, u32[]{:S(2)}, u32[]{:S(2)}) collective-permute-start(bf16[16,32,64]{2,1,0:T(8,128)(2,1)} %copy-done.296), channel_id=1, source_target_pairs={{16,0},{17,1},{18,2},{19,3},{20,4},{21,5},{22,6},{23,7},{24,8},{25... | collective-permute-start | bytes 196616 | tf_op jit(solution)/shard_map/ppermute | solution.py:36
  1160.4 945.6 %collective-permute-start.57 = (bf16[16,32,64]{2,1,0:T(8,128)(2,1)}, bf16[16,32,64]{2,1,0:T(8,128)(2,1)}, u32[]{:S(2)}, u32[]{:S(2)}) collective-permute-start(bf16[16,32,64]{2,1,0:T(8,128)(2,1)} %copy-done.297), channel_id=1, source_target_pairs={{16,0},{17,1},{18,2},{19,3},{20,4},{21,5},{22,6},{23,7},{24,8},{25... | collective-permute-start | bytes 196616 | tf_op jit(solution)/shard_map/ppermute | solution.py:36
  1161.7 951.7 %collective-permute-start.72 = (bf16[16,32,64]{2,1,0:T(8,128)(2,1)}, bf16[16,32,64]{2,1,0:T(8,128)(2,1)}, u32[]{:S(2)}, u32[]{:S(2)}) collective-permute-start(bf16[16,32,64]{2,1,0:T(8,128)(2,1)} %copy-done.298), channel_id=1, source_target_pairs={{16,0},{17,1},{18,2},{19,3},{20,4},{21,5},{22,6},{23,7},{24,8},{25... | collective-permute-start | bytes 196616 | tf_op jit(solution)/shard_map/ppermute | solution.py:36
  2058.3 76.5 %collective-permute-start.87 = (bf16[16,32,64]{2,1,0:T(8,128)(2,1)}, bf16[16,32,64]{2,1,0:T(8,128)(2,1)}, u32[]{:S(2)}, u32[]{:S(2)}) collective-permute-start(bf16[16,32,64]{2,1,0:T(8,128)(2,1)} %copy-done.299), channel_id=1, source_target_pairs={{16,0},{17,1},{18,2},{19,3},{20,4},{21,5},{22,6},{23,7},{24,8},{25... | collective-permute-start | bytes 196616 | tf_op jit(solution)/shard_map/ppermute | solution.py:36
  2080.9 62.1 %collective-permute-start.102 = (bf16[16,32,64]{2,1,0:T(8,128)(2,1)}, bf16[16,32,64]{2,1,0:T(8,128)(2,1)}, u32[]{:S(2)}, u32[]{:S(2)}) collective-permute-start(bf16[16,32,64]{2,1,0:T(8,128)(2,1)} %get-tuple-element.3287), channel_id=1, source_target_pairs={{16,0},{17,1},{18,2},{19,3},{20,4},{21,5},{22,6},{23,7},{24,8},{25... | collective-permute-start | bytes 196616 | tf_op jit(solution)/shard_map/ppermute | solution.py:36
  2088.3 62.2 %collective-permute-start.117 = (bf16[16,32,64]{2,1,0:T(8,128)(2,1)}, bf16[16,32,64]{2,1,0:T(8,128)(2,1)}, u32[]{:S(2)}, u32[]{:S(2)}) collective-permute-start(bf16[16,32,64]{2,1,0:T(8,128)(2,1)} %get-tuple-element.3322), channel_id=1, source_target_pairs={{16,0},{17,1},{18,2},{19,3},{20,4},{21,5},{22,6},{23,7},{24,8},{25... | collective-permute-start | bytes 196616 | tf_op jit(solution)/shard_map/ppermute | solution.py:36
  2106.0 228.2 %collective-permute-start.120 = (bf16[32,64,128]{2,1,0:T(8,128)(2,1)}, bf16[32,64,128]{2,1,0:T(8,128)(2,1)}, u32[]{:S(2)}, u32[]{:S(2)}) collective-permute-start(bf16[32,64,128]{2,1,0:T(8,128)(2,1)} %copy-done.205), channel_id=1, source_target_pairs={{16,0},{17,1},{18,2},{19,3},{20,4},{21,5},{22,6},{23,7},{24,8},{25... | collective-permute-start | bytes 1572872 | tf_op jit(solution)/shard_map/ppermute | solution.py:36
  2113.4 224.2 %collective-permute-start.121 = (bf16[32,64,128]{2,1,0:T(8,128)(2,1)}, bf16[32,64,128]{2,1,0:T(8,128)(2,1)}, u32[]{:S(2)}, u32[]{:S(2)}) collective-permute-start(bf16[32,64,128]{2,1,0:T(8,128)(2,1)} %copy-done.207), channel_id=1, source_target_pairs={{16,0},{17,1},{18,2},{19,3},{20,4},{21,5},{22,6},{23,7},{24,8},{25... | collective-permute-start | bytes 1572872 | tf_op jit(solution)/shard_map/ppermute | solution.py:36
  2134.8 206.1 %collective-permute-start.122 = (bf16[32,64,128]{2,1,0:T(8,128)(2,1)}, bf16[32,64,128]{2,1,0:T(8,128)(2,1)}, u32[]{:S(2)}, u32[]{:S(2)}) collective-permute-start(bf16[32,64,128]{2,1,0:T(8,128)(2,1)} %get-tuple-element.3398), channel_id=1, source_target_pairs={{16,0},{17,1},{18,2},{19,3},{20,4},{21,5},{22,6},{23,7},{24,8},{25... | collective-permute-start | bytes 1572872 | tf_op jit(solution)/shard_map/ppermute | solution.py:36
  2214.1 98.6 %collective-permute-start.119 = (bf16[1,32,64]{2,1,0:T(8,128)(2,1)}, bf16[1,32,64]{2,1,0:T(8,128)(2,1)S(1)}, u32[]{:S(2)}, u32[]{:S(2)}) collective-permute-start(bf16[1,32,64]{2,1,0:T(8,128)(2,1)} %get-tuple-element.6230), channel_id=1, source_target_pairs={{1,0},{2,1},{3,2},{4,3},{5,4},{6,5},{7,6},{8,7},{9,8},{10,9},{11,1... | collective-permute-start | bytes 12296 | tf_op jit(solution)/shard_map/ppermute | solution.py:28
  2215.4 98.6 %collective-permute-start.118 = (bf16[1,32,64]{2,1,0:T(8,128)(2,1)}, bf16[1,32,64]{2,1,0:T(8,128)(2,1)}, u32[]{:S(2)}, u32[]{:S(2)}) collective-permute-start(bf16[1,32,64]{2,1,0:T(8,128)(2,1)} %get-tuple-element.6229), channel_id=1, source_target_pairs={{0,1},{1,2},{2,3},{3,4},{4,5},{5,6},{6,7},{7,8},{8,9},{9,10},{10,1... | collective-permute-start | bytes 12296 | tf_op jit(solution)/shard_map/ppermute | solution.py:25
  (415 other events, 16947.7 us)
Sparse Core Ops, SparseCore 0:
  2334.3 140.9 all-reduce.51
where the time goes:
time: 2530 us; the launch traced here: 2510 us
  waiting for transfers between devices  994 us (39%)
  local copies, waits for them, and re-layouts  608 us (24%)
  starting transfers between devices  441 us (17%)
  matrix products  186 us (7%)
  other arithmetic  179 us (7%)
  blocking collectives  48.9 us (2%)
  between operations  26.2 us (1%)
    ppermute x32, waiting for transfers between devices, from_behind(): return lax.ppermute(x, axis, pairs)  929 us
    ppermute x48, starting transfers between devices, with_halo(): lax.ppermute(lax.slice_in_dim(block, block.shape[dim] - width, None, axis...  299 us
    another operation x200, local copies, waits for them, and re-layouts  184 us
    another operation x8, local copies, waits for them, and re-layouts, patchify(): picture.reshape(num_rows, 4, num_cols, 4, 3).transpose(0, 2, 1, 3, 4)  122 us
    dot_general x72, matrix products, matmul(): return jnp.dot(x, w, preferred_element_type=jnp.float32)  99.6 us
    transpose x40, local copies, waits for them, and re-layouts, patchify(): return picture.reshape(num_rows, 4, num_cols, 4, 3).transpose(0, 2, 1, 3,...  83.4 us
    ppermute x32, starting transfers between devices, from_behind(): return lax.ppermute(x, axis, pairs)  79.7 us
    dot_general x48, matrix products, weight_grad(): lax.dot_general(x, grad, (((0, 1), (0, 1)), ((), ())), preferred_element_...  71.6 us
  transfers between devices with their start and end apart: 129, of which 6 were waited for; matrix products, arithmetic and copies ran while one was open for 36% of the time, Pallas kernels for 0%

commit v1 on v0

v1 whole, which is shorter than its diff:
```python
import functools

import jax
import jax.numpy as jnp
from jax import lax
from jax.experimental import pallas as pl
from jax.experimental.pallas import tpu as pltpu
from jax.sharding import PartitionSpec as P

STEP = 10
COMMIT_WEIGHT = 0.25
CODE_DECAY = 0.9
CLIP_NORM = 0.001
LEARN_RATE = 0.03
MOMENT_ONE = 0.9
MOMENT_TWO = 0.999
WEIGHT_DECAY = 0.01
ADAM_EPSILON = 1e-08

F32 = jnp.float32
BF16 = jnp.bfloat16
VMEM_LIMIT = 56 * 1024 * 1024
CHUNK = 8

CONV_ROWS = 640
ROW_RES = 3 * CONV_ROWS
ROW_FROM = ROW_RES + 3 * 64
ROW_PIXEL = ROW_FROM + 5 * 64
ROW_DOWN = ROW_PIXEL + 2 * 48
ROW_SUMS = ROW_DOWN + 512
ROW_COUNT = ROW_SUMS + 512
ROW_DEAD = ROW_COUNT + 8
ROW_NUMER = ROW_DEAD + 8
ROW_END = ROW_NUMER + 8


def mm(x, w):
    return lax.dot_general(x, w, (((1,), (0,)), ((), ())), preferred_element_type=F32)


def mm_t(x, w):
    return lax.dot_general(x, w, (((1,), (1,)), ((), ())), preferred_element_type=F32)


def mm_w(x, g):
    return lax.dot_general(x, g, (((0,), (0,)), ((), ())), preferred_element_type=F32)


def lane_iota(shape):
    return lax.broadcasted_iota(jnp.int32, shape, len(shape) - 1)


def low_half(shape):
    return lane_iota(shape) % 128 < 64


def sigmoid(x):
    return 0.5 * jnp.tanh(0.5 * x) + 0.5


def slope(a):
    s = sigmoid(a)
    return s * (1.0 + a * (1.0 - s))


def shift_rows(x, by):
    rows = x.shape[1]
    moved = pltpu.roll(x, by % rows, 1)
    ids = lax.broadcasted_iota(jnp.int32, x.shape, 1)
    edge = 0 if by == 1 else rows - 1
    return jnp.where(ids == edge, 0.0, moved)


def flat(x):
    return x.reshape(x.shape[0] * x.shape[1], x.shape[2])


def pair_diag(w):
    zero = jnp.zeros_like(w)
    return jnp.concatenate(
        [jnp.concatenate([w, zero], axis=1), jnp.concatenate([zero, w], axis=1)], axis=0
    )


def swap_halves(x):
    return pltpu.roll(x, 64, len(x.shape) - 1)


def compute_kernel(
    place,
    valid_s,
    dead_source,
    valid_v,
    pix,
    ct_col,
    cb_col,
    ct_row,
    cb_row,
    w_conv,
    w_res,
    w_from,
    w_to,
    w_pix,
    w_down,
    book,
    out,
    b_fwd,
    b_bwd,
    wo_d,
    from_d,
    to_d,
    up_d,
    pix_d,
    down_b,
    book_a,
    book_b,
    sel,
    patches,
    stem,
    up,
    near,
    near_t,
    xs_dec,
    xs_bot,
    xs_top,
    wide,
    res,
    act_dec,
    act_bot,
    act_top,
    low_dec,
    low_bot,
    low_top,
    lat,
    lat_t,
    resid,
    grad_hi,
    grad_lo,
    d_two,
    d_slots,
    d_two_t,
    d_slots_t,
    gstem,
    gup,
    acc_conv,
    acc_res,
    acc_from,
    acc_up,
    acc_to,
    acc_pix,
    acc_down,
    acc_sums,
    acc_count,
    acc_dead,
    acc_num,
):
    step = pl.program_id(0)
    last = pl.num_programs(0) - 1
    pairs, rows = xs_bot.shape[0], xs_bot.shape[2]
    pairs_t = xs_top.shape[0]
    ch = CHUNK
    ch_t = CHUNK // 2
    valid_count = 3.0 * pix.shape[1] * jnp.sum(valid_v[...].astype(F32))
    loss_slope = 2.0 / valid_count
    commit_slope = loss_slope * COMMIT_WEIGHT

    def loop(total, size, fn):
        def run(k, _):
            fn(pl.multiple_of(k * size, size))
            return 0

        lax.fori_loop(0, total // size, run, 0)

    @pl.when(step == 0)
    def _():
        for ref in (acc_conv, acc_res, acc_from, acc_up, acc_to, acc_pix, acc_down, acc_sums, acc_count, acc_dead, acc_num):
            ref[...] = jnp.zeros(ref.shape, F32)
        wide[...] = jnp.zeros(wide.shape, F32)
        d_two[...] = jnp.zeros(d_two.shape, F32)
        d_two_t[...] = jnp.zeros(d_two_t.shape, F32)
        zero = jnp.zeros((128, 64), F32)
        for k in range(3):
            for i in range(3):
                t = [w_conv[k, pl.ds((i * 3 + j) * 128, 128), :] for j in range(3)]
                even = jnp.concatenate([t[1], t[0], zero, t[2]], axis=1).astype(BF16)
                odd = jnp.concatenate([t[2], t[1], t[0], zero], axis=1).astype(BF16)
                b_fwd[k, pl.ds(i * 256, 128), :] = even
                b_fwd[k, pl.ds(i * 256 + 128, 128), :] = odd
                b_bwd[k, pl.ds(0, 128), pl.ds((2 - i) * 256, 256)] = even
                b_bwd[k, pl.ds(128, 128), pl.ds((2 - i) * 256, 256)] = odd
            wo_d[k] = pair_diag(w_res[k]).astype(BF16)
        from_d[...] = pair_diag(w_from[0]).astype(BF16)
        for k in range(2):
            to_d[k] = pair_diag(w_to[k]).astype(BF16)
        up_d[...] = pair_diag(
            jnp.concatenate([w_from[k] for k in range(1, 5)], axis=1)
        ).astype(BF16)
        lane = lax.broadcasted_iota(jnp.int32, (128, 48), 0)
        tap = lax.broadcasted_iota(jnp.int32, (128, 48), 1)
        for k in range(2):
            low = w_pix[k].astype(BF16)
            for cp in range(2):
                pick = (lane == (tap // 12) * 24 + cp * 12 + tap % 12).astype(F32).astype(BF16)
                pix_d[k, :, pl.ds(cp * 128, 128)] = mm(pick, low).astype(BF16)
        for k in range(4):
            down_b[pl.ds(k * 128, 128), :] = w_down[k].astype(BF16)
        for k in range(2):
            full = book[k]
            hi = full.astype(BF16).astype(F32)
            mid = (full - hi).astype(BF16).astype(F32)
            lo = full - hi - mid
            empty = jnp.zeros_like(full)
            book_a[k] = jnp.concatenate([hi, mid, lo, empty], axis=1).astype(BF16)
            book_b[k] = jnp.concatenate([mid, hi, empty, lo], axis=1).astype(BF16)
        height = pix.shape[1]
        o = lax.broadcasted_iota(jnp.int32, (height, height), 0)
        s = lax.broadcasted_iota(jnp.int32, (height, height), 1)
        quarter = height // 4
        src = 8 * (o % rows) + 4 * ((o % quarter) // rows) + o // quarter
        sel[...] = (s == src).astype(F32).astype(BF16)

    def near_of(col, level):
        n = col.shape[0]
        codes = lax.broadcasted_iota(jnp.int32, (n, book.shape[1]), 1)
        v = []
        for cp, table in ((0, book_a), (1, book_b)):
            hot = (col[:, cp : cp + 1] == codes).astype(F32).astype(BF16)
            v.append(mm(hot, table[level]))
        half = low_half((n, 128))
        hi = jnp.where(half, v[0][:, :128], v[1][:, :128])
        mid = swap_halves(jnp.where(half, v[1][:, :128], v[0][:, :128]))
        lo = jnp.where(half, v[0][:, 128:], v[1][:, 128:])
        return hi, hi + mid + lo

    def top_codes(c0):
        hi, full = near_of(ct_col[0, pl.ds(c0 * rows, ch_t * rows), :], 0)
        near_t[pl.ds(c0 * rows, ch_t * rows), :] = full
        u = mm(hi.astype(BF16), up_d[...]).reshape(ch_t, rows, 1024)
        for cq in range(2):
            for rp in range(2):
                for c in range(ch_t):
                    at = (cq * 2 + rp) * 256
                    up[2 * (c0 + c) + cq, rp] = u[c, :, at : at + 256]

    loop(pairs_t, ch_t, top_codes)

    def put_slots(ref, c0, n, even, odd):
        ref[pl.ds(c0, n), 0] = shift_rows(odd, 1).astype(BF16)
        ref[pl.ds(c0, n), 1] = even.astype(BF16)
        ref[pl.ds(c0, n), 2] = odd.astype(BF16)
        ref[pl.ds(c0, n), 3] = shift_rows(even, -1).astype(BF16)

    def bottom_codes(c0):
        n = ch * 2 * rows
        hi, full = near_of(cb_col[0, pl.ds(c0 * 2 * rows, n), :], 1)
        near[pl.ds(c0 * 2 * rows, n), :] = full
        x = mm(hi.astype(BF16), from_d[...]).reshape(ch, 2, rows, 256) + up[pl.ds(c0, ch)]
        res[pl.ds(c0, ch)] = x
        put_slots(xs_dec, c0, ch, x[:, 0], x[:, 1])

    loop(pairs, ch, bottom_codes)

    def conv_wide(xs, k):
        def run(c0):
            for rp in range(2):
                taps = jnp.concatenate(
                    [flat(xs[pl.ds(c0, ch), rp + t]) for t in range(3)], axis=1
                )
                y = mm(taps, b_fwd[k])
                wide[pl.ds(c0 + 1, ch), rp] = y.reshape(ch, rows, 256)

        loop(pairs, ch, run)

    def gather_wide(c0, n, rp):
        before = wide[pl.ds(c0, n), rp, :, 128:]
        after = wide[pl.ds(c0 + 2, n), rp, :, 128:]
        return wide[pl.ds(c0 + 1, n), rp, :, :128] + jnp.where(low_half(before.shape), before, after)

    conv_wide(xs_dec, 2)

    def decode_out(c0):
        a = jnp.stack([gather_wide(c0, ch, rp) for rp in range(2)], axis=1)
        n = ch * 2 * rows
        a = a.reshape(n, 128)
        act_dec[pl.ds(c0 * 2 * rows, n), :] = a
        hidden = (a * sigmoid(a)).astype(BF16)
        y = res[pl.ds(c0, ch)].reshape(n, 256) + mm(hidden, wo_d[2])
        low = y.astype(BF16)
        low_dec[pl.ds(c0 * 2 * rows, n), :] = low
        resid[pl.ds(c0 * 2 * rows, n), :] = mm_t(low, pix_d[1])

    loop(pairs, ch, decode_out)

    per_tile = 2 * rows
    picked = mm(sel[...], pix[0])
    wide_px = pix.shape[2]
    lanes24 = lane_iota((per_tile, 128))
    for c2 in range(pairs):
        tile = jnp.zeros((per_tile, 128), F32)
        for i in range(4):
            start = 24 * c2
            want = 24 * i
            block = start // 128
            row = picked[i * per_tile : (i + 1) * per_tile]
            part = row[:, block * 128 : block * 128 + 128]
            part = pltpu.roll(part, (want - start % 128) % 128, 1)
            inside = min(24, 128 - start % 128)
            tile = jnp.where((lanes24 >= want) & (lanes24 < want + inside), part, tile)
            if inside < 24:
                part = row[:, block * 128 + 128 : block * 128 + 256]
                part = pltpu.roll(part, want + inside, 1)
                tile = jnp.where((lanes24 >= want + inside) & (lanes24 < want + 24), part, tile)
        patches[c2 * per_tile : (c2 + 1) * per_tile, :] = tile.astype(BF16)

    def stem_of(c0):
        n = ch * 2 * rows
        pre = mm(patches[pl.ds(c0 * 2 * rows, n), :], pix_d[0])
        s = (pre * sigmoid(pre)).astype(BF16)
        stem[pl.ds(c0, ch)] = s.reshape(ch, 2, rows, 256)

    loop(pairs, ch, stem_of)

    def top_in(c0):
        for cq in range(2):
            pieces = [stem[2 * (c0 + c) + cq, rp] for c in range(ch_t) for rp in range(2)]
            taps = jnp.concatenate(
                [jnp.concatenate(pieces[2 * c : 2 * c + 2], axis=1) for c in range(ch_t)], axis=0
            )
            x = mm(taps, down_b[...]).reshape(ch_t, rows, 128)
            grad_hi[pl.ds(c0, ch_t), 0, :, pl.ds(cq * 128, 128)] = x
            xs_top[pl.ds(c0, ch_t), 0, :, pl.ds(cq * 128, 128)] = shift_rows(x, 1).astype(BF16)
            xs_top[pl.ds(c0, ch_t), 1, :, pl.ds(cq * 128, 128)] = x.astype(BF16)
            xs_top[pl.ds(c0, ch_t), 2, :, pl.ds(cq * 128, 128)] = shift_rows(x, -1).astype(BF16)

    loop(pairs_t, ch_t, top_in)

    wide[pairs_t + 1, 0] = jnp.zeros((rows, 256), F32)

    def top_conv(c0):
        taps = jnp.concatenate([flat(xs_top[pl.ds(c0, ch_t), t]) for t in range(3)], axis=1)
        wide[pl.ds(c0 + 1, ch_t), 0] = mm(taps, b_fwd[0]).reshape(ch_t, rows, 256)

    loop(pairs_t, ch_t, top_conv)

    def add_num(x):
        acc_num[...] += jnp.sum(x.reshape(x.shape[0] // 8, 8, 128), axis=0)

    def top_out(c0):
        n = ch_t * rows
        here = pl.ds(c0 * rows, n)
        a = flat(gather_wide(c0, ch_t, 0))
        act_top[here, :] = a
        hidden = (a * sigmoid(a)).astype(BF16)
        y = flat(grad_hi[pl.ds(c0, ch_t), 0]) + mm(hidden, wo_d[0])
        low = y.astype(BF16)
        low_top[here, :] = low
        latent = mm(low, to_d[0])
        lat_t[here, :] = latent
        diff = latent - near_t[here, :]
        add_num(COMMIT_WEIGHT * diff * diff)

    loop(pairs_t, ch_t, top_out)

    def bottom_in(c0):
        x = stem[pl.ds(c0, ch)].astype(F32) + up[pl.ds(c0, ch)]
        res[pl.ds(c0, ch)] = x
        put_slots(xs_bot, c0, ch, x[:, 0], x[:, 1])

    loop(pairs, ch, bottom_in)
    conv_wide(xs_bot, 1)

    def bottom_out(c0):
        n = ch * 2 * rows
        here = pl.ds(c0 * 2 * rows, n)
        a = jnp.stack([gather_wide(c0, ch, rp) for rp in range(2)], axis=1).reshape(n, 128)
        act_bot[here, :] = a
        hidden = (a * sigmoid(a)).astype(BF16)
        y = res[pl.ds(c0, ch)].reshape(n, 256) + mm(hidden, wo_d[1])
        low = y.astype(BF16)
        low_bot[here, :] = low
        latent = mm(low, to_d[1])
        lat[here, :] = latent
        diff = latent - near[here, :]
        add_num(COMMIT_WEIGHT * diff * diff)

    loop(pairs, ch, bottom_out)

    def level_stats(level, lat_ref, row_ref, total):
        size = 256

        def run(p0):
            latent = lat_ref[pl.ds(p0, size), :]
            hi = latent.astype(BF16)
            lo = (latent - hi.astype(F32)).astype(BF16)
            both = jnp.concatenate([hi, lo], axis=1)
            codes = lax.broadcasted_iota(jnp.int32, (book.shape[1], size), 0)
            half = low_half((book.shape[1], 128))
            parts = []
            for cp in range(2):
                hot = (row_ref[0, cp : cp + 1, pl.ds(p0, size)] == codes).astype(F32)
                acc_count[level] += hot[:, :128] + hot[:, 128:]
                s = mm(hot.astype(BF16), both)
                parts.append(s[:, :128] + s[:, 128:])
            acc_sums[level] += jnp.where(half, parts[0], parts[1])

        loop(total, size, run)

    level_stats(0, lat_t, ct_row, pairs_t * rows)
    level_stats(1, lat, cb_row, pairs * 2 * rows)

    micro = place[0] + step
    image = place[1]
    images = valid_s.shape[1]
    for level, lat_ref in ((0, lat_t), (1, lat)):
        side = pairs * (level + 1)
        for r in range(8):
            pos = dead_source[level, r]
            col = lax.rem(pos, side)
            row_all = lax.div(pos, side)
            row = lax.rem(row_all, side)
            img_all = lax.div(row_all, side)
            mine = (lax.rem(img_all, images) == image) & (lax.div(img_all, images) == micro)
            if level == 0:
                local = lax.div(col, 2) * rows + row
            else:
                local = lax.div(col, 2) * (2 * rows) + lax.rem(row, 2) * rows + lax.div(row, 2)
            line = lat_ref[pl.ds(local, 1), :]
            odd = lax.rem(col, 2)
            line = jnp.where(low_half(line.shape) == (odd == 0), line, 0.0)
            line = line + swap_halves(line)
            line = jnp.where(low_half(line.shape) == (level == 0), line, 0.0)
            acc_dead[pl.ds(r, 1), :] += line * mine.astype(F32)

    limit = valid_s[micro, image]

    def decode_back(c0):
        n = ch * 2 * rows
        here = pl.ds(c0 * 2 * rows, n)
        lane = lane_iota((ch, 2, rows, 128))
        pixel_row = (
            8 * lax.broadcasted_iota(jnp.int32, lane.shape, 2)
            + 4 * lax.broadcasted_iota(jnp.int32, lane.shape, 1)
            + lane // 24
        )
        keep = ((pixel_row < limit) & (lane < 96)).astype(F32).reshape(n, 128)
        p = patches[here, :]
        diff = keep * (resid[here, :] - p.astype(F32))
        add_num(diff * diff)
        g_re = (loss_slope * diff).astype(BF16)
        acc_pix[1] += mm_w(g_re, low_dec[here, :])
        g = mm(g_re, pix_d[1])
        grad_hi[pl.ds(c0, ch)] = g.reshape(ch, 2, rows, 256)
        res_back(g, act_dec[here, :], 2, c0)

    def res_back(g, a, k, c0):
        n = ch * 2 * rows
        g_low = g.astype(BF16)
        s = sigmoid(a)
        hidden = (a * s).astype(BF16)
        acc_res[k] += mm_w(hidden, g_low)
        d = (mm_t(g_low, wo_d[k]) * (s * (1.0 + a * (1.0 - s)))).astype(BF16)
        d_two[pl.ds(c0 + 1, ch)] = d.astype(F32).reshape(ch, 2, rows, 128)

    def conv_back(k, xs, c0):
        outs = []
        total = None
        here = d_two[pl.ds(c0 + 1, ch)]
        before = d_two[pl.ds(c0, ch)]
        after = d_two[pl.ds(c0 + 2, ch)]
        d = jnp.concatenate([here, jnp.where(low_half(here.shape), after, before)], axis=3)
        put_slots(d_slots, c0, ch, d[:, 0], d[:, 1])
        for rp in range(2):
            taps = jnp.concatenate(
                [flat(d_slots[pl.ds(c0, ch), rp + t]) for t in range(3)], axis=1
            )
            outs.append(mm_t(taps, b_bwd[k]).reshape(ch, rows, 256))
            part = mm_w(flat(xs[pl.ds(c0, ch), rp + 1]), taps)
            total = part if total is None else total + part
        acc_conv[k] += total
        return jnp.stack(outs, axis=1)

    loop(pairs, ch, decode_back)

    def decode_in_back(c0):
        n = ch * 2 * rows
        here = pl.ds(c0 * 2 * rows, n)
        g = grad_hi[pl.ds(c0, ch)] + conv_back(2, xs_dec, c0)
        gup[pl.ds(c0, ch)] = g
        g_low = g.reshape(n, 256).astype(BF16)
        full = near[here, :]
        acc_from[...] += mm_w(full.astype(BF16), g_low)
        g_lat = mm_t(g_low, from_d[...]) + commit_slope * (lat[here, :] - full)
        g_lat = g_lat.astype(BF16)
        acc_to[1] += mm_w(low_bot[here, :], g_lat)
        grad_hi[pl.ds(c0, ch)] = mm_t(g_lat, to_d[1]).reshape(ch, 2, rows, 256)

    loop(pairs, ch, decode_in_back)

    def bottom_back(c0):
        n = ch * 2 * rows
        res_back(
            grad_hi[pl.ds(c0, ch)].reshape(n, 256), act_bot[pl.ds(c0 * 2 * rows, n), :], 1, c0
        )

    loop(pairs, ch, bottom_back)

    def bottom_in_back(c0):
        g = grad_hi[pl.ds(c0, ch)] + conv_back(1, xs_bot, c0)
        gstem[pl.ds(c0, ch)] = g.astype(BF16)
        total = (g + gup[pl.ds(c0, ch)]).astype(BF16)
        half = ch // 2
        total = total.reshape(half, 2, 2, rows, 256)
        wide_g = jnp.concatenate(
            [total[:, cq, rp].reshape(half * rows, 256) for cq in range(2) for rp in range(2)],
            axis=1,
        )
        t0 = pl.multiple_of(lax.div(c0, 2) * rows, half * rows)
        here = pl.ds(t0, half * rows)
        full = near_t[here, :]
        acc_up[...] += mm_w(full.astype(BF16), wide_g)
        g_q = mm_t(wide_g, up_d[...]).astype(BF16).astype(F32)
        g_lat = (g_q + commit_slope * (lat_t[here, :] - full)).astype(BF16)
        acc_to[0] += mm_w(low_top[here, :], g_lat)
        g_top = mm_t(g_lat, to_d[0])
        grad_lo[here, :] = g_top
        g_low = g_top.astype(BF16)
        a = act_top[here, :]
        s = sigmoid(a)
        acc_res[0] += mm_w((a * s).astype(BF16), g_low)
        d = (mm_t(g_low, wo_d[0]) * (s * (1.0 + a * (1.0 - s)))).astype(BF16)
        d_two_t[pl.ds(lax.div(c0, 2) + 1, half)] = d.astype(F32).reshape(half, rows, 128)

    loop(pairs, ch, bottom_in_back)

    def top_back(c0):
        n = ch_t * rows
        here = d_two_t[pl.ds(c0 + 1, ch_t)]
        before = d_two_t[pl.ds(c0, ch_t)]
        after = d_two_t[pl.ds(c0 + 2, ch_t)]
        d = jnp.concatenate([here, jnp.where(low_half(here.shape), after, before)], axis=2)
        taps = jnp.concatenate(
            [
                flat(shift_rows(d, 1)).astype(BF16),
                flat(d).astype(BF16),
                flat(shift_rows(d, -1)).astype(BF16),
            ],
            axis=1,
        )
        acc_conv[0] += mm_w(flat(xs_top[pl.ds(c0, ch_t), 1]), taps)
        g = grad_lo[pl.ds(c0 * rows, n), :] + mm_t(taps, b_bwd[0])
        g_low = g.astype(BF16).reshape(ch_t, rows, 256)
        for cq in range(2):
            g_cq = flat(g_low[:, :, cq * 128 : cq * 128 + 128])
            pieces = [stem[2 * (c0 + c) + cq, rp] for c in range(ch_t) for rp in range(2)]
            taps_s = jnp.concatenate(
                [jnp.concatenate(pieces[2 * c : 2 * c + 2], axis=1) for c in range(ch_t)], axis=0
            )
            acc_down[...] += mm_w(taps_s, g_cq)
            g_st = mm_t(g_cq, down_b[...]).reshape(ch_t, rows, 512)
            for c in range(ch_t):
                col = 2 * (c0 + c) + cq
                p = patches[pl.ds(pl.multiple_of(col * 2 * rows, 2 * rows), 2 * rows), :]
                sl = slope(mm(p, pix_d[0]))
                g_t = jnp.concatenate([g_st[c, :, :256], g_st[c, :, 256:]], axis=0)
                g_b = gstem[col].reshape(2 * rows, 256).astype(F32)
                both = jnp.concatenate([(g_t * sl).astype(BF16), (g_b * sl).astype(BF16)], axis=0)
                acc_pix[0] += mm_w(jnp.concatenate([p, p], axis=0), both)

    loop(pairs_t, ch_t, top_back)

    @pl.when(step == last)
    def _():
        half = low_half((128, 128))
        zero = jnp.zeros((128, 128), F32)

        def to_sum(k):
            return acc_to[k, :128, :] + swap_halves(acc_to[k, 128:, :])

        for k in range(3):
            twos = []
            for i in range(3):
                lanes = (2 - i) * 256
                e0 = acc_conv[k, :128, lanes : lanes + 128]
                e1 = acc_conv[k, :128, lanes + 128 : lanes + 256]
                o0 = acc_conv[k, 128:, lanes : lanes + 128]
                o1 = acc_conv[k, 128:, lanes + 128 : lanes + 256]
                first = e0 + swap_halves(jnp.where(half, o1, o0))
                out[k * CONV_ROWS + i * 128 : k * CONV_ROWS + i * 128 + 128, :] = first
                twos.append(o0 + swap_halves(e1))
            base = k * CONV_ROWS + 384
            out[base : base + 128, :] = jnp.where(half, twos[0], swap_halves(twos[1]))
            other = swap_halves(to_sum(k)) if k < 2 else zero
            out[base + 128 : base + 256, :] = jnp.where(half, twos[2], other)
            out[ROW_RES + k * 64 : ROW_RES + k * 64 + 64, :] = (
                acc_res[k, :64, :128] + acc_res[k, 64:, 128:]
            )
        out[ROW_FROM : ROW_FROM + 64, :] = acc_from[:64, :128] + acc_from[64:, 128:]
        for k in range(4):
            out[ROW_FROM + (k + 1) * 64 : ROW_FROM + (k + 2) * 64, :] = (
                acc_up[:64, k * 128 : k * 128 + 128] + acc_up[64:, 512 + k * 128 : 640 + k * 128]
            )
        for k in range(2):
            for i in range(4):
                even = acc_pix[k, 24 * i : 24 * i + 12, :128]
                odd = acc_pix[k, 24 * i + 12 : 24 * i + 24, 128:]
                at = ROW_PIXEL + k * 48 + i * 12
                out[at : at + 12, :] = even + odd
        out[ROW_DOWN : ROW_DOWN + 512, :] = acc_down[...]
        top = acc_sums[0] + swap_halves(acc_sums[0])
        bottom = acc_sums[1] + swap_halves(acc_sums[1])
        out[ROW_SUMS : ROW_SUMS + 512, :] = jnp.where(low_half(top.shape), top, bottom)
        same = lax.broadcasted_iota(jnp.int32, (128, 128), 0) == lane_iota((128, 128))
        for level in range(2):
            for b in range(4):
                col = jnp.sum(acc_count[level, b * 128 : b * 128 + 128, :], axis=1, keepdims=True)
                line = jnp.sum(jnp.where(same, col, 0.0), axis=0, keepdims=True)
                at = ROW_COUNT + level * 4 + b
                out[at : at + 1, :] = line
        out[ROW_DEAD : ROW_DEAD + 8, :] = acc_dead[...]
        out[ROW_NUMER : ROW_NUMER + 8, :] = acc_num[...]
        if out.shape[0] > ROW_END:
            out[ROW_END:, :] = jnp.zeros((out.shape[0] - ROW_END, 128), F32)


def compute(place, valid_rows, dead_source, pix, ct, cb, weights, book, total_rows):
    share, height, _ = pix.shape
    pairs = height // 8
    rows = height // 8
    pairs_t = pairs // 2
    n = pairs * 2 * rows
    n_t = pairs_t * rows
    ct_col, ct_row = ct
    cb_col, cb_row = cb
    smem = pl.BlockSpec(memory_space=pltpu.SMEM)

    def whole(x):
        zeros = (0,) * len(x.shape)
        return pl.BlockSpec(x.shape, lambda i: zeros)

    def each(x):
        zeros = (0,) * (len(x.shape) - 1)
        return pl.BlockSpec((1,) + x.shape[1:], lambda i: (i,) + zeros)

    v = pltpu.VMEM
    scratch = [
        v((3, 768, 256), BF16),
        v((3, 256, 768), BF16),
        v((3, 128, 256), BF16),
        v((128, 256), BF16),
        v((2, 256, 128), BF16),
        v((128, 1024), BF16),
        v((2, 128, 256), BF16),
        v((512, 128), BF16),
        v((2, 512, 256), BF16),
        v((2, 512, 256), BF16),
        v((height, height), BF16),
        v((n, 128), BF16),
        v((pairs, 2, rows, 256), BF16),
        v((pairs, 2, rows, 256), F32),
        v((n, 128), F32),
        v((n_t, 128), F32),
        v((pairs, 4, rows, 256), BF16),
        v((pairs, 4, rows, 256), BF16),
        v((pairs_t, 3, rows, 256), BF16),
        v((pairs + 2, 2, rows, 256), F32),
        v((pairs, 2, rows, 256), F32),
        v((n, 128), F32),
        v((n, 128), F32),
        v((n_t, 128), F32),
        v((n, 256), BF16),
        v((n, 256), BF16),
        v((n_t, 256), BF16),
        v((n, 128), F32),
        v((n_t, 128), F32),
        v((n, 128), F32),
        v((pairs, 2, rows, 256), F32),
        v((n_t, 256), F32),
        v((pairs + 2, 2, rows, 128), F32),
        v((pairs, 4, rows, 256), BF16),
        v((pairs_t + 2, rows, 128), F32),
        v((8, 128), BF16),
        v((pairs, 2, rows, 256), BF16),
        v((pairs, 2, rows, 256), F32),
        v((3, 256, 768), F32),
        v((3, 128, 256), F32),
        v((128, 256), F32),
        v((128, 1024), F32),
        v((2, 256, 128), F32),
        v((2, 128, 256), F32),
        v((512, 128), F32),
        v((2, 512, 128), F32),
        v((2, 512, 128), F32),
        v((8, 128), F32),
        v((8, 128), F32),
    ]
    return pl.pallas_call(
        compute_kernel,
        grid=(share,),
        out_shape=jax.ShapeDtypeStruct((total_rows, 128), F32),
        in_specs=[smem, smem, smem, whole(valid_rows), each(pix), each(ct_col), each(cb_col), each(ct_row), each(cb_row)]
        + [whole(w) for w in weights]
        + [whole(book)],
        out_specs=pl.BlockSpec((total_rows, 128), lambda i: (0, 0)),
        scratch_shapes=scratch,
        compiler_params=pltpu.CompilerParams(
            dimension_semantics=("arbitrary",), vmem_limit_bytes=VMEM_LIMIT
        ),
        name="step_compute",
    )(place, valid_rows, dead_source, valid_rows, pix, ct_col, cb_col, ct_row, cb_row, *weights, book)


def update_kernel(dead_codes, valid_v, total, *refs):
    w, m, v = refs[0:6], refs[6:12], refs[12:18]
    ema_count, ema_sum = refs[18:20]
    norm_o, pair_o = refs[20:22]
    new_o, mom_o, sec_o, low_o = refs[22:28], refs[28:34], refs[34:40], refs[40:46]
    book_o, count_o, sum_o = refs[46:49]
    grads = total[0:ROW_SUMS, :]
    squares = jnp.sum(jnp.sum((grads * grads).reshape(ROW_SUMS // 8, 8, 128), axis=0))
    norm = jnp.sqrt(jnp.full((8, 128), squares, F32))
    norm_o[0] = norm[0, 0]
    factor = (CLIP_NORM / jnp.maximum(norm, CLIP_NORM))[0, 0]
    pair_o[0] = jnp.sum(total[ROW_NUMER : ROW_NUMER + 8, :])
    pair_o[1] = 3.0 * 256.0 * jnp.sum(valid_v[...].astype(F32))

    def apply(t, index, grad):
        g = grad * factor
        first = MOMENT_ONE * m[t][index] + (1.0 - MOMENT_ONE) * g
        second = MOMENT_TWO * v[t][index] + (1.0 - MOMENT_TWO) * g * g
        step = first / (1.0 - MOMENT_ONE**STEP) / (
            jnp.sqrt(second / (1.0 - MOMENT_TWO**STEP)) + ADAM_EPSILON
        )
        weight = w[t][index]
        fresh = weight - LEARN_RATE * (step + WEIGHT_DECAY * weight)
        new_o[t][index] = fresh
        mom_o[t][index] = first
        sec_o[t][index] = second
        low_o[t][index] = fresh.astype(BF16)

    for k in range(3):
        base = k * CONV_ROWS
        for i in range(3):
            both = total[base + i * 128 : base + i * 128 + 128, :]
            apply(0, (k, pl.ds((i * 3 + 1) * 128, 128)), both[:, :64])
            apply(0, (k, pl.ds(i * 3 * 128, 128)), swap_halves(both)[:, :64])
        both = total[base + 384 : base + 512, :]
        apply(0, (k, pl.ds(2 * 128, 128)), both[:, :64])
        apply(0, (k, pl.ds(5 * 128, 128)), swap_halves(both)[:, :64])
        both = total[base + 512 : base + 640, :]
        apply(0, (k, pl.ds(8 * 128, 128)), both[:, :64])
        if k < 2:
            apply(3, (k,), swap_halves(both)[:, :64])
        apply(1, (k,), total[ROW_RES + k * 64 : ROW_RES + k * 64 + 64, :])
    for k in range(5):
        apply(2, (k,), total[ROW_FROM + k * 64 : ROW_FROM + k * 64 + 64, :])
    for k in range(2):
        apply(4, (k,), total[ROW_PIXEL + k * 48 : ROW_PIXEL + k * 48 + 48, :])
    for k in range(4):
        apply(5, (k,), total[ROW_DOWN + k * 128 : ROW_DOWN + k * 128 + 128, :])

    same = lax.broadcasted_iota(jnp.int32, (128, 128), 0) == lane_iota((128, 128))
    sums = total[ROW_SUMS : ROW_SUMS + 512, :]
    dead = total[ROW_DEAD : ROW_DEAD + 8, :]
    for level in range(2):
        mine = (sums if level == 0 else swap_halves(sums))[:, :64]
        lines = (dead if level == 0 else swap_halves(dead))[:, :64]
        sum_o[level] = CODE_DECAY * ema_sum[level] + (1.0 - CODE_DECAY) * mine
        for r in range(8):
            sum_o[level, pl.ds(dead_codes[level, r], 1), :] = lines[r : r + 1]
        for b in range(4):
            at = ROW_COUNT + level * 4 + b
            used = total[at : at + 1, :]
            count = CODE_DECAY * ema_count[level : level + 1, b * 128 : b * 128 + 128] + (
                1.0 - CODE_DECAY
            ) * used
            ids = lane_iota((1, 128)) + b * 128
            for r in range(8):
                count = jnp.where(ids == dead_codes[level, r], 1.0, count)
            count_o[level : level + 1, b * 128 : b * 128 + 128] = count
            col = jnp.sum(jnp.where(same, count, 0.0), axis=1, keepdims=True)
            book_o[level, b * 128 : b * 128 + 128, :] = (
                sum_o[level, b * 128 : b * 128 + 128, :] / col
            )


def update(dead_codes, valid_rows, total, weights, firsts, seconds, ema_count, ema_sum):
    sds = jax.ShapeDtypeStruct
    shapes = [sds((1,), F32), sds((2,), F32)]
    for _ in range(3):
        shapes += [sds(w.shape, F32) for w in weights]
    shapes += [sds(w.shape, BF16) for w in weights]
    shapes += [sds(ema_sum.shape, F32), sds(ema_count.shape, F32), sds(ema_sum.shape, F32)]
    vm = pl.BlockSpec(memory_space=pltpu.VMEM)
    sm = pl.BlockSpec(memory_space=pltpu.SMEM)
    return pl.pallas_call(
        update_kernel,
        out_shape=shapes,
        in_specs=[sm] + [vm] * 22,
        out_specs=[sm, sm] + [vm] * 27,
        compiler_params=pltpu.CompilerParams(vmem_limit_bytes=VMEM_LIMIT),
        name="step_update",
    )(dead_codes, valid_rows, total, *weights, *firsts, *seconds, ema_count, ema_sum)


def body(sections, devices, *args):
    pixels, codes_top, codes_bottom, valid_rows, dead_codes, dead_source = args[:6]
    weights, firsts, seconds = args[6:12], args[12:18], args[18:24]
    codebook, ema_count, ema_sum = args[24:27]
    batches, part_rows, lanes = pixels.shape
    height = lanes // 3
    parts = height // part_rows
    share = batches // (sections * parts)
    section = lax.axis_index("section")
    device = lax.axis_index("dp")
    part = device % parts
    image = device // parts

    def regroup(x):
        pieces = []
        for k in range(parts):
            target = (part + k) % parts
            piece = lax.dynamic_slice_in_dim(x, (section * parts + target) * share, share, 0)
            if k > 0:
                pairs = [
                    (base + p, base + (p + k) % parts)
                    for base in range(0, devices, parts)
                    for p in range(parts)
                ]
                piece = lax.ppermute(piece, "dp", pairs)
            pieces.append(piece)
        ordered = [lax.select_n((part - p) % parts, *pieces) if parts == 2 else None for p in range(parts)]
        return jnp.stack(ordered, axis=1).reshape(share, parts * x.shape[1], x.shape[2])

    def code_layouts(codes, level):
        side = codes.shape[1]
        if level == 0:
            x = codes.reshape(share, side, side // 2, 2)
            col = x.transpose(0, 2, 1, 3).reshape(share, side * side // 2, 2)
            row = x.transpose(0, 3, 2, 1).reshape(share, 2, side * side // 2)
        else:
            x = codes.reshape(share, side // 2, 2, side // 2, 2)
            col = x.transpose(0, 3, 2, 1, 4).reshape(share, side * side // 2, 2)
            row = x.transpose(0, 4, 3, 2, 1).reshape(share, 2, side * side // 2)
        return col, row

    ct = code_layouts(regroup(codes_top), 0)
    cb = code_layouts(regroup(codes_bottom), 1)
    pix = regroup(pixels)
    place = jnp.stack([(section * parts + part) * share, image]).astype(jnp.int32)
    multiple = 8 * sections * devices
    total_rows = -(-ROW_END // multiple) * multiple
    packed = compute(place, valid_rows, dead_source, pix, ct, cb, weights, codebook, total_rows)
    total = lax.psum(packed, ("section", "dp"))
    outs = update(dead_codes, valid_rows, total, weights, firsts, seconds, ema_count, ema_sum)
    return (outs[0].reshape(()),) + tuple(outs[1:])


def solution(mesh):
    return jax.shard_map(
        functools.partial(body, mesh.shape["section"], mesh.shape["dp"]),
        mesh=mesh,
        in_specs=(P(None, "dp", None),) * 3 + (P(),) * 24,
        out_specs=(P(),) * 29,
        check_vma=False,
    )
```

time: 2530 us -> 283 us (0.11)
  waiting for transfers between devices: 994 us -> 127 us
  local copies, waits for them, and re-layouts: 608 us -> 40.6 us
  starting transfers between devices: 441 us -> 5.07 us
  matrix products: 186 us -> 0 us
  other arithmetic: 179 us -> 3.22 us
  Pallas kernels: 0 us -> 92.9 us
  blocking collectives: 48.9 us -> 0 us
    ppermute x128 -> x3, waiting for transfers between devices: 929 us -> 0.01 us  [regroup(): piece = lax.ppermute(piece, 'dp', pairs)]
    ppermute x128 -> x3, starting transfers between devices: 441 us -> 5.03 us  [regroup(): piece = lax.ppermute(piece, 'dp', pairs)]
    another operation x272 -> x5, local copies, waits for them, and re-layouts: 318 us -> 3.3 us  [the longest x1 2.15 us: code_layouts(): x = codes.reshape(share, side // 2, 2, side // 2, 2)]
    dot_general x137 -> x0, matrix products: 186 us -> none  [the longest x72 99.6 us: matmul(): return jnp.dot(x, w, preferred_element_type=jnp.float32)]
    transpose x89 -> x4, local copies, waits for them, and re-layouts: 120 us -> 4.99 us  [the longest x1 2.51 us: code_layouts(): col = x.transpose(0, 3, 2, 1, 4).reshape(share, side * side // 2, 2)]
    pallas_call x0 -> x2, Pallas kernels: none -> 92.9 us  [the longest x1 80.8 us: compute(): pl.pallas_call(compute_kernel, grid=(share,), out_shape=jax.ShapeDtypeStr...]
    concatenate x48 -> x0, other arithmetic: 64.5 us -> none  [with_halo(): block = jnp.concatenate([low, block, high], axis=dim)]
    psum x1, waiting for transfers between devices: 65.2 us -> 126 us  [body(): total = lax.psum(packed, ('section', 'dp'))]
  transfers between devices with their start and end apart: 129 -> 4, of which waited for: 6 -> 1; matrix products, arithmetic and copies ran while one was open for 36% -> 9% of each run, Pallas kernels for 0% -> 0%
where the time goes in v1:
time: 283 us
  waiting for transfers between devices  127 us (45%)
  Pallas kernels  92.9 us (33%)
  local copies, waits for them, and re-layouts  40.6 us (14%)
  between operations  14.2 us (5%)
  starting transfers between devices  5.07 us (2%)
  other arithmetic  3.22 us (1%)
    psum x1, waiting for transfers between devices, body(): total = lax.psum(packed, ('section', 'dp'))  126 us
    pallas_call x1, Pallas kernels, compute(): pl.pallas_call(compute_kernel, grid=(share,), out_shape=jax.ShapeDtypeStr...  80.8 us
    unnamed x38, local copies, waits for them, and re-layouts  28.3 us
    pallas_call x1, Pallas kernels, update(): pl.pallas_call(update_kernel, out_shape=shapes, in_specs=[sm] + [vm] * 22...  12.1 us
  transfers between devices with their start and end apart: 4, of which 1 were waited for; matrix products, arithmetic and copies ran while one was open for 9% of the time, Pallas kernels for 0%

profile of v1, /device:TPU:0, one launch (start us, length us, event | category | flops | bytes accessed | tf_op | source)
XLA Modules:
  0.0 282.5 jit_solution(16444144543256302371)
XLA Ops:
  7.2 0.0 copy-start.3
  7.2 0.0 all-reduce.2.cloned.1.call-start
  7.3 0.8 constant_dynamic-slice_fusion.1
  8.1 2.9 %collective-permute-start.1 = (s32[2,16,32]{2,1,0:T(8,128)S(1)}, s32[2,16,32]{2,1,0:T(8,128)S(1)}, u32[]{:S(2)}, u32[]{:S(2)}) collective-permute-start(s32[2,16,32]{2,1,0:T(8,128)S(1)} %constant_dynamic-slice_fusion.1), channel_id=1, source_target_pairs={{0,1},{1,0},{2,3},{3,2},{4,5},{5,4},{6,7},{7,6},{8,9},{9,8},{10,11... | collective-permute-start | bytes 12296 | tf_op jit(solution)/shard_map/ppermute | solution.py:829
  11.0 0.8 constant_dynamic-slice_fusion
  11.8 0.0 collective-permute-start.2
  11.8 1.0 constant_dynamic-slice_fusion.2
  12.8 2.1 collective-permute-start
  14.9 0.6 pad_add_fusion.2.place
  15.5 1.6 copy.87.w_to.refs_3_
  17.1 1.9 copy.88.book
  19.0 0.0 copy-done.3
  19.0 1.8 copy.86.w_conv.refs_0_
  20.8 0.0 collective-permute-done.1
  20.8 0.7 select_bitcast_fusion.5
  21.5 0.1 copy.80
  21.6 0.1 reshape_reshape.6
  21.8 0.7 reshape.79.ct_row
  22.5 1.1 copy.81
  23.5 0.0 collective-permute-done.2
  23.5 0.8 select_bitcast_fusion.3
  24.3 2.1 reshape_reshape.7
  26.5 1.4 copy.85
  27.9 0.8 reshape.80.cb_row
  28.7 2.5 copy.83
  31.2 0.0 collective-permute-done
  31.2 1.1 select_bitcast_fusion.1
  32.2 0.1 pad_maximum_fusion
  32.3 0.9 copy.79
  33.2 80.8 %step_compute.1 = f32[3584,128]{1,0:T(8,128)} custom-call(s32[2]{0:T(128)} %pad_add_fusion.2.place, s32[8,8]{1,0:T(8,128)} %valid_v.3, s32[2,8]{1,0:T(2,128)} %dead_source.1, s32[8,8]{1,0:T(8,128)} %valid_v.3, bf16[2,256,768]{2,1,0:T(8,128)(2,1)} %bitcast.31, s32[2,512,2]{2,1,0:T(8,128)} %bitcast.32, s32[2,2048,2]{2,1,0:T(8,128)} %bitcast.30, ...), custom_call_target="tpu_custom_call" | custom-call | tf_op jit(solution)/shard_map/step_compute/pallas_call | solution.py:696
  114.1 0.0 copy-start.9
  114.1 0.0 copy-start.7
  114.1 0.0 copy-start.4
  114.1 0.0 all-reduce.2.cloned.1.call-update
  114.1 0.8 copy-done.8
  114.9 0.8 copy.92.refs_9_
  115.6 0.0 copy-done.9
  115.7 0.0 copy-start.5
  115.7 0.8 copy.94.refs_15_
  116.4 0.0 copy-done.7
  116.4 1.0 copy.95.refs_19_
  117.4 0.0 copy-done.4
  117.4 1.8 copy.91.refs_6_
  119.2 0.0 copy-done.5
  119.2 1.8 copy.93.refs_12_
  121.0 126.5 %all-reduce.2.cloned.1.call-done.total = f32[3584,128]{1,0:T(8,128)} async-done(((f32[3584,128]{1,0:T(8,128)}), f32[3584,128]{1,0:T(8,128)}) %all-reduce.2.cloned.1.call-update) | async-done | bytes 1835024 | tf_op jit(solution)/shard_map/psum | solution.py:853
  247.5 12.1 %step_update.1 = (f32[1]{0:T(128)}, f32[2]{0:T(128)}, f32[3,1152,64]{2,1,0:T(8,128)}, f32[3,64,128]{2,1,0:T(8,128)}, f32[5,64,128]{2,1,0:T(8,128)}, /*index=5*/f...) custom-call(s32[2,8]{1,0:T(2,128)} %dead_codes.1, ...), custom_call_target="tpu_custom_call" | custom-call | tf_op jit(solution)/shard_map/step_update/pallas_call | solution.py:795
  259.6 0.0 copy-start.6
  259.6 1.6 copy.103
  261.2 0.0 copy-start.2
  261.2 1.7 copy.97
  262.9 1.6 copy.99
  264.6 1.6 copy.101
  266.2 1.9 copy.104
  268.1 0.0 copy-done.6
  268.1 0.9 copy.105
  269.0 0.0 copy-start.1
  269.0 2.3 copy.102
  271.3 0.0 copy-done.2
  271.4 1.4 copy.96
  272.8 0.0 copy-done.1
  272.8 1.4 copy.98
  274.2 0.0 copy-done
  274.3 1.4 copy.100
  (6 shorter events, 0.0 us)
Async XLA Ops:
  7.2 11.8 %copy-start.3 = (f32[3,1152,64]{1,2,0:T(8,128)S(1)}, f32[3,1152,64]{1,2,0:T(8,128)}, u32[]{:S(2)}) copy-start(f32[3,1152,64]{1,2,0:T(8,128)} %param.33) | copy-start | bytes 2654212
  7.2 240.3 %all-reduce.2.cloned.1.call-start = ((), (), s32[]{:S(2)}) async-start(), calls=%async_computation | async-start | bytes 3670016 | tf_op jit(solution)/shard_map/psum | solution.py:853
  8.1 12.7 %collective-permute-start.1 = (s32[2,16,32]{2,1,0:T(8,128)S(1)}, s32[2,16,32]{2,1,0:T(8,128)S(1)}, u32[]{:S(2)}, u32[]{:S(2)}) collective-permute-start(s32[2,16,32]{2,1,0:T(8,128)S(1)} %constant_dynamic-slice_fusion.1), channel_id=1, source_target_pairs={{0,1},{1,0},{2,3},{3,2},{4,5},{5,4},{6,7},{7,6},{8,9},{9,8},{10,11... | collective-permute-start | bytes 12296 | tf_op jit(solution)/shard_map/ppermute | solution.py:829
  11.8 11.7 %collective-permute-start.2 = (s32[2,32,64]{2,1,0:T(8,128)S(1)}, s32[2,32,64]{2,1,0:T(8,128)S(1)}, u32[]{:S(2)}, u32[]{:S(2)}) collective-permute-start(s32[2,32,64]{2,1,0:T(8,128)S(1)} %constant_dynamic-slice_fusion), channel_id=1, source_target_pairs={{0,1},{1,0},{2,3},{3,2},{4,5},{5,4},{6,7},{7,6},{8,9},{9,8},{10,11... | collective-permute-start | bytes 49160 | tf_op jit(solution)/shard_map/ppermute | solution.py:829
  12.8 18.4 %collective-permute-start = (bf16[2,128,768]{2,1,0:T(8,128)(2,1)S(1)}, bf16[2,128,768]{2,1,0:T(8,128)(2,1)S(1)}, u32[]{:S(2)}, u32[]{:S(2)}) collective-permute-start(bf16[2,128,768]{2,1,0:T(8,128)(2,1)S(1)} %constant_dynamic-slice_fusion.2), channel_id=1, source_target_pairs={{0,1},{1,0},{2,3},{3,2},{4,5},{5,4},{6,7},{7,6},{8,9},{9,8},{10,11... | collective-permute-start | bytes 1179656 | tf_op jit(solution)/shard_map/ppermute | solution.py:829
  114.1 0.8 copy-start.8
  114.1 1.6 copy-start.9
  114.1 2.3 copy-start.7
  114.1 3.3 %copy-start.4 = (f32[3,1152,64]{1,2,0:T(8,128)S(1)}, f32[3,1152,64]{1,2,0:T(8,128)}, u32[]{:S(2)}) copy-start(f32[3,1152,64]{1,2,0:T(8,128)} %param.39) | copy-start | bytes 2654212
  115.7 3.6 %copy-start.5 = (f32[3,1152,64]{1,2,0:T(8,128)S(1)}, f32[3,1152,64]{1,2,0:T(8,128)}, u32[]{:S(2)}) copy-start(f32[3,1152,64]{1,2,0:T(8,128)} %param.45) | copy-start | bytes 2654212
  259.6 8.5 %copy-start.6 = (f32[2,512,64]{2,1,0:T(8,128)S(1)}, f32[2,512,64]{2,1,0:T(8,128)}, u32[]{:S(2)}) copy-start(f32[2,512,64]{2,1,0:T(8,128)} %get-tuple-element.144) | copy-start | bytes 786436
  261.2 10.2 %copy-start.2 = (f32[3,1152,64]{2,1,0:T(8,128)S(1)}, f32[3,1152,64]{2,1,0:T(8,128)}, u32[]{:S(2)}) copy-start(f32[3,1152,64]{2,1,0:T(8,128)} %get-tuple-element.118) | copy-start | bytes 2654212
  269.0 3.8 %copy-start.1 = (f32[3,1152,64]{2,1,0:T(8,128)S(1)}, f32[3,1152,64]{2,1,0:T(8,128)}, u32[]{:S(2)}) copy-start(f32[3,1152,64]{2,1,0:T(8,128)} %get-tuple-element.124) | copy-start | bytes 2654212
  272.8 1.5 copy-start
Sparse Core Ops, SparseCore 0:
  114.2 133.2 all-reduce.1

commit v2 on v1

--- a/solution.py
+++ b/solution.py
@@ -22,10 +22,12 @@
 VMEM_LIMIT = 56 * 1024 * 1024
 CHUNK = 8
 
-CONV_ROWS = 640
+TAP_ROWS = 64
+CONV_ROWS = 9 * TAP_ROWS
 ROW_RES = 3 * CONV_ROWS
 ROW_FROM = ROW_RES + 3 * 64
-ROW_PIXEL = ROW_FROM + 5 * 64
+ROW_TO = ROW_FROM + 5 * 64
+ROW_PIXEL = ROW_TO + 2 * 64
 ROW_DOWN = ROW_PIXEL + 2 * 48
 ROW_SUMS = ROW_DOWN + 512
 ROW_COUNT = ROW_SUMS + 512
@@ -92,10 +94,11 @@
     dead_source,
     valid_v,
     pix,
-    ct_col,
-    cb_col,
-    ct_row,
-    cb_row,
+    pix_far,
+    ct_near,
+    ct_far,
+    cb_near,
+    cb_far,
     w_conv,
     w_res,
     w_from,
@@ -115,6 +118,8 @@
     book_a,
     book_b,
     sel,
+    hot_t,
+    hot_b,
     patches,
     stem,
     up,
@@ -160,7 +165,8 @@
     pairs_t = xs_top.shape[0]
     ch = CHUNK
     ch_t = CHUNK // 2
-    valid_count = 3.0 * pix.shape[1] * jnp.sum(valid_v[...].astype(F32))
+    height = 2 * pix.shape[1]
+    valid_count = 3.0 * height * jnp.sum(valid_v[...].astype(F32))
     loss_slope = 2.0 / valid_count
     commit_slope = loss_slope * COMMIT_WEIGHT
 
@@ -170,6 +176,12 @@
             return 0
 
         lax.fori_loop(0, total // size, run, 0)
+
+    def picker(src, start):
+        size = src.shape[0]
+        at = lax.broadcasted_iota(jnp.int32, src.shape, 1) + start
+        at = jnp.where(at >= size, at - size, at)
+        return (at == src).astype(F32).astype(BF16)
 
     @pl.when(step == 0)
     def _():
@@ -178,16 +190,15 @@
         wide[...] = jnp.zeros(wide.shape, F32)
         d_two[...] = jnp.zeros(d_two.shape, F32)
         d_two_t[...] = jnp.zeros(d_two_t.shape, F32)
-        zero = jnp.zeros((128, 64), F32)
+        zero = jnp.zeros((64, 128), F32)
         for k in range(3):
             for i in range(3):
-                t = [w_conv[k, pl.ds((i * 3 + j) * 128, 128), :] for j in range(3)]
-                even = jnp.concatenate([t[1], t[0], zero, t[2]], axis=1).astype(BF16)
-                odd = jnp.concatenate([t[2], t[1], t[0], zero], axis=1).astype(BF16)
-                b_fwd[k, pl.ds(i * 256, 128), :] = even
-                b_fwd[k, pl.ds(i * 256 + 128, 128), :] = odd
-                b_bwd[k, pl.ds(0, 128), pl.ds((2 - i) * 256, 256)] = even
-                b_bwd[k, pl.ds(128, 128), pl.ds((2 - i) * 256, 256)] = odd
+                t = [w_conv[k, :, pl.ds((i * 3 + j) * 128, 128)] for j in range(3)]
+                even = jnp.concatenate([t[1], t[0], zero, t[2]], axis=0).astype(BF16)
+                odd = jnp.concatenate([t[2], t[1], t[0], zero], axis=0).astype(BF16)
+                both = jnp.concatenate([even, odd], axis=1)
+                b_fwd[k, :, pl.ds(i * 256, 256)] = both
+                b_bwd[k, pl.ds((2 - i) * 256, 256), :] = both
             wo_d[k] = pair_diag(w_res[k]).astype(BF16)
         from_d[...] = pair_diag(w_from[0]).astype(BF16)
         for k in range(2):
@@ -210,30 +221,51 @@
             mid = (full - hi).astype(BF16).astype(F32)
             lo = full - hi - mid
             empty = jnp.zeros_like(full)
-            book_a[k] = jnp.concatenate([hi, mid, lo, empty], axis=1).astype(BF16)
-            book_b[k] = jnp.concatenate([mid, hi, empty, lo], axis=1).astype(BF16)
-        height = pix.shape[1]
+            book_a[k] = jnp.concatenate([hi, mid, lo, empty], axis=0).astype(BF16)
+            book_b[k] = jnp.concatenate([mid, hi, empty, lo], axis=0).astype(BF16)
         o = lax.broadcasted_iota(jnp.int32, (height, height), 0)
-        s = lax.broadcasted_iota(jnp.int32, (height, height), 1)
         quarter = height // 4
         src = 8 * (o % rows) + 4 * ((o % quarter) // rows) + o // quarter
-        sel[...] = (s == src).astype(F32).astype(BF16)
-
-    def near_of(col, level):
-        n = col.shape[0]
-        codes = lax.broadcasted_iota(jnp.int32, (n, book.shape[1]), 1)
+        sel[...] = picker(src, place[2] * (height // 2))
+
+    def codes_of(near_ref, far_ref, split):
+        both = jnp.concatenate([near_ref[0], far_ref[0]], axis=0).astype(F32)
+        size = both.shape[0]
+        o = lax.broadcasted_iota(jnp.int32, (size, size), 0)
+        src = 2 * (o % rows) + o // rows if split else o
+        pick = picker(src, place[2] * (size // 2))
+        high = jnp.floor(both * (1.0 / 256.0))
+        low = both - 256.0 * high
+        codes = 256.0 * mm(pick, high.astype(BF16)) + mm(pick, low.astype(BF16))
+        pad = jnp.zeros((size, 128 - size), F32)
+        return jnp.concatenate([codes, pad], axis=1)
+
+    codes_t = codes_of(ct_near, ct_far, False)
+    codes_b = codes_of(cb_near, cb_far, True)
+
+    def near_of(codes, level, c0, n, hot_ref):
+        size = codes.shape[0]
+        here = pl.ds(pl.multiple_of(c0 * size, size), n * size)
+        moved = pltpu.roll(codes, lax.rem(128 - 2 * c0, 128), 1)
+        ids = lax.broadcasted_iota(jnp.int32, (size, 512), 1).astype(F32)
         v = []
+        used = jnp.zeros((8, 512), F32)
         for cp, table in ((0, book_a), (1, book_b)):
-            hot = (col[:, cp : cp + 1] == codes).astype(F32).astype(BF16)
-            v.append(mm(hot, table[level]))
-        half = low_half((n, 128))
+            for j in range(n):
+                hot = (moved[:, 2 * j + cp : 2 * j + cp + 1] == ids).astype(F32)
+                used = used + jnp.sum(hot.reshape(size // 8, 8, 512), axis=0)
+                at = pl.ds(pl.multiple_of((c0 + j) * size, size), size)
+                hot_ref[at, pl.ds(cp * 512, 512)] = hot.astype(BF16)
+            v.append(mm_t(hot_ref[here, pl.ds(cp * 512, 512)], table[level]))
+        acc_count[level] += used
+        half = low_half((n * size, 128))
         hi = jnp.where(half, v[0][:, :128], v[1][:, :128])
         mid = swap_halves(jnp.where(half, v[1][:, :128], v[0][:, :128]))
         lo = jnp.where(half, v[0][:, 128:], v[1][:, 128:])
         return hi, hi + mid + lo
 
     def top_codes(c0):
-        hi, full = near_of(ct_col[0, pl.ds(c0 * rows, ch_t * rows), :], 0)
+        hi, full = near_of(codes_t, 0, c0, ch_t, hot_t)
         near_t[pl.ds(c0 * rows, ch_t * rows), :] = full
         u = mm(hi.astype(BF16), up_d[...]).reshape(ch_t, rows, 1024)
         for cq in range(2):
@@ -252,7 +284,7 @@
 
     def bottom_codes(c0):
         n = ch * 2 * rows
-        hi, full = near_of(cb_col[0, pl.ds(c0 * 2 * rows, n), :], 1)
+        hi, full = near_of(codes_b, 1, c0, ch, hot_b)
         near[pl.ds(c0 * 2 * rows, n), :] = full
         x = mm(hi.astype(BF16), from_d[...]).reshape(ch, 2, rows, 256) + up[pl.ds(c0, ch)]
         res[pl.ds(c0, ch)] = x
@@ -266,7 +298,7 @@
                 taps = jnp.concatenate(
                     [flat(xs[pl.ds(c0, ch), rp + t]) for t in range(3)], axis=1
                 )
-                y = mm(taps, b_fwd[k])
+                y = mm_t(taps, b_fwd[k])
                 wide[pl.ds(c0 + 1, ch), rp] = y.reshape(ch, rows, 256)
 
         loop(pairs, ch, run)
@@ -292,8 +324,7 @@
     loop(pairs, ch, decode_out)
 
     per_tile = 2 * rows
-    picked = mm(sel[...], pix[0])
-    wide_px = pix.shape[2]
+    picked = mm(sel[...], jnp.concatenate([pix[0], pix_far[0]], axis=0))
     lanes24 = lane_iota((per_tile, 128))
     for c2 in range(pairs):
         tile = jnp.zeros((per_tile, 128), F32)
@@ -338,12 +369,22 @@
 
     def top_conv(c0):
         taps = jnp.concatenate([flat(xs_top[pl.ds(c0, ch_t), t]) for t in range(3)], axis=1)
-        wide[pl.ds(c0 + 1, ch_t), 0] = mm(taps, b_fwd[0]).reshape(ch_t, rows, 256)
+        wide[pl.ds(c0 + 1, ch_t), 0] = mm_t(taps, b_fwd[0]).reshape(ch_t, rows, 256)
 
     loop(pairs_t, ch_t, top_conv)
 
     def add_num(x):
         acc_num[...] += jnp.sum(x.reshape(x.shape[0] // 8, 8, 128), axis=0)
+
+    def add_sums(level, latent, hot_ref, here):
+        hi = latent.astype(BF16).astype(F32)
+        lo = latent - hi
+        half = low_half(hi.shape)
+        even = jnp.where(half, hi, swap_halves(lo)).astype(BF16)
+        odd = jnp.where(half, swap_halves(hi), lo).astype(BF16)
+        acc_sums[level] += mm_w(even, hot_ref[here, pl.ds(0, 512)]) + mm_w(
+            odd, hot_ref[here, pl.ds(512, 512)]
+        )
 
     def top_out(c0):
         n = ch_t * rows
@@ -354,8 +395,9 @@
         y = flat(grad_hi[pl.ds(c0, ch_t), 0]) + mm(hidden, wo_d[0])
         low = y.astype(BF16)
         low_top[here, :] = low
-        latent = mm(low, to_d[0])
+        latent = mm_t(low, to_d[0])
         lat_t[here, :] = latent
+        add_sums(0, latent, hot_t, here)
         diff = latent - near_t[here, :]
         add_num(COMMIT_WEIGHT * diff * diff)
 
@@ -378,35 +420,13 @@
         y = res[pl.ds(c0, ch)].reshape(n, 256) + mm(hidden, wo_d[1])
         low = y.astype(BF16)
         low_bot[here, :] = low
-        latent = mm(low, to_d[1])
+        latent = mm_t(low, to_d[1])
         lat[here, :] = latent
+        add_sums(1, latent, hot_b, here)
         diff = latent - near[here, :]
         add_num(COMMIT_WEIGHT * diff * diff)
 
     loop(pairs, ch, bottom_out)
-
-    def level_stats(level, lat_ref, row_ref, total):
-        size = 256
-
-        def run(p0):
-            latent = lat_ref[pl.ds(p0, size), :]
-            hi = latent.astype(BF16)
-            lo = (latent - hi.astype(F32)).astype(BF16)
-            both = jnp.concatenate([hi, lo], axis=1)
-            codes = lax.broadcasted_iota(jnp.int32, (book.shape[1], size), 0)
-            half = low_half((book.shape[1], 128))
-            parts = []
-            for cp in range(2):
-                hot = (row_ref[0, cp : cp + 1, pl.ds(p0, size)] == codes).astype(F32)
-                acc_count[level] += hot[:, :128] + hot[:, 128:]
-                s = mm(hot.astype(BF16), both)
-                parts.append(s[:, :128] + s[:, 128:])
-            acc_sums[level] += jnp.where(half, parts[0], parts[1])
-
-        loop(total, size, run)
-
-    level_stats(0, lat_t, ct_row, pairs_t * rows)
-    level_stats(1, lat, cb_row, pairs * 2 * rows)
 
     micro = place[0] + step
     image = place[1]
@@ -473,7 +493,7 @@
             taps = jnp.concatenate(
                 [flat(d_slots[pl.ds(c0, ch), rp + t]) for t in range(3)], axis=1
             )
-            outs.append(mm_t(taps, b_bwd[k]).reshape(ch, rows, 256))
+            outs.append(mm(taps, b_bwd[k]).reshape(ch, rows, 256))
             part = mm_w(flat(xs[pl.ds(c0, ch), rp + 1]), taps)
             total = part if total is None else total + part
         acc_conv[k] += total
@@ -491,8 +511,8 @@
         acc_from[...] += mm_w(full.astype(BF16), g_low)
         g_lat = mm_t(g_low, from_d[...]) + commit_slope * (lat[here, :] - full)
         g_lat = g_lat.astype(BF16)
-        acc_to[1] += mm_w(low_bot[here, :], g_lat)
-        grad_hi[pl.ds(c0, ch)] = mm_t(g_lat, to_d[1]).reshape(ch, 2, rows, 256)
+        acc_to[1] += mm_w(g_lat, low_bot[here, :])
+        grad_hi[pl.ds(c0, ch)] = mm(g_lat, to_d[1]).reshape(ch, 2, rows, 256)
 
     loop(pairs, ch, decode_in_back)
 
@@ -520,8 +540,8 @@
         acc_up[...] += mm_w(full.astype(BF16), wide_g)
         g_q = mm_t(wide_g, up_d[...]).astype(BF16).astype(F32)
         g_lat = (g_q + commit_slope * (lat_t[here, :] - full)).astype(BF16)
-        acc_to[0] += mm_w(low_top[here, :], g_lat)
-        g_top = mm_t(g_lat, to_d[0])
+        acc_to[0] += mm_w(g_lat, low_top[here, :])
+        g_top = mm(g_lat, to_d[0])
         grad_lo[here, :] = g_top
         g_low = g_top.astype(BF16)
         a = act_top[here, :]
@@ -547,7 +567,7 @@
             axis=1,
         )
         acc_conv[0] += mm_w(flat(xs_top[pl.ds(c0, ch_t), 1]), taps)
-        g = grad_lo[pl.ds(c0 * rows, n), :] + mm_t(taps, b_bwd[0])
+        g = grad_lo[pl.ds(c0 * rows, n), :] + mm(taps, b_bwd[0])
         g_low = g.astype(BF16).reshape(ch_t, rows, 256)
         for cq in range(2):
             g_cq = flat(g_low[:, :, cq * 128 : cq * 128 + 128])
@@ -570,27 +590,18 @@
 
     @pl.when(step == last)
     def _():
-        half = low_half((128, 128))
-        zero = jnp.zeros((128, 128), F32)
-
-        def to_sum(k):
-            return acc_to[k, :128, :] + swap_halves(acc_to[k, 128:, :])
-
         for k in range(3):
-            twos = []
             for i in range(3):
                 lanes = (2 - i) * 256
-                e0 = acc_conv[k, :128, lanes : lanes + 128]
-                e1 = acc_conv[k, :128, lanes + 128 : lanes + 256]
-                o0 = acc_conv[k, 128:, lanes : lanes + 128]
-                o1 = acc_conv[k, 128:, lanes + 128 : lanes + 256]
-                first = e0 + swap_halves(jnp.where(half, o1, o0))
-                out[k * CONV_ROWS + i * 128 : k * CONV_ROWS + i * 128 + 128, :] = first
-                twos.append(o0 + swap_halves(e1))
-            base = k * CONV_ROWS + 384
-            out[base : base + 128, :] = jnp.where(half, twos[0], swap_halves(twos[1]))
-            other = swap_halves(to_sum(k)) if k < 2 else zero
-            out[base + 128 : base + 256, :] = jnp.where(half, twos[2], other)
+                t = jnp.transpose(acc_conv[k, :, lanes : lanes + 256])
+                taps = (
+                    t[64:128, :128] + t[128:192, 128:],
+                    t[:64, :128] + t[64:128, 128:],
+                    t[:64, 128:] + t[192:, :128],
+                )
+                for j in range(3):
+                    at = k * CONV_ROWS + (i * 3 + j) * TAP_ROWS
+                    out[at : at + 64, :] = taps[j]
             out[ROW_RES + k * 64 : ROW_RES + k * 64 + 64, :] = (
                 acc_res[k, :64, :128] + acc_res[k, 64:, 128:]
             )
@@ -600,22 +611,22 @@
                 acc_up[:64, k * 128 : k * 128 + 128] + acc_up[64:, 512 + k * 128 : 640 + k * 128]
             )
         for k in range(2):
+            at = ROW_TO + k * 64
+            out[at : at + 64, :] = acc_to[k, :64, :128] + acc_to[k, 64:, 128:]
             for i in range(4):
                 even = acc_pix[k, 24 * i : 24 * i + 12, :128]
                 odd = acc_pix[k, 24 * i + 12 : 24 * i + 24, 128:]
                 at = ROW_PIXEL + k * 48 + i * 12
                 out[at : at + 12, :] = even + odd
         out[ROW_DOWN : ROW_DOWN + 512, :] = acc_down[...]
-        top = acc_sums[0] + swap_halves(acc_sums[0])
-        bottom = acc_sums[1] + swap_halves(acc_sums[1])
-        out[ROW_SUMS : ROW_SUMS + 512, :] = jnp.where(low_half(top.shape), top, bottom)
-        same = lax.broadcasted_iota(jnp.int32, (128, 128), 0) == lane_iota((128, 128))
         for level in range(2):
+            sums = acc_sums[level, :64, :] + acc_sums[level, 64:, :]
+            used = jnp.sum(acc_count[level], axis=0, keepdims=True)
             for b in range(4):
-                col = jnp.sum(acc_count[level, b * 128 : b * 128 + 128, :], axis=1, keepdims=True)
-                line = jnp.sum(jnp.where(same, col, 0.0), axis=0, keepdims=True)
+                at = ROW_SUMS + (level * 4 + b) * 64
+                out[at : at + 64, :] = sums[:, b * 128 : b * 128 + 128]
                 at = ROW_COUNT + level * 4 + b
-                out[at : at + 1, :] = line
+                out[at : at + 1, :] = used[:, b * 128 : b * 128 + 128]
         out[ROW_DEAD : ROW_DEAD + 8, :] = acc_dead[...]
         out[ROW_NUMER : ROW_NUMER + 8, :] = acc_num[...]
         if out.shape[0] > ROW_END:
@@ -623,37 +634,40 @@
 
 
 def compute(place, valid_rows, dead_source, pix, ct, cb, weights, book, total_rows):
-    share, height, _ = pix.shape
+    share, part_rows, _ = pix[1].shape
+    height = 2 * part_rows
     pairs = height // 8
     rows = height // 8
     pairs_t = pairs // 2
     n = pairs * 2 * rows
     n_t = pairs_t * rows
-    ct_col, ct_row = ct
-    cb_col, cb_row = cb
     smem = pl.BlockSpec(memory_space=pltpu.SMEM)
 
     def whole(x):
         zeros = (0,) * len(x.shape)
-        return pl.BlockSpec(x.shape, lambda i: zeros)
-
-    def each(x):
-        zeros = (0,) * (len(x.shape) - 1)
-        return pl.BlockSpec((1,) + x.shape[1:], lambda i: (i,) + zeros)
+        return pl.BlockSpec(x.shape, lambda i, place: zeros)
+
+    def near(x):
+        return pl.BlockSpec((1,) + x.shape[1:], lambda i, place: (place[0] + i, 0, 0))
+
+    def far(x):
+        return pl.BlockSpec((1,) + x.shape[1:], lambda i, place: (i, 0, 0))
 
     v = pltpu.VMEM
     scratch = [
+        v((3, 256, 768), BF16),
         v((3, 768, 256), BF16),
-        v((3, 256, 768), BF16),
         v((3, 128, 256), BF16),
         v((128, 256), BF16),
-        v((2, 256, 128), BF16),
+        v((2, 128, 256), BF16),
         v((128, 1024), BF16),
         v((2, 128, 256), BF16),
         v((512, 128), BF16),
-        v((2, 512, 256), BF16),
-        v((2, 512, 256), BF16),
+        v((2, 256, 512), BF16),
+        v((2, 256, 512), BF16),
         v((height, height), BF16),
+        v((n_t, 1024), BF16),
+        v((n, 1024), BF16),
         v((n, 128), BF16),
         v((pairs, 2, rows, 256), BF16),
         v((pairs, 2, rows, 256), F32),
@@ -685,28 +699,159 @@
         v((3, 128, 256), F32),
         v((128, 256), F32),
         v((128, 1024), F32),
-        v((2, 256, 128), F32),
+        v((2, 128, 256), F32),
         v((2, 128, 256), F32),
         v((512, 128), F32),
-        v((2, 512, 128), F32),
-        v((2, 512, 128), F32),
+        v((2, 128, 512), F32),
+        v((2, 8, 512), F32),
         v((8, 128), F32),
         v((8, 128), F32),
     ]
     return pl.pallas_call(
         compute_kernel,
-        grid=(share,),
+        grid_spec=pltpu.PrefetchScalarGridSpec(
+            num_scalar_prefetch=1,
+            grid=(share,),
+            in_specs=[smem, smem, whole(valid_rows)]
+            + [spec(x) for pair in (pix, ct, cb) for spec, x in zip((near, far), pair)]
+            + [whole(w) for w in weights]
+            + [whole(book)],
+            out_specs=pl.BlockSpec((total_rows, 128), lambda i, place: (0, 0)),
+            scratch_shapes=scratch,
+        ),
         out_shape=jax.ShapeDtypeStruct((total_rows, 128), F32),
-        in_specs=[smem, smem, smem, whole(valid_rows), each(pix), each(ct_col), each(cb_col), each(ct_row), each(cb_row)]
-        + [whole(w) for w in weights]
-        + [whole(book)],
-        out_specs=pl.BlockSpec((total_rows, 128), lambda i: (0, 0)),
-        scratch_shapes=scratch,
         compiler_params=pltpu.CompilerParams(
             dimension_semantics=("arbitrary",), vmem_limit_bytes=VMEM_LIMIT
         ),
         name="step_compute",
-    )(place, valid_rows, dead_source, valid_rows, pix, ct_col, cb_col, ct_row, cb_row, *weights, book)
+    )(place, valid_rows, dead_source, valid_rows, *pix, *ct, *cb, *weights, book)
+
+
+MESH = pl.DeviceIdType.MESH
+Z_SIZE = 4
+
+
+def reduce_kernel(plane, x, out, one, two, sums, three, acc, s1, r1, s2, r2, s3, r3, a3s, a3r, a2s, a2r, a1s, a1r):
+    total = x.shape[0]
+    half, part = total // 2, total // 2 // plane
+    chunk = part // Z_SIZE
+    s = lax.axis_index("section")
+    d = lax.axis_index("dp")
+    z, q = d // plane, d % plane
+    peer = (1 - s, d)
+    mates = [lax.rem(q + k, plane) for k in range(plane)]
+    levels = [lax.rem(z + k, Z_SIZE) for k in range(Z_SIZE)]
+
+    def rows(ref, sec, q_at, z_at=None):
+        start = sec * half + q_at * part
+        size = part
+        if z_at is not None:
+            start = start + z_at * chunk
+            size = chunk
+        return ref.at[pl.ds(pl.multiple_of(start, 8), size)]
+
+    def piece(ref, index, size):
+        return ref.at[pl.ds(pl.multiple_of(index * size, 8), size)]
+
+    partners = [peer] + [(s, z * plane + m) for m in mates[1:]] + [(s, l * plane + q) for l in levels[1:]]
+    barrier = pltpu.get_barrier_semaphore()
+    for p in partners:
+        pl.semaphore_signal(barrier, inc=1, device_id=p, device_id_type=MESH)
+    pl.semaphore_wait(barrier, len(partners))
+
+    def send(src, dst, ssem, rsem, to):
+        c = pltpu.make_async_remote_copy(src, dst, ssem, rsem, device_id=to, device_id_type=MESH)
+        c.start()
+        return c
+
+    order = list(range(1, plane)) + [0]
+    first = {}
+    for k in order:
+        first[k] = send(rows(x, 1 - s, mates[k]), one.at[k], s1.at[k], r1.at[k], peer)
+    second = {}
+    for k in order:
+        first[k].wait_recv()
+        mine = rows(x, s, mates[k])[...] + one[k]
+        if k == 0:
+            acc[...] = mine
+        else:
+            sums[k - 1] = mine
+            second[k] = send(
+                sums.at[k - 1], two.at[k - 1], s2.at[k - 1], r2.at[k - 1], (s, z * plane + mates[k])
+            )
+    for k in range(1, plane):
+        second[k].wait_recv()
+    third = {}
+    for k in [1, 2, 3, 0]:
+        at = pl.ds(pl.multiple_of(levels[k] * chunk, 8), chunk)
+        value = acc[at, :]
+        for j in range(plane - 1):
+            value = value + two[j, at, :]
+        acc[at, :] = value
+        if k > 0:
+            third[k] = send(
+                acc.at[at], three.at[k - 1], s3.at[k - 1], r3.at[k - 1], (s, levels[k] * plane + q)
+            )
+    value = acc[pl.ds(pl.multiple_of(z * chunk, 8), chunk), :]
+    for k in range(1, Z_SIZE):
+        third[k].wait_recv()
+        value = value + three[k - 1]
+    own = rows(out, s, q, z)
+    own[...] = value
+    up = {}
+    for k in range(1, Z_SIZE):
+        up[k] = send(own, own, a3s.at[k - 1], a3r.at[k - 1], (s, levels[k] * plane + q))
+    across, over = {}, {}
+
+    def spread(k):
+        src = rows(out, s, q, lax.rem(z + Z_SIZE - k, Z_SIZE))
+        for j in range(1, plane):
+            at = (j - 1) * Z_SIZE + k
+            across[j, k] = send(src, src, a2s.at[at], a2r.at[at], (s, z * plane + mates[j]))
+        over[0, k] = send(src, src, a1s.at[k], a1r.at[k], peer)
+
+    spread(0)
+    for k in range(1, Z_SIZE):
+        up[k].wait_recv()
+        spread(k)
+    for k in range(Z_SIZE):
+        for j in range(1, plane):
+            across[j, k].wait_recv()
+            src = rows(out, s, lax.rem(q + plane - j, plane), lax.rem(z + Z_SIZE - k, Z_SIZE))
+            at = j * Z_SIZE + k
+            over[j, k] = send(src, src, a1s.at[at], a1r.at[at], peer)
+    for c in over.values():
+        c.wait_recv()
+    for group in (first, second, third, up, across, over):
+        for c in group.values():
+            c.wait_send()
+
+
+def all_sum(x, devices):
+    total = x.shape[0]
+    plane = devices // Z_SIZE
+    part = total // 2 // plane
+    chunk = part // Z_SIZE
+    dma = pltpu.SemaphoreType.DMA
+    v = pltpu.VMEM
+    vm = pl.BlockSpec(memory_space=pltpu.VMEM)
+    pairs = [plane, plane - 1, Z_SIZE - 1, Z_SIZE - 1, (plane - 1) * Z_SIZE, plane * Z_SIZE]
+    return pl.pallas_call(
+        functools.partial(reduce_kernel, plane),
+        out_shape=jax.ShapeDtypeStruct(x.shape, F32),
+        in_specs=[vm],
+        out_specs=vm,
+        scratch_shapes=[
+            v((plane, part, 128), F32),
+            v((plane - 1, part, 128), F32),
+            v((plane - 1, part, 128), F32),
+            v((Z_SIZE - 1, chunk, 128), F32),
+            v((part, 128), F32),
+        ]
+        + [dma((n,)) for n in pairs for _ in range(2)],
+        compiler_params=pltpu.CompilerParams(collective_id=0, has_side_effects=True, vmem_limit_bytes=VMEM_LIMIT),
+        name="step_reduce",
+    )(x)
 
 
 def update_kernel(dead_codes, valid_v, total, *refs):
@@ -738,49 +883,39 @@
         low_o[t][index] = fresh.astype(BF16)
 
     for k in range(3):
-        base = k * CONV_ROWS
-        for i in range(3):
-            both = total[base + i * 128 : base + i * 128 + 128, :]
-            apply(0, (k, pl.ds((i * 3 + 1) * 128, 128)), both[:, :64])
-            apply(0, (k, pl.ds(i * 3 * 128, 128)), swap_halves(both)[:, :64])
-        both = total[base + 384 : base + 512, :]
-        apply(0, (k, pl.ds(2 * 128, 128)), both[:, :64])
-        apply(0, (k, pl.ds(5 * 128, 128)), swap_halves(both)[:, :64])
-        both = total[base + 512 : base + 640, :]
-        apply(0, (k, pl.ds(8 * 128, 128)), both[:, :64])
-        if k < 2:
-            apply(3, (k,), swap_halves(both)[:, :64])
+        for t in range(9):
+            at = k * CONV_ROWS + t * TAP_ROWS
+            apply(0, (k, slice(None), pl.ds(t * 128, 128)), total[at : at + 64, :])
         apply(1, (k,), total[ROW_RES + k * 64 : ROW_RES + k * 64 + 64, :])
     for k in range(5):
         apply(2, (k,), total[ROW_FROM + k * 64 : ROW_FROM + k * 64 + 64, :])
     for k in range(2):
+        apply(3, (k,), total[ROW_TO + k * 64 : ROW_TO + k * 64 + 64, :])
         apply(4, (k,), total[ROW_PIXEL + k * 48 : ROW_PIXEL + k * 48 + 48, :])
     for k in range(4):
         apply(5, (k,), total[ROW_DOWN + k * 128 : ROW_DOWN + k * 128 + 128, :])
 
-    same = lax.broadcasted_iota(jnp.int32, (128, 128), 0) == lane_iota((128, 128))
-    sums = total[ROW_SUMS : ROW_SUMS + 512, :]
-    dead = total[ROW_DEAD : ROW_DEAD + 8, :]
+    dead = jnp.concatenate(
+        [total[ROW_DEAD : ROW_DEAD + 8, :], jnp.zeros((120, 128), F32)], axis=0
+    )
+    dead = jnp.transpose(dead)
     for level in range(2):
-        mine = (sums if level == 0 else swap_halves(sums))[:, :64]
-        lines = (dead if level == 0 else swap_halves(dead))[:, :64]
-        sum_o[level] = CODE_DECAY * ema_sum[level] + (1.0 - CODE_DECAY) * mine
-        for r in range(8):
-            sum_o[level, pl.ds(dead_codes[level, r], 1), :] = lines[r : r + 1]
         for b in range(4):
+            lanes = pl.ds(b * 128, 128)
             at = ROW_COUNT + level * 4 + b
-            used = total[at : at + 1, :]
+            ids = lane_iota((64, 128)) + b * 128
             count = CODE_DECAY * ema_count[level : level + 1, b * 128 : b * 128 + 128] + (
                 1.0 - CODE_DECAY
-            ) * used
-            ids = lane_iota((1, 128)) + b * 128
+            ) * total[at : at + 1, :]
+            at = ROW_SUMS + (level * 4 + b) * 64
+            sums = CODE_DECAY * ema_sum[level, :, lanes] + (1.0 - CODE_DECAY) * total[at : at + 64, :]
             for r in range(8):
-                count = jnp.where(ids == dead_codes[level, r], 1.0, count)
+                taken = ids == dead_codes[level, r]
+                count = jnp.where(taken[:1], 1.0, count)
+                sums = jnp.where(taken, dead[level * 64 : level * 64 + 64, r : r + 1], sums)
             count_o[level : level + 1, b * 128 : b * 128 + 128] = count
-            col = jnp.sum(jnp.where(same, count, 0.0), axis=1, keepdims=True)
-            book_o[level, b * 128 : b * 128 + 128, :] = (
-                sum_o[level, b * 128 : b * 128 + 128, :] / col
-            )
+            sum_o[level, :, lanes] = sums
+            book_o[level, :, lanes] = sums / count
 
 
 def update(dead_codes, valid_rows, total, weights, firsts, seconds, ema_count, ema_sum):
@@ -815,44 +950,31 @@
     part = device % parts
     image = device // parts
 
-    def regroup(x):
-        pieces = []
-        for k in range(parts):
-            target = (part + k) % parts
-            piece = lax.dynamic_slice_in_dim(x, (section * parts + target) * share, share, 0)
-            if k > 0:
-                pairs = [
-                    (base + p, base + (p + k) % parts)
-                    for base in range(0, devices, parts)
-                    for p in range(parts)
-                ]
-                piece = lax.ppermute(piece, "dp", pairs)
-            pieces.append(piece)
-        ordered = [lax.select_n((part - p) % parts, *pieces) if parts == 2 else None for p in range(parts)]
-        return jnp.stack(ordered, axis=1).reshape(share, parts * x.shape[1], x.shape[2])
-
-    def code_layouts(codes, level):
-        side = codes.shape[1]
-        if level == 0:
-            x = codes.reshape(share, side, side // 2, 2)
-            col = x.transpose(0, 2, 1, 3).reshape(share, side * side // 2, 2)
-            row = x.transpose(0, 3, 2, 1).reshape(share, 2, side * side // 2)
-        else:
-            x = codes.reshape(share, side // 2, 2, side // 2, 2)
-            col = x.transpose(0, 3, 2, 1, 4).reshape(share, side * side // 2, 2)
-            row = x.transpose(0, 4, 3, 2, 1).reshape(share, 2, side * side // 2)
-        return col, row
-
-    ct = code_layouts(regroup(codes_top), 0)
-    cb = code_layouts(regroup(codes_bottom), 1)
-    pix = regroup(pixels)
-    place = jnp.stack([(section * parts + part) * share, image]).astype(jnp.int32)
+    assert parts == 2 and sections == 2
+    first = (section * parts + part) * share
+    pairs = [(base + p, base + 1 - p) for base in range(0, devices, 2) for p in range(2)]
+
+    def swapped(x):
+        theirs = (section * parts + 1 - part) * share
+        return (x, lax.ppermute(lax.dynamic_slice_in_dim(x, theirs, share, 0), "dp", pairs))
+
+    def turn(arrays):
+        return [x.transpose(0, 2, 1) if x.shape[2] == 64 else x for x in arrays]
+
+    ct, cb, pix = swapped(codes_top), swapped(codes_bottom), swapped(pixels)
+    place = jnp.stack([first, image, part]).astype(jnp.int32)
     multiple = 8 * sections * devices
     total_rows = -(-ROW_END // multiple) * multiple
+    weights, firsts, seconds = turn(weights), turn(firsts), turn(seconds)
+    codebook, ema_sum = turn([codebook, ema_sum])
     packed = compute(place, valid_rows, dead_source, pix, ct, cb, weights, codebook, total_rows)
-    total = lax.psum(packed, ("section", "dp"))
+    total = all_sum(packed, devices)
     outs = update(dead_codes, valid_rows, total, weights, firsts, seconds, ema_count, ema_sum)
+    outs = [x.transpose(0, 2, 1) if len(x.shape) == 3 and x.shape[1] == 64 and turned else x for x, turned in zip(outs, TURNED)]
     return (outs[0].reshape(()),) + tuple(outs[1:])
+
+
+TURNED = (False, False) + (True, False, False, True, False, False) * 4 + (True, False, True)
 
 
 def solution(mesh):

time: 283 us -> 146 us (0.52)
  waiting for transfers between devices: 127 us -> 6.07 us
  local copies, waits for them, and re-layouts: 40.6 us -> 3.26 us
  Pallas kernels: 92.9 us -> 130 us
  between operations: 14.2 us -> 0.71 us
    psum x1 -> x0, waiting for transfers between devices: 126 us -> none  [body(): total = lax.psum(packed, ('section', 'dp'))]
    pallas_call x1 -> x2, Pallas kernels: 80.8 us -> 124 us  [the longest x1 82.8 us: compute(): pl.pallas_call(compute_kernel, grid_spec=pltpu.PrefetchScalarGridSpec(num...]
    unnamed x38 -> x6, local copies, waits for them, and re-layouts: 28.3 us -> 0.75 us
    ppermute x3, waiting for transfers between devices: 0.01 us -> 6.07 us  [swapped(): lax.ppermute(lax.dynamic_slice_in_dim(x, theirs, share, 0), 'dp', pairs)]
    pallas_call x1, Pallas kernels: 12.1 us -> 6.81 us  [update(): pl.pallas_call(update_kernel, out_shape=shapes, in_specs=[sm] + [vm] * 22...]
    transpose x4 -> x0, local copies, waits for them, and re-layouts: 4.99 us -> none  [the longest x1 2.51 us: code_layouts(): col = x.transpose(0, 3, 2, 1, 4).reshape(share, side * side // 2, 2)]
    another operation x5 -> x0, local copies, waits for them, and re-layouts: 3.3 us -> none  [the longest x1 2.15 us: code_layouts(): x = codes.reshape(share, side // 2, 2, side // 2, 2)]
  transfers between devices with their start and end apart: 4 -> 3, of which waited for: 1 -> 2; matrix products, arithmetic and copies ran while one was open for 9% -> 1% of each run, Pallas kernels for 0% -> 0%
where the time goes in v2:
time: 146 us
  Pallas kernels  130 us (89%)
  waiting for transfers between devices  6.07 us (4%)
  starting transfers between devices  5.03 us (3%)
  local copies, waits for them, and re-layouts  3.26 us (2%)
    pallas_call x1, Pallas kernels, compute(): pl.pallas_call(compute_kernel, grid_spec=pltpu.PrefetchScalarGridSpec(num...  82.8 us
    pallas_call x1, Pallas kernels, all_sum(): pl.pallas_call(functools.partial(reduce_kernel, plane), out_shape=jax.Sha...  40.9 us
    pallas_call x1, Pallas kernels, update(): pl.pallas_call(update_kernel, out_shape=shapes, in_specs=[sm] + [vm] * 22...  6.81 us
    ppermute x3, waiting for transfers between devices, swapped(): lax.ppermute(lax.dynamic_slice_in_dim(x, theirs, share, 0), 'dp', pairs)  6.07 us
    ppermute x3, starting transfers between devices, swapped(): lax.ppermute(lax.dynamic_slice_in_dim(x, theirs, share, 0), 'dp', pairs)  5.03 us
  transfers between devices with their start and end apart: 3, of which 2 were waited for; matrix products, arithmetic and copies ran while one was open for 1% of the time, Pallas kernels for 0%

profile of v2, /device:TPU:0, one launch (start us, length us, event | category | flops | bytes accessed | tf_op | source)
XLA Modules:
  0.0 146.1 jit_solution(13587845323697206734)
XLA Ops:
  0.7 1.0 constant_dynamic-slice_fusion.2
  1.7 3.0 %collective-permute-start = (bf16[2,128,768]{2,1,0:T(8,128)(2,1)S(1)}, bf16[2,128,768]{2,1,0:T(8,128)(2,1)S(1)}, u32[]{:S(2)}, u32[]{:S(2)}) collective-permute-start(bf16[2,128,768]{2,1,0:T(8,128)(2,1)S(1)} %constant_dynamic-slice_fusion.2), channel_id=1, source_target_pairs={{0,1},{1,0},{2,3},{3,2},{4,5},{5,4},{6,7},{7,6},{8,9},{9,8},{10,11... | collective-permute-start | bytes 1179656 | tf_op jit(solution)/shard_map/ppermute | solution.py:959
  4.7 0.7 constant_dynamic-slice_fusion.1
  5.4 0.0 collective-permute-start.1
  5.5 0.8 constant_dynamic-slice_fusion
  6.2 2.0 %collective-permute-start.2 = (s32[2,32,64]{2,1,0:T(8,128)S(1)}, s32[2,32,64]{2,1,0:T(8,128)S(1)}, u32[]{:S(2)}, u32[]{:S(2)}) collective-permute-start(s32[2,32,64]{2,1,0:T(8,128)S(1)} %constant_dynamic-slice_fusion), channel_id=1, source_target_pairs={{0,1},{1,0},{2,3},{3,2},{4,5},{5,4},{6,7},{7,6},{8,9},{9,8},{10,11... | collective-permute-start | bytes 49160 | tf_op jit(solution)/shard_map/ppermute | solution.py:959
  8.2 0.6 pad_add_fusion.place
  8.8 5.7 %collective-permute-done.1.ct_far = s32[2,16,32]{2,1,0:T(8,128)S(1)} collective-permute-done((s32[2,16,32]{2,1,0:T(8,128)S(1)}, s32[2,16,32]{2,1,0:T(8,128)S(1)}, u32[]{:S(2)}, u32[]{:S(2)}) %collective-permute-start.1) | collective-permute-done | bytes 4128 | tf_op jit(solution)/shard_map/ppermute | solution.py:959
  14.5 0.0 copy-start.2
  14.5 0.3 collective-permute-done.2.cb_far
  14.9 0.0 copy-start.1
  14.9 0.0 collective-permute-done.pix_far
  14.9 0.0 copy-start
  14.9 0.2 copy-done.2
  15.1 0.4 copy-done.1
  15.5 0.1 copy-done
  15.6 82.8 %step_compute.1.x = f32[3584,128]{1,0:T(8,128)} custom-call(s32[3]{0:T(128)} %pad_add_fusion.place, s32[8,8]{1,0:T(8,128)} %valid_v.3, s32[2,8]{1,0:T(2,128)} %dead_source.1, s32[8,8]{1,0:T(8,128)} %valid_v.3, bf16[8,128,768]{2,1,0:T(8,128)(2,1)} %pix.1, bf16[2,128,768]{2,1,0:T(8,128)(2,1)} %copy-done, s32[8,16,32]{2,1,0:T(8,128)} %ct_near.1, ...), custom_call_target="tpu_custom_call" | custom-call | tf_op jit(solution)/shard_map/step_compute/pallas_call | solution.py:710
  98.4 40.9 %step_reduce.1.total = f32[3584,128]{1,0:T(8,128)} custom-call(f32[3584,128]{1,0:T(8,128)} %step_compute.1.x), custom_call_target="tpu_custom_call" | custom-call | tf_op jit(solution)/shard_map/step_reduce/pallas_call | solution.py:839
  139.3 6.8 %step_update.1 = (f32[1]{0:T(128)}, f32[2]{0:T(128)}, f32[3,64,1152]{2,1,0:T(8,128)}, f32[3,64,128]{2,1,0:T(8,128)}, f32[5,64,128]{2,1,0:T(8,128)}, /*index=5*/f...) custom-call(s32[2,8]{1,0:T(2,128)} %dead_codes.1, ...), custom_call_target="tpu_custom_call" | custom-call | tf_op jit(solution)/shard_map/step_update/pallas_call | solution.py:930
Async XLA Ops:
  1.7 13.2 %collective-permute-start = (bf16[2,128,768]{2,1,0:T(8,128)(2,1)S(1)}, bf16[2,128,768]{2,1,0:T(8,128)(2,1)S(1)}, u32[]{:S(2)}, u32[]{:S(2)}) collective-permute-start(bf16[2,128,768]{2,1,0:T(8,128)(2,1)S(1)} %constant_dynamic-slice_fusion.2), channel_id=1, source_target_pairs={{0,1},{1,0},{2,3},{3,2},{4,5},{5,4},{6,7},{7,6},{8,9},{9,8},{10,11... | collective-permute-start | bytes 1179656 | tf_op jit(solution)/shard_map/ppermute | solution.py:959
  5.4 9.1 %collective-permute-start.1 = (s32[2,16,32]{2,1,0:T(8,128)S(1)}, s32[2,16,32]{2,1,0:T(8,128)S(1)}, u32[]{:S(2)}, u32[]{:S(2)}) collective-permute-start(s32[2,16,32]{2,1,0:T(8,128)S(1)} %constant_dynamic-slice_fusion.1), channel_id=1, source_target_pairs={{0,1},{1,0},{2,3},{3,2},{4,5},{5,4},{6,7},{7,6},{8,9},{9,8},{10,11... | collective-permute-start | bytes 12296 | tf_op jit(solution)/shard_map/ppermute | solution.py:959
  6.2 8.7 %collective-permute-start.2 = (s32[2,32,64]{2,1,0:T(8,128)S(1)}, s32[2,32,64]{2,1,0:T(8,128)S(1)}, u32[]{:S(2)}, u32[]{:S(2)}) collective-permute-start(s32[2,32,64]{2,1,0:T(8,128)S(1)} %constant_dynamic-slice_fusion), channel_id=1, source_target_pairs={{0,1},{1,0},{2,3},{3,2},{4,5},{5,4},{6,7},{7,6},{8,9},{9,8},{10,11... | collective-permute-start | bytes 49160 | tf_op jit(solution)/shard_map/ppermute | solution.py:959
  14.5 0.6 copy-start.2
  14.9 0.6 copy-start.1
  14.9 0.8 copy-start

commit v3 on v2

--- a/solution.py
+++ b/solution.py
@@ -20,7 +20,6 @@
 F32 = jnp.float32
 BF16 = jnp.bfloat16
 VMEM_LIMIT = 56 * 1024 * 1024
-CHUNK = 8
 
 TAP_ROWS = 64
 CONV_ROWS = 9 * TAP_ROWS
@@ -144,7 +143,7 @@
     d_two,
     d_slots,
     d_two_t,
-    d_slots_t,
+    gpre,
     gstem,
     gup,
     acc_conv,
@@ -163,19 +162,11 @@
     last = pl.num_programs(0) - 1
     pairs, rows = xs_bot.shape[0], xs_bot.shape[2]
     pairs_t = xs_top.shape[0]
-    ch = CHUNK
-    ch_t = CHUNK // 2
+    ch, ch_t = pairs, pairs_t
     height = 2 * pix.shape[1]
     valid_count = 3.0 * height * jnp.sum(valid_v[...].astype(F32))
     loss_slope = 2.0 / valid_count
     commit_slope = loss_slope * COMMIT_WEIGHT
-
-    def loop(total, size, fn):
-        def run(k, _):
-            fn(pl.multiple_of(k * size, size))
-            return 0
-
-        lax.fori_loop(0, total // size, run, 0)
 
     def picker(src, start):
         size = src.shape[0]
@@ -245,8 +236,8 @@
 
     def near_of(codes, level, c0, n, hot_ref):
         size = codes.shape[0]
-        here = pl.ds(pl.multiple_of(c0 * size, size), n * size)
-        moved = pltpu.roll(codes, lax.rem(128 - 2 * c0, 128), 1)
+        here = pl.ds(c0 * size, n * size)
+        moved = codes
         ids = lax.broadcasted_iota(jnp.int32, (size, 512), 1).astype(F32)
         v = []
         used = jnp.zeros((8, 512), F32)
@@ -254,7 +245,7 @@
             for j in range(n):
                 hot = (moved[:, 2 * j + cp : 2 * j + cp + 1] == ids).astype(F32)
                 used = used + jnp.sum(hot.reshape(size // 8, 8, 512), axis=0)
-                at = pl.ds(pl.multiple_of((c0 + j) * size, size), size)
+                at = pl.ds((c0 + j) * size, size)
                 hot_ref[at, pl.ds(cp * 512, 512)] = hot.astype(BF16)
             v.append(mm_t(hot_ref[here, pl.ds(cp * 512, 512)], table[level]))
         acc_count[level] += used
@@ -274,7 +265,7 @@
                     at = (cq * 2 + rp) * 256
                     up[2 * (c0 + c) + cq, rp] = u[c, :, at : at + 256]
 
-    loop(pairs_t, ch_t, top_codes)
+    top_codes(0)
 
     def put_slots(ref, c0, n, even, odd):
         ref[pl.ds(c0, n), 0] = shift_rows(odd, 1).astype(BF16)
@@ -290,7 +281,7 @@
         res[pl.ds(c0, ch)] = x
         put_slots(xs_dec, c0, ch, x[:, 0], x[:, 1])
 
-    loop(pairs, ch, bottom_codes)
+    bottom_codes(0)
 
     def conv_wide(xs, k):
         def run(c0):
@@ -301,7 +292,7 @@
                 y = mm_t(taps, b_fwd[k])
                 wide[pl.ds(c0 + 1, ch), rp] = y.reshape(ch, rows, 256)
 
-        loop(pairs, ch, run)
+        run(0)
 
     def gather_wide(c0, n, rp):
         before = wide[pl.ds(c0, n), rp, :, 128:]
@@ -321,7 +312,7 @@
         low_dec[pl.ds(c0 * 2 * rows, n), :] = low
         resid[pl.ds(c0 * 2 * rows, n), :] = mm_t(low, pix_d[1])
 
-    loop(pairs, ch, decode_out)
+    decode_out(0)
 
     per_tile = 2 * rows
     picked = mm(sel[...], jnp.concatenate([pix[0], pix_far[0]], axis=0))
@@ -349,7 +340,7 @@
         s = (pre * sigmoid(pre)).astype(BF16)
         stem[pl.ds(c0, ch)] = s.reshape(ch, 2, rows, 256)
 
-    loop(pairs, ch, stem_of)
+    stem_of(0)
 
     def top_in(c0):
         for cq in range(2):
@@ -363,7 +354,7 @@
             xs_top[pl.ds(c0, ch_t), 1, :, pl.ds(cq * 128, 128)] = x.astype(BF16)
             xs_top[pl.ds(c0, ch_t), 2, :, pl.ds(cq * 128, 128)] = shift_rows(x, -1).astype(BF16)
 
-    loop(pairs_t, ch_t, top_in)
+    top_in(0)
 
     wide[pairs_t + 1, 0] = jnp.zeros((rows, 256), F32)
 
@@ -371,7 +362,7 @@
         taps = jnp.concatenate([flat(xs_top[pl.ds(c0, ch_t), t]) for t in range(3)], axis=1)
         wide[pl.ds(c0 + 1, ch_t), 0] = mm_t(taps, b_fwd[0]).reshape(ch_t, rows, 256)
 
-    loop(pairs_t, ch_t, top_conv)
+    top_conv(0)
 
     def add_num(x):
         acc_num[...] += jnp.sum(x.reshape(x.shape[0] // 8, 8, 128), axis=0)
@@ -401,14 +392,14 @@
         diff = latent - near_t[here, :]
         add_num(COMMIT_WEIGHT * diff * diff)
 
-    loop(pairs_t, ch_t, top_out)
+    top_out(0)
 
     def bottom_in(c0):
         x = stem[pl.ds(c0, ch)].astype(F32) + up[pl.ds(c0, ch)]
         res[pl.ds(c0, ch)] = x
         put_slots(xs_bot, c0, ch, x[:, 0], x[:, 1])
 
-    loop(pairs, ch, bottom_in)
+    bottom_in(0)
     conv_wide(xs_bot, 1)
 
     def bottom_out(c0):
@@ -426,7 +417,7 @@
         diff = latent - near[here, :]
         add_num(COMMIT_WEIGHT * diff * diff)
 
-    loop(pairs, ch, bottom_out)
+    bottom_out(0)
 
     micro = place[0] + step
     image = place[1]
@@ -499,7 +490,7 @@
         acc_conv[k] += total
         return jnp.stack(outs, axis=1)
 
-    loop(pairs, ch, decode_back)
+    decode_back(0)
 
     def decode_in_back(c0):
         n = ch * 2 * rows
@@ -514,7 +505,7 @@
         acc_to[1] += mm_w(g_lat, low_bot[here, :])
         grad_hi[pl.ds(c0, ch)] = mm(g_lat, to_d[1]).reshape(ch, 2, rows, 256)
 
-    loop(pairs, ch, decode_in_back)
+    decode_in_back(0)
 
     def bottom_back(c0):
         n = ch * 2 * rows
@@ -522,7 +513,7 @@
             grad_hi[pl.ds(c0, ch)].reshape(n, 256), act_bot[pl.ds(c0 * 2 * rows, n), :], 1, c0
         )
 
-    loop(pairs, ch, bottom_back)
+    bottom_back(0)
 
     def bottom_in_back(c0):
         g = grad_hi[pl.ds(c0, ch)] + conv_back(1, xs_bot, c0)
@@ -534,7 +525,7 @@
             [total[:, cq, rp].reshape(half * rows, 256) for cq in range(2) for rp in range(2)],
             axis=1,
         )
-        t0 = pl.multiple_of(lax.div(c0, 2) * rows, half * rows)
+        t0 = c0 // 2 * rows
         here = pl.ds(t0, half * rows)
         full = near_t[here, :]
         acc_up[...] += mm_w(full.astype(BF16), wide_g)
@@ -548,9 +539,9 @@
         s = sigmoid(a)
         acc_res[0] += mm_w((a * s).astype(BF16), g_low)
         d = (mm_t(g_low, wo_d[0]) * (s * (1.0 + a * (1.0 - s)))).astype(BF16)
-        d_two_t[pl.ds(lax.div(c0, 2) + 1, half)] = d.astype(F32).reshape(half, rows, 128)
-
-    loop(pairs, ch, bottom_in_back)
+        d_two_t[pl.ds(c0 // 2 + 1, half)] = d.astype(F32).reshape(half, rows, 128)
+
+    bottom_in_back(0)
 
     def top_back(c0):
         n = ch_t * rows
@@ -579,14 +570,15 @@
             g_st = mm_t(g_cq, down_b[...]).reshape(ch_t, rows, 512)
             for c in range(ch_t):
                 col = 2 * (c0 + c) + cq
-                p = patches[pl.ds(pl.multiple_of(col * 2 * rows, 2 * rows), 2 * rows), :]
-                sl = slope(mm(p, pix_d[0]))
+                at = pl.ds(col * 2 * rows, 2 * rows)
+                sl = slope(mm(patches[at, :], pix_d[0]))
                 g_t = jnp.concatenate([g_st[c, :, :256], g_st[c, :, 256:]], axis=0)
                 g_b = gstem[col].reshape(2 * rows, 256).astype(F32)
-                both = jnp.concatenate([(g_t * sl).astype(BF16), (g_b * sl).astype(BF16)], axis=0)
-                acc_pix[0] += mm_w(jnp.concatenate([p, p], axis=0), both)
-
-    loop(pairs_t, ch_t, top_back)
+                gpre[0, at, :] = (g_t * sl).astype(BF16)
+                gpre[1, at, :] = (g_b * sl).astype(BF16)
+        acc_pix[0] += mm_w(patches[...], gpre[0]) + mm_w(patches[...], gpre[1])
+
+    top_back(0)
 
     @pl.when(step == last)
     def _():
@@ -692,7 +684,7 @@
         v((pairs + 2, 2, rows, 128), F32),
         v((pairs, 4, rows, 256), BF16),
         v((pairs_t + 2, rows, 128), F32),
-        v((8, 128), BF16),
+        v((2, n, 256), BF16),
         v((pairs, 2, rows, 256), BF16),
         v((pairs, 2, rows, 256), F32),
         v((3, 256, 768), F32),

time: 146 us -> 108 us (0.74)
  Pallas kernels: 130 us -> 91.7 us
    pallas_call x1, Pallas kernels: 82.8 us -> 43.9 us  [compute(): pl.pallas_call(compute_kernel, grid_spec=pltpu.PrefetchScalarGridSpec(num...]
  transfers between devices with their start and end apart: 3 -> 3, of which waited for: 2 -> 2; matrix products, arithmetic and copies ran while one was open for 1% -> 2% of each run, Pallas kernels for 0% -> 0%
where the time goes in v3:
time: 108 us
  Pallas kernels  91.7 us (85%)
  waiting for transfers between devices  6.07 us (6%)
  starting transfers between devices  5.03 us (5%)
  local copies, waits for them, and re-layouts  3.26 us (3%)
    pallas_call x1, Pallas kernels, compute(): pl.pallas_call(compute_kernel, grid_spec=pltpu.PrefetchScalarGridSpec(num...  43.9 us
    pallas_call x1, Pallas kernels, all_sum(): pl.pallas_call(functools.partial(reduce_kernel, plane), out_shape=jax.Sha...  40.9 us
    pallas_call x1, Pallas kernels, update(): pl.pallas_call(update_kernel, out_shape=shapes, in_specs=[sm] + [vm] * 22...  6.87 us
    ppermute x3, waiting for transfers between devices, swapped(): lax.ppermute(lax.dynamic_slice_in_dim(x, theirs, share, 0), 'dp', pairs)  6.07 us
    ppermute x3, starting transfers between devices, swapped(): lax.ppermute(lax.dynamic_slice_in_dim(x, theirs, share, 0), 'dp', pairs)  5.03 us
    dynamic_slice x3, local copies, waits for them, and re-layouts, swapped(): lax.dynamic_slice_in_dim(x, theirs, share, 0)  2.5 us
  transfers between devices with their start and end apart: 3, of which 2 were waited for; matrix products, arithmetic and copies ran while one was open for 2% of the time, Pallas kernels for 0%

profile of v3, /device:TPU:0, one launch (start us, length us, event | category | flops | bytes accessed | tf_op | source)
XLA Modules:
  0.0 107.5 jit_solution(15676016265744488659)
XLA Ops:
  0.7 1.0 constant_dynamic-slice_fusion.2
  1.7 3.0 %collective-permute-start = (bf16[2,128,768]{2,1,0:T(8,128)(2,1)S(1)}, bf16[2,128,768]{2,1,0:T(8,128)(2,1)S(1)}, u32[]{:S(2)}, u32[]{:S(2)}) collective-permute-start(bf16[2,128,768]{2,1,0:T(8,128)(2,1)S(1)} %constant_dynamic-slice_fusion.2), channel_id=1, source_target_pairs={{0,1},{1,0},{2,3},{3,2},{4,5},{5,4},{6,7},{7,6},{8,9},{9,8},{10,11... | collective-permute-start | bytes 1179656 | tf_op jit(solution)/shard_map/ppermute | solution.py:951
  4.7 0.7 constant_dynamic-slice_fusion.1
  5.4 0.0 collective-permute-start.1
  5.5 0.8 constant_dynamic-slice_fusion
  6.2 2.0 %collective-permute-start.2 = (s32[2,32,64]{2,1,0:T(8,128)S(1)}, s32[2,32,64]{2,1,0:T(8,128)S(1)}, u32[]{:S(2)}, u32[]{:S(2)}) collective-permute-start(s32[2,32,64]{2,1,0:T(8,128)S(1)} %constant_dynamic-slice_fusion), channel_id=1, source_target_pairs={{0,1},{1,0},{2,3},{3,2},{4,5},{5,4},{6,7},{7,6},{8,9},{9,8},{10,11... | collective-permute-start | bytes 49160 | tf_op jit(solution)/shard_map/ppermute | solution.py:951
  8.2 0.6 pad_add_fusion.place
  8.8 5.7 %collective-permute-done.1.ct_far = s32[2,16,32]{2,1,0:T(8,128)S(1)} collective-permute-done((s32[2,16,32]{2,1,0:T(8,128)S(1)}, s32[2,16,32]{2,1,0:T(8,128)S(1)}, u32[]{:S(2)}, u32[]{:S(2)}) %collective-permute-start.1) | collective-permute-done | bytes 4128 | tf_op jit(solution)/shard_map/ppermute | solution.py:951
  14.5 0.0 copy-start.2
  14.5 0.3 collective-permute-done.2.cb_far
  14.9 0.0 copy-start.1
  14.9 0.0 collective-permute-done.pix_far
  14.9 0.0 copy-start
  14.9 0.2 copy-done.2
  15.1 0.4 copy-done.1
  15.5 0.1 copy-done
  15.6 43.9 %step_compute.1.x = f32[3584,128]{1,0:T(8,128)} custom-call(s32[3]{0:T(128)} %pad_add_fusion.place, s32[8,8]{1,0:T(8,128)} %valid_v.3, s32[2,8]{1,0:T(2,128)} %dead_source.1, s32[8,8]{1,0:T(8,128)} %valid_v.3, bf16[8,128,768]{2,1,0:T(8,128)(2,1)} %pix.1, bf16[2,128,768]{2,1,0:T(8,128)(2,1)} %copy-done, s32[8,16,32]{2,1,0:T(8,128)} %ct_near.1, ...), custom_call_target="tpu_custom_call" | custom-call | tf_op jit(solution)/shard_map/step_compute/pallas_call | solution.py:702
  59.6 40.9 %step_reduce.1.total = f32[3584,128]{1,0:T(8,128)} custom-call(f32[3584,128]{1,0:T(8,128)} %step_compute.1.x), custom_call_target="tpu_custom_call" | custom-call | tf_op jit(solution)/shard_map/step_reduce/pallas_call | solution.py:831
  100.5 6.9 %step_update.1 = (f32[1]{0:T(128)}, f32[2]{0:T(128)}, f32[3,64,1152]{2,1,0:T(8,128)}, f32[3,64,128]{2,1,0:T(8,128)}, f32[5,64,128]{2,1,0:T(8,128)}, /*index=5*/f...) custom-call(s32[2,8]{1,0:T(2,128)} %dead_codes.1, ...), custom_call_target="tpu_custom_call" | custom-call | tf_op jit(solution)/shard_map/step_update/pallas_call | solution.py:922
Async XLA Ops:
  1.7 13.2 %collective-permute-start = (bf16[2,128,768]{2,1,0:T(8,128)(2,1)S(1)}, bf16[2,128,768]{2,1,0:T(8,128)(2,1)S(1)}, u32[]{:S(2)}, u32[]{:S(2)}) collective-permute-start(bf16[2,128,768]{2,1,0:T(8,128)(2,1)S(1)} %constant_dynamic-slice_fusion.2), channel_id=1, source_target_pairs={{0,1},{1,0},{2,3},{3,2},{4,5},{5,4},{6,7},{7,6},{8,9},{9,8},{10,11... | collective-permute-start | bytes 1179656 | tf_op jit(solution)/shard_map/ppermute | solution.py:951
  5.4 9.1 %collective-permute-start.1 = (s32[2,16,32]{2,1,0:T(8,128)S(1)}, s32[2,16,32]{2,1,0:T(8,128)S(1)}, u32[]{:S(2)}, u32[]{:S(2)}) collective-permute-start(s32[2,16,32]{2,1,0:T(8,128)S(1)} %constant_dynamic-slice_fusion.1), channel_id=1, source_target_pairs={{0,1},{1,0},{2,3},{3,2},{4,5},{5,4},{6,7},{7,6},{8,9},{9,8},{10,11... | collective-permute-start | bytes 12296 | tf_op jit(solution)/shard_map/ppermute | solution.py:951
  6.2 8.7 %collective-permute-start.2 = (s32[2,32,64]{2,1,0:T(8,128)S(1)}, s32[2,32,64]{2,1,0:T(8,128)S(1)}, u32[]{:S(2)}, u32[]{:S(2)}) collective-permute-start(s32[2,32,64]{2,1,0:T(8,128)S(1)} %constant_dynamic-slice_fusion), channel_id=1, source_target_pairs={{0,1},{1,0},{2,3},{3,2},{4,5},{5,4},{6,7},{7,6},{8,9},{9,8},{10,11... | collective-permute-start | bytes 49160 | tf_op jit(solution)/shard_map/ppermute | solution.py:951
  14.5 0.6 copy-start.2
  14.9 0.6 copy-start.1
  14.9 0.8 copy-start

commit v4 on v1

v4 whole, which is shorter than its diff:
```python
import functools

import jax
import jax.numpy as jnp
from jax import lax
from jax.experimental import pallas as pl
from jax.experimental.pallas import tpu as pltpu
from jax.sharding import PartitionSpec as P

STEP = 10
COMMIT_WEIGHT = 0.25
CODE_DECAY = 0.9
CLIP_NORM = 0.001
LEARN_RATE = 0.03
MOMENT_ONE = 0.9
MOMENT_TWO = 0.999
WEIGHT_DECAY = 0.01
ADAM_EPSILON = 1e-08

F32 = jnp.float32
BF16 = jnp.bfloat16
VMEM_LIMIT = 62 * 1024 * 1024
PARTS = 2

MESH = pl.DeviceIdType.MESH
Z_SIZE = 4
DEAD = 8
GROUPS = (
    (("conv2", 576), ("res2", 64), ("from0", 64), ("pixel1", 48)),
    (("sums", 512), ("count", 8), ("dead", 8), ("numer", 8)),
    (("conv1", 576), ("res1", 64), ("from1", 64), ("from2", 64), ("from3", 64), ("from4", 64), ("to1", 64), ("to0", 64)),
    (("conv0", 576), ("res0", 64), ("pixel0", 48), ("down", 512)),
)


def row_layout(devices):
    multiple = 16 * devices
    at, groups, row = {}, [], 0
    for group in GROUPS:
        start = row
        for name, size in group:
            at[name] = row
            row += size
        row = start + -(-(row - start) // multiple) * multiple
        groups.append((start, row - start))
    return at, groups, row


def mm(x, w):
    return lax.dot_general(x, w, (((1,), (0,)), ((), ())), preferred_element_type=F32)


def mm_t(x, w):
    return lax.dot_general(x, w, (((1,), (1,)), ((), ())), preferred_element_type=F32)


def mm_w(x, g):
    return lax.dot_general(x, g, (((0,), (0,)), ((), ())), preferred_element_type=F32)


def lane_iota(shape):
    return lax.broadcasted_iota(jnp.int32, shape, len(shape) - 1)


def low_half(shape):
    return lane_iota(shape) % 128 < 64


def sigmoid(x):
    return 0.5 * jnp.tanh(0.5 * x) + 0.5


def slope(a):
    s = sigmoid(a)
    return s * (1.0 + a * (1.0 - s))


def shift_rows(x, by):
    rows = x.shape[1]
    moved = pltpu.roll(x, by % rows, 1)
    ids = lax.broadcasted_iota(jnp.int32, x.shape, 1)
    edge = 0 if by == 1 else rows - 1
    return jnp.where(ids == edge, 0.0, moved)


def flat(x):
    return x.reshape(x.shape[0] * x.shape[1], x.shape[2])


def pair_diag(w):
    zero = jnp.zeros_like(w)
    return jnp.concatenate(
        [jnp.concatenate([w, zero], axis=1), jnp.concatenate([zero, w], axis=1)], axis=0
    )


def swap_halves(x):
    return pltpu.roll(x, 64, len(x.shape) - 1)


def partners_of(plane):
    s = lax.axis_index("section")
    d = lax.axis_index("dp")
    z, q = lax.div(d, plane), lax.rem(d, plane)
    peer = (1 - s, d)
    mates = [lax.rem(q + k, plane) for k in range(plane)]
    levels = [lax.rem(z + k, Z_SIZE) for k in range(Z_SIZE)]
    partners = [peer] + [(s, z * plane + m) for m in mates[1:]] + [(s, l * plane + q) for l in levels[1:]]
    return s, z, q, peer, mates, levels, partners


class Reduction:
    def __init__(self, plane, base, total, x, out, one, two, sums, three, acc, ssem, rsem):
        half, part = total // 2, total // 2 // plane
        chunk = part // Z_SIZE
        s, z, q, peer, mates, levels, _ = partners_of(plane)
        mine = base + s * half
        self.x, self.out, self.one, self.two, self.sums, self.three, self.acc = x, out, one, two, sums, three, acc
        self.plane, self.part, self.chunk = plane, part, chunk
        self.own = mine + q * part + z * chunk
        self.z_row = z * chunk
        self.mates, self.mine = mates, mine
        to_mates = [(s, z * plane + m) for m in mates[1:]]
        to_levels = [(s, l * plane + q) for l in levels[1:]]
        moves = [(self.rows(x, base + (1 - s) * half, half), one, peer)]
        moves += [(sums.at[k], two.at[k], to) for k, to in enumerate(to_mates)]
        moves += [
            (self.rows(acc, l * chunk, chunk), three.at[k], to)
            for k, (l, to) in enumerate(zip(levels[1:], to_levels))
        ]
        own = self.rows(out, self.own, chunk)
        moves += [(own, own, to) for to in to_levels]
        own = self.rows(out, mine + q * part, part)
        moves += [(own, own, to) for to in to_mates]
        own = self.rows(out, mine, half)
        moves += [(own, own, peer)]
        self.moves, self.ssem, self.rsem = moves, ssem, rsem
        a, b = plane - 1, Z_SIZE - 1
        stops = [0, 1, 1 + a, 1 + a + b, 1 + a + 2 * b, 1 + 2 * a + 2 * b, 2 + 2 * a + 2 * b]
        self.stage = [range(lo, hi) for lo, hi in zip(stops, stops[1:])]

    def rows(self, ref, start, size):
        return ref.at[pl.ds(pl.multiple_of(start, 8), size)]

    def copy(self, k):
        src, dst, to = self.moves[k]
        return pltpu.make_async_remote_copy(
            src, dst, self.ssem.at[k], self.rsem.at[k], device_id=to, device_id_type=MESH
        )

    def step(self, number):
        if number > 0:
            for k in self.stage[number - 1]:
                self.copy(k).wait_recv()
        part, chunk = self.part, self.chunk
        if number == 1:
            for k in list(range(1, self.plane)) + [0]:
                at = self.mates[k] * part
                value = self.rows(self.x, self.mine + at, part)[...] + self.rows(self.one, at, part)[...]
                if k == 0:
                    self.acc[...] = value
                else:
                    self.sums[k - 1] = value
                    self.copy(k).start()
            return
        if number == 2:
            value = self.acc[...]
            for j in range(self.plane - 1):
                value = value + self.two[j]
            self.acc[...] = value
        if number == 3:
            value = self.rows(self.acc, self.z_row, chunk)[...]
            for k in range(1, Z_SIZE):
                value = value + self.three[k - 1]
            self.rows(self.out, self.own, chunk)[...] = value
        if number < 6:
            for k in self.stage[number]:
                self.copy(k).start()
        else:
            for k in range(len(self.moves)):
                self.copy(k).wait_send()


def reduce_scratch(plane, total):
    part = total // 2 // plane
    chunk = part // Z_SIZE
    v = pltpu.VMEM
    count = 2 + 2 * (plane - 1) + 2 * (Z_SIZE - 1)
    return [
        v((total // 2, 128), F32),
        v((plane - 1, part, 128), F32),
        v((plane - 1, part, 128), F32),
        v((Z_SIZE - 1, chunk, 128), F32),
        v((part, 128), F32),
        pltpu.SemaphoreType.DMA((count,)),
        pltpu.SemaphoreType.DMA((count,)),
    ]


REDUCE_REFS = 7
SCRATCH = (
    "b_fwd", "b_bwd", "wo_d", "from_d", "to_d", "up_d", "pix_d", "down_b", "book_a", "book_b", "sel", "hot",
    "near", "near_t", "quant_t", "patches", "stem", "xs", "xs_top", "wide", "res", "act", "act_t", "low",
    "low_t", "lat_t", "resid", "gup", "gquant", "gtop", "d_two", "d_two_t", "d_slots", "acc_conv",
    "acc_res", "acc_from", "acc_up", "acc_to", "acc_pix", "acc_down", "acc_sums", "acc_count", "acc_dead",
    "acc_num", "pix", "pix_far", "ct_near", "ct_far", "cb_near", "cb_far", "in_sems", "weight_sems",
    "packed", "valid_s", "valid_v", "dead_source", "codes_t", "codes_b", "w_conv", "w_res", "w_from", "w_to",
    "w_pix", "w_down", "book",
)


def scratch_of(share, height, valid, dead, pixels, ct, cb, weights, total_rows, plane, groups):
    pairs, rows = height // 8, height // 8
    pairs_t = pairs // 2
    n, n_t = pairs * 2 * rows, pairs_t * rows
    v = pltpu.VMEM
    shapes = dict(
        b_fwd=v((3, 256, 768), BF16),
        b_bwd=v((3, 768, 256), BF16),
        wo_d=v((3, 128, 256), BF16),
        from_d=v((128, 256), BF16),
        to_d=v((2, 128, 256), BF16),
        up_d=v((128, 1024), BF16),
        pix_d=v((2, 128, 256), BF16),
        down_b=v((512, 128), BF16),
        book_a=v((2, 256, 512), BF16),
        book_b=v((2, 256, 512), BF16),
        sel=v((height, height), BF16),
        hot=v((n, 512), BF16),
        near=v((share, n, 128), F32),
        near_t=v((share, n_t, 128), F32),
        quant_t=v((share, n_t, 128), BF16),
        patches=v((share, n, 128), BF16),
        stem=v((share, pairs, 2, rows, 256), BF16),
        xs=v((share, pairs, 4, rows, 256), BF16),
        xs_top=v((share, pairs_t, 3, rows, 256), BF16),
        wide=v((pairs + 2, 2, rows, 256), F32),
        res=v((pairs, 2, rows, 256), F32),
        act=v((share, n, 128), F32),
        act_t=v((share, n_t, 128), F32),
        low=v((share, n, 256), BF16),
        low_t=v((share, n_t, 256), BF16),
        lat_t=v((n_t, 128), F32),
        resid=v((share, n, 128), F32),
        gup=v((share, pairs, 2, rows, 256), F32),
        gquant=v((share, n, 128), F32),
        gtop=v((share, n_t, 256), F32),
        d_two=v((pairs + 2, 2, rows, 128), F32),
        d_two_t=v((share, pairs_t + 2, rows, 128), F32),
        d_slots=v((pairs, 4, rows, 256), BF16),
        acc_conv=v((3, 256, 768), F32),
        acc_res=v((3, 128, 256), F32),
        acc_from=v((128, 256), F32),
        acc_up=v((128, 1024), F32),
        acc_to=v((2, 128, 256), F32),
        acc_pix=v((2, 128, 256), F32),
        acc_down=v((512, 128), F32),
        acc_sums=v((2, 128, 512), F32),
        acc_count=v((2, 8, 512), F32),
        acc_dead=v((DEAD, 128), F32),
        acc_num=v((8, 128), F32),
        pix=v((share,) + pixels.shape[1:], pixels.dtype),
        pix_far=v((share,) + pixels.shape[1:], pixels.dtype),
        ct_near=v((share,) + ct.shape[1:], ct.dtype),
        ct_far=v((share,) + ct.shape[1:], ct.dtype),
        cb_near=v((share,) + cb.shape[1:], cb.dtype),
        cb_far=v((share,) + cb.shape[1:], cb.dtype),
        in_sems=pltpu.SemaphoreType.DMA((9,)),
        codes_t=v((share, height // 8, height // 8), F32),
        codes_b=v((share, height // 4, height // 4), F32),
        weight_sems=pltpu.SemaphoreType.DMA((10,)),
        valid_s=pltpu.SMEM(valid.shape, valid.dtype),
        valid_v=v(valid.shape, valid.dtype),
        dead_source=pltpu.SMEM(dead.shape, dead.dtype),
        packed=v((total_rows, 128), F32),
    )
    for name, w in zip(SCRATCH[-7:], weights):
        shapes[name] = v(w.shape, w.dtype)
    scratch = [shapes[name] for name in SCRATCH]
    for _, size in groups:
        scratch += reduce_scratch(plane, size)
    return scratch


class Refs:
    def __init__(self, names, refs):
        for name, ref in zip(names, refs):
            setattr(self, name, ref)


def compute_kernel(devices, valid_rows, dead_rows, pixels, codes_top, codes_bottom, *refs):
    weights_hbm, out, scratch = refs[:7], refs[7], refs[8:]
    r = Refs(SCRATCH, scratch)
    reduce_refs = scratch[len(SCRATCH) :]
    plane = devices // Z_SIZE
    at, groups, _ = row_layout(devices)
    packed = r.packed
    section, _, _, _, _, _, partners = partners_of(plane)
    device = lax.axis_index("dp")
    part, image = lax.rem(device, 2), lax.div(device, 2)
    share = r.pix.shape[0]
    first = (section * 2 + part) * share
    theirs = (section * 2 + 1 - part) * share
    mate = (section, device + 1 - 2 * part)
    height = 2 * r.pix.shape[1]
    pairs, rows = r.res.shape[0], r.res.shape[2]
    pairs_t = r.xs_top.shape[1]
    n, n_t = pairs * 2 * rows, pairs_t * rows
    ch = pairs // PARTS
    starts = range(0, pairs, ch)
    size = ch * 2 * rows

    def span(c0):
        return pl.ds(c0 * 2 * rows, size)

    inputs = (
        (pixels, r.pix, r.pix_far),
        (codes_top, r.ct_near, r.ct_far),
        (codes_bottom, r.cb_near, r.cb_far),
    )
    barrier = pltpu.get_barrier_semaphore()
    for p in partners:
        pl.semaphore_signal(barrier, inc=1, device_id=p, device_id_type=MESH)
    local, remote, loads = {}, {}, {}
    for k in (1, 2):
        src, near_ref, _ = inputs[k]
        local[k] = pltpu.make_async_copy(src.at[pl.ds(first, share)], near_ref, r.in_sems.at[k])
        local[k].start()
    w_conv, w_res, w_from, w_to, w_pix, w_down, book = [getattr(r, name) for name in SCRATCH[-7:]]
    for k in (6, 2, 0, 1, 3, 4, 5):
        loads[k] = pltpu.make_async_copy(weights_hbm[k], getattr(r, SCRATCH[k - 7]), r.weight_sems.at[k])
        loads[k].start()
    valid_s, valid_v, dead_source = r.valid_s, r.valid_v, r.dead_source
    for k, src, dst in ((7, valid_rows, valid_s), (8, valid_rows, valid_v), (9, dead_rows, dead_source)):
        loads[k] = pltpu.make_async_copy(src, dst, r.weight_sems.at[k])
        loads[k].start()
    local[0] = pltpu.make_async_copy(pixels.at[pl.ds(first, share)], r.pix, r.in_sems.at[0])
    local[0].start()
    pl.semaphore_wait(barrier, len(partners))
    for k in (1, 2, 0):
        src, near_ref, far_ref = inputs[k]
        remote[k] = pltpu.make_async_remote_copy(
            src.at[pl.ds(theirs, share)],
            far_ref,
            r.in_sems.at[3 + k],
            r.in_sems.at[6 + k],
            device_id=mate,
            device_id_type=MESH,
        )
        remote[k].start()

    reductions = []
    for group, (base, count) in enumerate(groups):
        refs = reduce_refs[group * REDUCE_REFS : (group + 1) * REDUCE_REFS]
        reductions.append(Reduction(plane, base, count, packed, out, *refs))

    def begin(group):
        start, size = groups[group]
        used = sum(size for _, size in GROUPS[group])
        if size > used:
            packed[start + used : start + size, :] = jnp.zeros((size - used, 128), F32)
        reductions[group].step(0)

    def steps(*which):
        for group, number in which:
            reductions[group].step(number)

    def between(*per_image):
        def run(img):
            for want, which in enumerate(per_image):
                if which:
                    pl.when(img == want)(functools.partial(steps, *which))

        return run

    def accum(ref, index, value, img):
        ref[index] += value

    def picker(src, start):
        size = src.shape[0]
        ids = lax.broadcasted_iota(jnp.int32, src.shape, 1) + start
        ids = jnp.where(ids >= size, ids - size, ids)
        return (ids == src).astype(F32).astype(BF16)

    for name in SCRATCH:
        if name[:4] == "acc_":
            ref = getattr(r, name)
            ref[...] = jnp.zeros(ref.shape, F32)
    for edge in (0, pairs + 1):
        r.wide[edge] = jnp.zeros(r.wide.shape[1:], F32)
        r.d_two[edge] = jnp.zeros(r.d_two.shape[1:], F32)
    for img in range(share):
        for edge in (0, pairs_t + 1):
            r.d_two_t[img, edge] = jnp.zeros(r.d_two_t.shape[2:], F32)
    for c in loads.values():
        c.wait()
    valid_count = 3.0 * height * jnp.sum(valid_v[...].astype(F32))
    loss_slope = 2.0 / valid_count
    commit_slope = loss_slope * COMMIT_WEIGHT

    zero = jnp.zeros((64, 128), F32)
    for k in range(3):
        for i in range(3):
            t = [w_conv[k, :, pl.ds((i * 3 + j) * 128, 128)] for j in range(3)]
            even = jnp.concatenate([t[1], t[0], zero, t[2]], axis=0).astype(BF16)
            odd = jnp.concatenate([t[2], t[1], t[0], zero], axis=0).astype(BF16)
            both = jnp.concatenate([even, odd], axis=1)
            r.b_fwd[k, :, pl.ds(i * 256, 256)] = both
            r.b_bwd[k, pl.ds((2 - i) * 256, 256), :] = both
        r.wo_d[k] = pair_diag(w_res[k]).astype(BF16)
    r.from_d[...] = pair_diag(w_from[0]).astype(BF16)
    for k in range(2):
        r.to_d[k] = pair_diag(w_to[k]).astype(BF16)
    r.up_d[...] = pair_diag(jnp.concatenate([w_from[k] for k in range(1, 5)], axis=1)).astype(BF16)
    lane = lax.broadcasted_iota(jnp.int32, (128, 48), 0)
    tap = lax.broadcasted_iota(jnp.int32, (128, 48), 1)
    for k in range(2):
        w_low = w_pix[k].astype(BF16)
        for cp in range(2):
            pick = (lane == (tap // 12) * 24 + cp * 12 + tap % 12).astype(F32).astype(BF16)
            r.pix_d[k, :, pl.ds(cp * 128, 128)] = mm(pick, w_low).astype(BF16)
    for k in range(4):
        r.down_b[pl.ds(k * 128, 128), :] = w_down[k].astype(BF16)
    for k in range(2):
        full = book[k]
        hi = full.astype(BF16).astype(F32)
        mid = (full - hi).astype(BF16).astype(F32)
        lo = full - hi - mid
        empty = jnp.zeros_like(full)
        r.book_a[k] = jnp.concatenate([hi, mid, lo, empty], axis=0).astype(BF16)
        r.book_b[k] = jnp.concatenate([mid, hi, empty, lo], axis=0).astype(BF16)
    o = lax.broadcasted_iota(jnp.int32, (height, height), 0)
    quarter = height // 4
    r.sel[...] = picker(8 * (o % rows) + 4 * ((o % quarter) // rows) + o // quarter, part * (height // 2))

    for k in (1, 2):
        local[k].wait()
        remote[k].wait()

    def codes_of(near_ref, far_ref, img, split):
        both = jnp.concatenate([near_ref[img], far_ref[img]], axis=0).astype(F32)
        size = both.shape[0]
        o = lax.broadcasted_iota(jnp.int32, (size, size), 0)
        pick = picker(2 * (o % rows) + o // rows if split else o, part * (size // 2))
        high = jnp.floor(both * (1.0 / 256.0))
        rest = both - 256.0 * high
        return 256.0 * mm(pick, high.astype(BF16)) + mm(pick, rest.astype(BF16))

    for img in range(share):
        r.codes_t[img] = codes_of(r.ct_near, r.ct_far, img, False)
        r.codes_b[img] = codes_of(r.cb_near, r.cb_far, img, True)

    def make_hot(level, img, cp, count, j0, j1):
        c = (r.codes_b if level else r.codes_t)[img]
        side = c.shape[0]
        ids = lax.broadcasted_iota(jnp.int32, (side, 512), 1).astype(F32)
        used = jnp.zeros((8, 512), F32)
        for j in range(j0, j1):
            hot = (c[:, 2 * j + cp : 2 * j + cp + 1] == ids).astype(F32)
            if count:
                used = used + jnp.sum(hot.reshape(side // 8, 8, 512), axis=0)
            r.hot[j * side : (j + 1) * side, :] = hot.astype(BF16)
        return r.hot[j0 * side : j1 * side, :], used

    def near_of(level, img, j0, j1):
        v = []
        used = jnp.zeros((8, 512), F32)
        for cp, table in ((0, r.book_a), (1, r.book_b)):
            hot, more = make_hot(level, img, cp, True, j0, j1)
            used = used + more
            v.append(mm_t(hot, table[level]))
        accum(r.acc_count, level, used, img)
        half = low_half(v[0][:, :128].shape)
        hi = jnp.where(half, v[0][:, :128], v[1][:, :128])
        mid = swap_halves(jnp.where(half, v[1][:, :128], v[0][:, :128]))
        lo = jnp.where(half, v[0][:, 128:], v[1][:, 128:])
        return hi, hi + mid + lo

    def add_sums(level, img, latent, j0, j1):
        hi = latent.astype(BF16).astype(F32)
        lo = latent - hi
        half = low_half(hi.shape)
        even = jnp.where(half, hi, swap_halves(lo)).astype(BF16)
        odd = jnp.where(half, swap_halves(hi), lo).astype(BF16)
        total = mm_w(even, make_hot(level, img, 0, False, j0, j1)[0])
        total = total + mm_w(odd, make_hot(level, img, 1, False, j0, j1)[0])
        accum(r.acc_sums, level, total, img)

    def put_up(img):
        u = mm(r.quant_t[img], r.up_d[...]).reshape(pairs_t, rows, 1024)
        for c in range(pairs_t):
            for cq in range(2):
                for rp in range(2):
                    lanes = (cq * 2 + rp) * 256
                    r.res[2 * c + cq, rp] = u[c, :, lanes : lanes + 256]

    def put_slots(ref, c0, even, odd):
        ref[c0 : c0 + ch, 0] = shift_rows(odd, 1).astype(BF16)
        ref[c0 : c0 + ch, 1] = even.astype(BF16)
        ref[c0 : c0 + ch, 2] = odd.astype(BF16)
        ref[c0 : c0 + ch, 3] = shift_rows(even, -1).astype(BF16)

    def taps_of(ref, c0, c1, rp):
        return jnp.concatenate([flat(ref[c0:c1, rp + t]) for t in range(3)], axis=1)

    def gather_wide(c0, c1, rp):
        before = r.wide[c0:c1, rp, :, 128:]
        after = r.wide[c0 + 2 : c1 + 2, rp, :, 128:]
        return r.wide[c0 + 1 : c1 + 1, rp, :, :128] + jnp.where(low_half(before.shape), before, after)

    def conv(img, k, then):
        for c0 in starts:
            for rp in range(2):
                y = mm_t(taps_of(r.xs.at[img], c0, c0 + ch, rp), r.b_fwd[k])
                r.wide[c0 + 1 : c0 + 1 + ch, rp] = y.reshape(ch, rows, 256)
        for c0 in starts:
            a = jnp.stack([gather_wide(c0, c0 + ch, rp) for rp in range(2)], axis=1).reshape(size, 128)
            r.act[img, span(c0), :] = a
            hidden = (a * sigmoid(a)).astype(BF16)
            y = r.res[c0 : c0 + ch].reshape(size, 256) + mm(hidden, r.wo_d[k])
            y = y.astype(BF16)
            r.low[img, span(c0), :] = y
            then(img, c0, y)

    def add_num(x):
        r.acc_num[...] += jnp.sum(x.reshape(x.shape[0] // 8, 8, 128), axis=0)

    def decode_forward(img):
        hi, full = near_of(0, img, 0, pairs_t)
        r.near_t[img] = full
        r.quant_t[img] = hi.astype(BF16)
        put_up(img)
        for c0 in starts:
            hi, full = near_of(1, img, c0, c0 + ch)
            r.near[img, span(c0), :] = full
            x = mm(hi.astype(BF16), r.from_d[...]).reshape(ch, 2, rows, 256) + r.res[c0 : c0 + ch]
            r.res[c0 : c0 + ch] = x
            put_slots(r.xs.at[img], c0, x[:, 0], x[:, 1])
        conv(img, 2, rebuild)

    def rebuild(img, c0, low):
        r.resid[img, span(c0), :] = mm_t(low, r.pix_d[1])

    def make_patches(img):
        size = 2 * rows
        picked = mm(r.sel[...], jnp.concatenate([r.pix[img], r.pix_far[img]], axis=0))
        lanes24 = lane_iota((size, 128))
        for c2 in range(pairs):
            tile = jnp.zeros((size, 128), F32)
            for i in range(4):
                start, want = 24 * c2, 24 * i
                block = start // 128 * 128
                row = picked[i * size : (i + 1) * size]
                piece = pltpu.roll(row[:, block : block + 128], (want - start % 128) % 128, 1)
                inside = min(24, 128 - start % 128)
                tile = jnp.where((lanes24 >= want) & (lanes24 < want + inside), piece, tile)
                if inside < 24:
                    piece = pltpu.roll(row[:, block + 128 : block + 256], want + inside, 1)
                    tile = jnp.where((lanes24 >= want + inside) & (lanes24 < want + 24), piece, tile)
            r.patches[img, c2 * size : (c2 + 1) * size, :] = tile.astype(BF16)

    def hidden_back(img, g, a, k):
        g_low = g.astype(BF16)
        s = sigmoid(a)
        accum(r.acc_res, k, mm_w((a * s).astype(BF16), g_low), img)
        return (mm_t(g_low, r.wo_d[k]) * (s * (1.0 + a * (1.0 - s)))).astype(BF16).astype(F32)

    def conv_back(img, k, c0):
        here, before, after = r.d_two[c0 + 1 : c0 + 1 + ch], r.d_two[c0 : c0 + ch], r.d_two[c0 + 2 : c0 + 2 + ch]
        d = jnp.concatenate([here, jnp.where(low_half(here.shape), after, before)], axis=3)
        put_slots(r.d_slots, c0, d[:, 0], d[:, 1])
        outs, total = [], None
        for rp in range(2):
            taps = taps_of(r.d_slots, c0, c0 + ch, rp)
            outs.append(mm(taps, r.b_bwd[k]).reshape(ch, rows, 256))
            more = mm_w(flat(r.xs[img, c0 : c0 + ch, rp + 1]), taps)
            total = more if total is None else total + more
        accum(r.acc_conv, k, total, img)
        return jnp.stack(outs, axis=1)

    def decode_back(img):
        limit = valid_s[first + img, image]
        lane = lane_iota((ch, 2, rows, 128))
        pixel_row = (
            8 * lax.broadcasted_iota(jnp.int32, lane.shape, 2)
            + 4 * lax.broadcasted_iota(jnp.int32, lane.shape, 1)
            + lane // 24
        )
        keep = ((pixel_row < limit) & (lane < 96)).astype(F32).reshape(size, 128)
        for c0 in starts:
            at_rows = span(c0)
            diff = keep * (r.resid[img, at_rows, :] - r.patches[img, at_rows, :].astype(F32))
            add_num(diff * diff)
            g_re = (loss_slope * diff).astype(BF16)
            accum(r.acc_pix, 1, mm_w(g_re, r.low[img, at_rows, :]), img)
            g = mm(g_re, r.pix_d[1])
            r.res[c0 : c0 + ch] = g.reshape(ch, 2, rows, 256)
            d = hidden_back(img, g, r.act[img, at_rows, :], 2)
            r.d_two[c0 + 1 : c0 + 1 + ch] = d.reshape(ch, 2, rows, 128)

    def decode_in_back(img):
        for c0 in starts:
            g = r.res[c0 : c0 + ch] + conv_back(img, 2, c0)
            r.gup[img, c0 : c0 + ch] = g
            g_low = g.reshape(size, 256).astype(BF16)
            accum(r.acc_from, Ellipsis, mm_w(r.near[img, span(c0), :].astype(BF16), g_low), img)
            r.gquant[img, span(c0), :] = mm_t(g_low, r.from_d[...])

    def dead_lines(level, img, lat_ref):
        side = pairs * (level + 1)
        images = valid_s.shape[1]
        for k in range(DEAD):
            pos = dead_source[level, k]
            col, row_all = lax.rem(pos, side), lax.div(pos, side)
            row, img_all = lax.rem(row_all, side), lax.div(row_all, side)
            mine = (lax.rem(img_all, images) == image) & (lax.div(img_all, images) == first + img)
            if level == 0:
                place = lax.div(col, 2) * rows + row
            else:
                place = lax.div(col, 2) * (2 * rows) + lax.rem(row, 2) * rows + lax.div(row, 2)
            line = lat_ref[pl.ds(place, 1), :]
            line = jnp.where(low_half(line.shape) == (lax.rem(col, 2) == 0), line, 0.0)
            line = line + swap_halves(line)
            line = jnp.where(low_half(line.shape) == (level == 0), line, 0.0)
            r.acc_dead[k : k + 1, :] += line * mine.astype(F32)

    def top_forward(img):
        for c0 in starts:
            pre = mm(r.patches[img, span(c0), :], r.pix_d[0])
            r.stem[img, c0 : c0 + ch] = (pre * sigmoid(pre)).astype(BF16).reshape(ch, 2, rows, 256)
        xs = r.xs_top.at[img]
        inputs = []
        for cq in range(2):
            x = mm(stem_blocks(img, cq), r.down_b[...])
            inputs.append(x)
            x = x.reshape(pairs_t, rows, 128)
            lanes = pl.ds(cq * 128, 128)
            xs[:, 0, :, lanes] = shift_rows(x, 1).astype(BF16)
            xs[:, 1, :, lanes] = x.astype(BF16)
            xs[:, 2, :, lanes] = shift_rows(x, -1).astype(BF16)
        r.wide[pairs_t + 1, 0] = jnp.zeros((rows, 256), F32)
        r.wide[1 : pairs_t + 1, 0] = mm_t(taps_of(xs, 0, pairs_t, 0), r.b_fwd[0]).reshape(pairs_t, rows, 256)
        a = flat(gather_wide(0, pairs_t, 0))
        r.act_t[img] = a
        hidden = (a * sigmoid(a)).astype(BF16)
        y = (jnp.concatenate(inputs, axis=1) + mm(hidden, r.wo_d[0])).astype(BF16)
        r.low_t[img] = y
        latent = mm_t(y, r.to_d[0])
        r.lat_t[...] = latent
        diff = latent - r.near_t[img]
        r.near_t[img] = diff
        add_num(COMMIT_WEIGHT * diff * diff)
        add_sums(0, img, latent, 0, pairs_t)
        dead_lines(0, img, r.lat_t)

    def stem_blocks(img, cq):
        return jnp.concatenate(
            [
                jnp.concatenate([r.stem[img, 2 * c + cq, rp] for rp in range(2)], axis=1)
                for c in range(pairs_t)
            ],
            axis=0,
        )

    def bottom_forward(img):
        put_up(img)
        for c0 in starts:
            x = r.stem[img, c0 : c0 + ch].astype(F32) + r.res[c0 : c0 + ch]
            r.res[c0 : c0 + ch] = x
            put_slots(r.xs.at[img], c0, x[:, 0], x[:, 1])
        conv(img, 1, bottom_latent)
        dead_lines(1, img, r.resid.at[0])

    def bottom_latent(img, c0, low):
        latent = mm_t(low, r.to_d[1])
        r.resid[0, span(c0), :] = latent
        diff = latent - r.near[img, span(c0), :]
        r.near[img, span(c0), :] = diff
        add_num(COMMIT_WEIGHT * diff * diff)
        add_sums(1, img, latent, c0, c0 + ch)

    def bottom_back(img):
        for c0 in starts:
            at_rows = span(c0)
            g_lat = (r.gquant[img, at_rows, :] + commit_slope * r.near[img, at_rows, :]).astype(BF16)
            accum(r.acc_to, 1, mm_w(g_lat, r.low[img, at_rows, :]), img)
            g = mm(g_lat, r.to_d[1])
            r.res[c0 : c0 + ch] = g.reshape(ch, 2, rows, 256)
            d = hidden_back(img, g, r.act[img, at_rows, :], 1)
            r.d_two[c0 + 1 : c0 + 1 + ch] = d.reshape(ch, 2, rows, 128)

    def bottom_in_back(img):
        half, size_t = ch // 2, ch // 2 * rows
        for c0 in starts:
            g = r.res[c0 : c0 + ch] + conv_back(img, 1, c0)
            r.xs[img, c0 : c0 + ch, 0] = g[:, 0].astype(BF16)
            r.xs[img, c0 : c0 + ch, 3] = g[:, 1].astype(BF16)
            total = (g + r.gup[img, c0 : c0 + ch]).astype(BF16).reshape(half, 2, 2, rows, 256)
            wide_g = jnp.concatenate(
                [total[:, cq, rp].reshape(size_t, 256) for cq in range(2) for rp in range(2)], axis=1
            )
            here = pl.ds(c0 // 2 * rows, size_t)
            accum(r.acc_up, Ellipsis, mm_w(r.quant_t[img, here, :], wide_g), img)
            g_q = mm_t(wide_g, r.up_d[...]).astype(BF16).astype(F32)
            g_lat = (g_q + commit_slope * r.near_t[img, here, :]).astype(BF16)
            accum(r.acc_to, 0, mm_w(g_lat, r.low_t[img, here, :]), img)
            r.gtop[img, here, :] = mm(g_lat, r.to_d[0])

    def top_back(img):
        g = r.gtop[img]
        d = hidden_back(img, g, r.act_t[img], 0)
        r.d_two_t[img, 1 : pairs_t + 1] = d.reshape(pairs_t, rows, 128)
        here, before, after = (
            r.d_two_t[img, 1 : pairs_t + 1],
            r.d_two_t[img, :pairs_t],
            r.d_two_t[img, 2:],
        )
        d = jnp.concatenate([here, jnp.where(low_half(here.shape), after, before)], axis=2)
        taps = jnp.concatenate(
            [flat(x).astype(BF16) for x in (shift_rows(d, 1), d, shift_rows(d, -1))], axis=1
        )
        accum(r.acc_conv, 0, mm_w(flat(r.xs_top[img, :, 1]), taps), img)
        g_low = (g + mm(taps, r.b_bwd[0])).astype(BF16)
        total = None
        sl = slope(mm(r.patches[img], r.pix_d[0])).reshape(pairs, 2, rows, 256)
        g_b = jnp.stack([r.xs[img, :, 0], r.xs[img, :, 3]], axis=1).astype(F32) * sl
        r.d_slots[:, 2:4] = g_b.astype(BF16)
        for cq in range(2):
            g_cq = g_low[:, cq * 128 : cq * 128 + 128]
            more = mm_w(stem_blocks(img, cq), g_cq)
            total = more if total is None else total + more
            g_st = mm_t(g_cq, r.down_b[...]).reshape(pairs_t, rows, 512)
            for c in range(pairs_t):
                for rp in range(2):
                    g_t = g_st[c, :, rp * 256 : rp * 256 + 256] * sl[2 * c + cq, rp]
                    r.d_slots[2 * c + cq, rp] = g_t.astype(BF16)
        accum(r.acc_down, Ellipsis, total, img)
        p = r.patches[img]
        more = mm_w(p, r.d_slots[:, 0:2].reshape(n, 256)) + mm_w(p, r.d_slots[:, 2:4].reshape(n, 256))
        accum(r.acc_pix, 0, more, img)

    def put(name, value):
        packed[at[name] : at[name] + value.shape[0], :] = value

    def pack_conv(k):
        for i in range(3):
            lanes = (2 - i) * 256
            t = jnp.transpose(r.acc_conv[k, :, lanes : lanes + 256])
            taps = (
                t[64:128, :128] + t[128:192, 128:],
                t[:64, :128] + t[64:128, 128:],
                t[:64, 128:] + t[192:, :128],
            )
            for j in range(3):
                row = at[f"conv{k}"] + (i * 3 + j) * 64
                packed[row : row + 64, :] = taps[j]
        put(f"res{k}", r.acc_res[k, :64, :128] + r.acc_res[k, 64:, 128:])

    def pack_pixel(k):
        for i in range(4):
            even = r.acc_pix[k, 24 * i : 24 * i + 12, :128]
            odd = r.acc_pix[k, 24 * i + 12 : 24 * i + 24, 128:]
            row = at[f"pixel{k}"] + i * 12
            packed[row : row + 12, :] = even + odd

    def each_image(*stages):
        def run(img, _):
            for stage in stages:
                stage(img)
            return 0

        lax.fori_loop(0, share, run, 0)

    each_image(decode_forward)
    local[0].wait()
    remote[0].wait()
    each_image(make_patches, decode_back, decode_in_back)
    pack_conv(2)
    pack_pixel(1)
    put("from0", r.acc_from[:64, :128] + r.acc_from[64:, 128:])
    begin(0)
    each_image(top_forward, between([(0, 1)], [(0, 2)]), bottom_forward)
    for level in range(2):
        sums = r.acc_sums[level, :64, :] + r.acc_sums[level, 64:, :]
        used = jnp.sum(r.acc_count[level], axis=0, keepdims=True)
        for b in range(4):
            row = at["sums"] + (level * 4 + b) * 64
            packed[row : row + 64, :] = sums[:, b * 128 : b * 128 + 128]
            row = at["count"] + level * 4 + b
            packed[row : row + 1, :] = used[:, b * 128 : b * 128 + 128]
    put("dead", r.acc_dead[...])
    put("numer", r.acc_num[...])
    steps((0, 3))
    begin(1)
    each_image(
        bottom_back,
        between([(1, 1)], [(1, 2)]),
        bottom_in_back,
        between([(0, 4)], [(0, 5)]),
    )
    pack_conv(1)
    for k in range(4):
        put(
            f"from{k + 1}",
            r.acc_up[:64, k * 128 : k * 128 + 128] + r.acc_up[64:, 512 + k * 128 : 640 + k * 128],
        )
    for k in range(2):
        put(f"to{k}", r.acc_to[k, :64, :128] + r.acc_to[k, 64:, 128:])
    begin(2)
    steps((1, 3))
    each_image(top_back, between([(2, 1), (0, 6)], []))
    pack_conv(0)
    pack_pixel(0)
    put("down", r.acc_down[...])
    begin(3)
    steps(
        (1, 4), (3, 1), (2, 2), (1, 5), (3, 2), (2, 3), (1, 6),
        (3, 3), (2, 4), (3, 4), (2, 5), (3, 5), (2, 6), (3, 6),
    )


def compute(devices, valid_rows, dead_source, pixels, ct, cb, weights, book):
    plane = devices // Z_SIZE
    _, groups, total_rows = row_layout(devices)
    share = pixels.shape[0] // 4
    vm = pl.BlockSpec(memory_space=pltpu.VMEM)
    anywhere = pl.BlockSpec(memory_space=pl.ANY)
    return pl.pallas_call(
        functools.partial(compute_kernel, devices),
        in_specs=[anywhere] * 12,
        out_specs=vm,
        scratch_shapes=scratch_of(
            share, 2 * pixels.shape[1], valid_rows, dead_source, pixels, ct, cb, [*weights, book], total_rows, plane, groups
        ),
        out_shape=jax.ShapeDtypeStruct((total_rows, 128), F32),
        compiler_params=pltpu.CompilerParams(
            collective_id=0, has_side_effects=True, vmem_limit_bytes=VMEM_LIMIT
        ),
        name="step_compute",
    )(valid_rows, dead_source, pixels, ct, cb, *weights, book)


def update_kernel(devices, dead_codes, valid_v, total, *refs):
    w, m, v = refs[0:6], refs[6:12], refs[12:18]
    ema_count, ema_sum = refs[18:20]
    norm_o, pair_o = refs[20:22]
    new_o, mom_o, sec_o, low_o = refs[22:28], refs[28:34], refs[34:40], refs[40:46]
    book_o, count_o, sum_o = refs[46:49]
    at, groups, _ = row_layout(devices)
    squares = jnp.zeros((8, 128), F32)
    for group in (0, 2, 3):
        start, size = groups[group]
        grads = total[start : start + size, :]
        squares = squares + jnp.sum((grads * grads).reshape(size // 8, 8, 128), axis=0)
    squares = jnp.sum(squares)
    norm = jnp.sqrt(jnp.full((8, 128), squares, F32))
    norm_o[0] = norm[0, 0]
    factor = (CLIP_NORM / jnp.maximum(norm, CLIP_NORM))[0, 0]
    pair_o[0] = jnp.sum(total[at["numer"] : at["numer"] + 8, :])
    pair_o[1] = 3.0 * 256.0 * jnp.sum(valid_v[...].astype(F32))

    def apply(t, index, grad):
        g = grad * factor
        first = MOMENT_ONE * m[t][index] + (1.0 - MOMENT_ONE) * g
        second = MOMENT_TWO * v[t][index] + (1.0 - MOMENT_TWO) * g * g
        step = first / (1.0 - MOMENT_ONE**STEP) / (
            jnp.sqrt(second / (1.0 - MOMENT_TWO**STEP)) + ADAM_EPSILON
        )
        weight = w[t][index]
        fresh = weight - LEARN_RATE * (step + WEIGHT_DECAY * weight)
        new_o[t][index] = fresh
        mom_o[t][index] = first
        sec_o[t][index] = second
        low_o[t][index] = fresh.astype(BF16)

    def piece(name, size, offset=0):
        return total[at[name] + offset : at[name] + offset + size, :]

    for k in range(3):
        for t in range(9):
            apply(0, (k, slice(None), pl.ds(t * 128, 128)), piece(f"conv{k}", 64, t * 64))
        apply(1, (k,), piece(f"res{k}", 64))
    for k in range(5):
        apply(2, (k,), piece(f"from{k}", 64))
    for k in range(2):
        apply(3, (k,), piece(f"to{k}", 64))
        apply(4, (k,), piece(f"pixel{k}", 48))
    for k in range(4):
        apply(5, (k,), piece("down", 128, k * 128))

    dead = jnp.concatenate(
        [piece("dead", DEAD), jnp.zeros((128 - DEAD, 128), F32)], axis=0
    )
    dead = jnp.transpose(dead)
    for level in range(2):
        for b in range(4):
            lanes = pl.ds(b * 128, 128)
            ids = lane_iota((64, 128)) + b * 128
            count = CODE_DECAY * ema_count[level : level + 1, b * 128 : b * 128 + 128] + (
                1.0 - CODE_DECAY
            ) * piece("count", 1, level * 4 + b)
            sums = CODE_DECAY * ema_sum[level, :, lanes] + (
                1.0 - CODE_DECAY
            ) * piece("sums", 64, (level * 4 + b) * 64)
            for r in range(8):
                taken = ids == dead_codes[level, r]
                count = jnp.where(taken[:1], 1.0, count)
                sums = jnp.where(taken, dead[level * 64 : level * 64 + 64, r : r + 1], sums)
            count_o[level : level + 1, b * 128 : b * 128 + 128] = count
            sum_o[level, :, lanes] = sums
            book_o[level, :, lanes] = sums / count


def update(devices, dead_codes, valid_rows, total, weights, firsts, seconds, ema_count, ema_sum):
    sds = jax.ShapeDtypeStruct
    shapes = [sds((1,), F32), sds((2,), F32)]
    for _ in range(3):
        shapes += [sds(w.shape, F32) for w in weights]
    shapes += [sds(w.shape, BF16) for w in weights]
    shapes += [sds(ema_sum.shape, F32), sds(ema_count.shape, F32), sds(ema_sum.shape, F32)]
    vm = pl.BlockSpec(memory_space=pltpu.VMEM)
    sm = pl.BlockSpec(memory_space=pltpu.SMEM)
    return pl.pallas_call(
        functools.partial(update_kernel, devices),
        out_shape=shapes,
        in_specs=[sm] + [vm] * 22,
        out_specs=[sm, sm] + [vm] * 27,
        compiler_params=pltpu.CompilerParams(vmem_limit_bytes=VMEM_LIMIT),
        name="step_update",
    )(dead_codes, valid_rows, total, *weights, *firsts, *seconds, ema_count, ema_sum)


def body(sections, devices, *args):
    pixels, codes_top, codes_bottom, valid_rows, dead_codes, dead_source = args[:6]
    weights, firsts, seconds = args[6:12], args[12:18], args[18:24]
    codebook, ema_count, ema_sum = args[24:27]
    batches, part_rows, lanes = pixels.shape
    height = lanes // 3
    parts = height // part_rows
    assert parts == 2 and sections == 2

    def turn(arrays):
        return [x.transpose(0, 2, 1) if x.shape[2] == 64 else x for x in arrays]

    weights, firsts, seconds = turn(weights), turn(firsts), turn(seconds)
    codebook, ema_sum = turn([codebook, ema_sum])
    total = compute(
        devices, valid_rows, dead_source, pixels, codes_top, codes_bottom, weights, codebook
    )
    outs = update(devices, dead_codes, valid_rows, total, weights, firsts, seconds, ema_count, ema_sum)
    outs = [x.transpose(0, 2, 1) if len(x.shape) == 3 and x.shape[1] == 64 and turned else x for x, turned in zip(outs, TURNED)]
    return (outs[0].reshape(()),) + tuple(outs[1:])


TURNED = (False, False) + (True, False, False, True, False, False) * 4 + (True, False, True)


def solution(mesh):
    return jax.shard_map(
        functools.partial(body, mesh.shape["section"], mesh.shape["dp"]),
        mesh=mesh,
        in_specs=(P(None, "dp", None),) * 3 + (P(),) * 24,
        out_specs=(P(),) * 29,
        check_vma=False,
    )
```

time: 283 us -> 84.1 us (0.30)
  waiting for transfers between devices: 127 us -> 0 us
  local copies, waits for them, and re-layouts: 40.6 us -> 0 us
  between operations: 14.2 us -> 0.86 us
  Pallas kernels: 92.9 us -> 83.1 us
  starting transfers between devices: 5.07 us -> 0 us
  other arithmetic: 3.22 us -> 0 us
    psum x1 -> x0, waiting for transfers between devices: 126 us -> none  [body(): total = lax.psum(packed, ('section', 'dp'))]
    unnamed x38 -> x0, local copies, waits for them, and re-layouts: 28.3 us -> none
    pallas_call x2, Pallas kernels: 92.9 us -> 83.1 us  [the longest x1 76.4 us: compute(): pl.pallas_call(functools.partial(compute_kernel, devices), in_specs=[anyw...]
    ppermute x3 -> x0, starting transfers between devices: 5.03 us -> none  [regroup(): piece = lax.ppermute(piece, 'dp', pairs)]
    transpose x4 -> x0, local copies, waits for them, and re-layouts: 4.99 us -> none  [the longest x1 2.51 us: code_layouts(): col = x.transpose(0, 3, 2, 1, 4).reshape(share, side * side // 2, 2)]
    another operation x5 -> x0, local copies, waits for them, and re-layouts: 3.3 us -> none  [the longest x1 2.15 us: code_layouts(): x = codes.reshape(share, side // 2, 2, side // 2, 2)]
    another operation x7 -> x0, other arithmetic: 3.22 us -> none  [the longest x6 2.63 us: regroup(): jnp.stack(ordered, axis=1).reshape(share, parts * x.shape[1], x.shape[2])]
  transfers between devices with their start and end apart: 4 -> 0, of which waited for: 1 -> 0; matrix products, arithmetic and copies ran while one was open for 9% -> 0% of each run, Pallas kernels for 0% -> 0%
where the time goes in v4:
time: 84.1 us; the launch traced here: 83.9 us
  Pallas kernels  83.1 us (99%)
  between operations  0.86 us (1%)
    pallas_call x1, Pallas kernels, compute(): pl.pallas_call(functools.partial(compute_kernel, devices), in_specs=[anyw...  76.4 us
    pallas_call x1, Pallas kernels, update(): pl.pallas_call(functools.partial(update_kernel, devices), out_shape=shape...  6.66 us

profile of v4, /device:TPU:0, one launch (start us, length us, event | category | flops | bytes accessed | tf_op | source)
XLA Modules:
  0.0 83.9 jit_solution(3672395551087932793)
XLA Ops:
  0.7 76.4 %step_compute.1.total = f32[3840,128]{1,0:T(8,128)} custom-call(s32[8,8]{1,0:T(8,128)} %valid_v.1, s32[2,8]{1,0:T(2,128)} %dead_rows.1, bf16[8,128,768]{2,1,0:T(8,128)(2,1)} %pixels.1, s32[8,16,32]{2,1,0:T(8,128)} %codes_top.1, s32[8,32,64]{2,1,0:T(8,128)} %codes_bottom.1, f32[3,64,1152]{2,1,0:T(8,128)} %bitcast.19, f32[3,64,128]{2,1,0:T(8,128)} %refs_1_.3, ...), custom_call_target="tpu_custom_call" | custom-call | tf_op jit(solution)/shard_map/step_compute/pallas_call | solution.py:828
  77.1 6.7 %step_update.1 = (f32[1]{0:T(128)}, f32[2]{0:T(128)}, f32[3,64,1152]{2,1,0:T(8,128)}, f32[3,64,128]{2,1,0:T(8,128)}, f32[5,64,128]{2,1,0:T(8,128)}, /*index=5*/f...) custom-call(s32[2,8]{1,0:T(2,128)} %dead_codes.1, ...), custom_call_target="tpu_custom_call" | custom-call | tf_op jit(solution)/shard_map/step_update/pallas_call | solution.py:923

commit v5 on v4

--- a/solution.py
+++ b/solution.py
@@ -29,14 +29,21 @@
     (("conv2", 576), ("res2", 64), ("from0", 64), ("pixel1", 48)),
     (("sums", 512), ("count", 8), ("dead", 8), ("numer", 8)),
     (("conv1", 576), ("res1", 64), ("from1", 64), ("from2", 64), ("from3", 64), ("from4", 64), ("to1", 64), ("to0", 64)),
-    (("conv0", 576), ("res0", 64), ("pixel0", 48), ("down", 512)),
+    (("conv0", 576), ("res0", 64), ("pixel0", 48)),
+    (("down", 512),),
 )
+
+
+def groups_of(devices):
+    if devices > 16:
+        return GROUPS[:-2] + (GROUPS[-2] + GROUPS[-1],)
+    return GROUPS
 
 
 def row_layout(devices):
     multiple = 16 * devices
     at, groups, row = {}, [], 0
-    for group in GROUPS:
+    for group in groups_of(devices):
         start = row
         for name, size in group:
             at[name] = row
@@ -98,46 +105,40 @@
     return pltpu.roll(x, 64, len(x.shape) - 1)
 
 
-def partners_of(plane):
+def exchange_stages(plane):
     s = lax.axis_index("section")
     d = lax.axis_index("dp")
     z, q = lax.div(d, plane), lax.rem(d, plane)
-    peer = (1 - s, d)
-    mates = [lax.rem(q + k, plane) for k in range(plane)]
-    levels = [lax.rem(z + k, Z_SIZE) for k in range(Z_SIZE)]
-    partners = [peer] + [(s, z * plane + m) for m in mates[1:]] + [(s, l * plane + q) for l in levels[1:]]
-    return s, z, q, peer, mates, levels, partners
+    mates = [(s, z * plane + lax.rem(q + k, plane)) for k in range(1, plane)]
+    levels = [(s, lax.rem(z + k, Z_SIZE) * plane + q) for k in range(1, Z_SIZE)]
+    return [(s, [(1 - s, d)]), (q, mates), (z, levels)]
 
 
 class Reduction:
-    def __init__(self, plane, base, total, x, out, one, two, sums, three, acc, ssem, rsem):
-        half, part = total // 2, total // 2 // plane
-        chunk = part // Z_SIZE
-        s, z, q, peer, mates, levels, _ = partners_of(plane)
-        mine = base + s * half
-        self.x, self.out, self.one, self.two, self.sums, self.three, self.acc = x, out, one, two, sums, three, acc
-        self.plane, self.part, self.chunk = plane, part, chunk
-        self.own = mine + q * part + z * chunk
-        self.z_row = z * chunk
-        self.mates, self.mine = mates, mine
-        to_mates = [(s, z * plane + m) for m in mates[1:]]
-        to_levels = [(s, l * plane + q) for l in levels[1:]]
-        moves = [(self.rows(x, base + (1 - s) * half, half), one, peer)]
-        moves += [(sums.at[k], two.at[k], to) for k, to in enumerate(to_mates)]
-        moves += [
-            (self.rows(acc, l * chunk, chunk), three.at[k], to)
-            for k, (l, to) in enumerate(zip(levels[1:], to_levels))
-        ]
-        own = self.rows(out, self.own, chunk)
-        moves += [(own, own, to) for to in to_levels]
-        own = self.rows(out, mine + q * part, part)
-        moves += [(own, own, to) for to in to_mates]
-        own = self.rows(out, mine, half)
-        moves += [(own, own, peer)]
-        self.moves, self.ssem, self.rsem = moves, ssem, rsem
-        a, b = plane - 1, Z_SIZE - 1
-        stops = [0, 1, 1 + a, 1 + a + b, 1 + a + 2 * b, 1 + 2 * a + 2 * b, 2 + 2 * a + 2 * b]
-        self.stage = [range(lo, hi) for lo, hi in zip(stops, stops[1:])]
+    def __init__(self, plane, base, total, x, out, *refs):
+        stages = exchange_stages(plane)
+        landed, (ssem, rsem) = refs[: len(stages)], refs[len(stages) :]
+        self.x, self.out, self.landed, self.ssem, self.rsem = x, out, landed, ssem, rsem
+        self.moves, self.stage, self.block = [], [], []
+        start, size = base, total
+        back = []
+        for (place, members), buffer in zip(stages, landed):
+            count = len(members) + 1
+            back.append((start, size, place, members))
+            size = size // count
+            first = len(self.moves)
+            for k, to in enumerate(members):
+                theirs = lax.rem(place + k + 1, count)
+                self.moves.append((self.rows(x, start + theirs * size, size), buffer.at[k], to))
+            self.stage.append(range(first, len(self.moves)))
+            start = start + place * size
+            self.block.append((start, size, len(members)))
+        for _, _, _, members in reversed(back):
+            first = len(self.moves)
+            own = self.rows(out, start, size)
+            self.moves += [(own, own, to) for to in members]
+            self.stage.append(range(first, len(self.moves)))
+            start, size = back[len(stages) - 1 - (len(self.stage) - len(stages) - 1)][:2]
 
     def rows(self, ref, start, size):
         return ref.at[pl.ds(pl.multiple_of(start, 8), size)]
@@ -149,31 +150,17 @@
         )
 
     def step(self, number):
+        stages = len(self.landed)
         if number > 0:
             for k in self.stage[number - 1]:
                 self.copy(k).wait_recv()
-        part, chunk = self.part, self.chunk
-        if number == 1:
-            for k in list(range(1, self.plane)) + [0]:
-                at = self.mates[k] * part
-                value = self.rows(self.x, self.mine + at, part)[...] + self.rows(self.one, at, part)[...]
-                if k == 0:
-                    self.acc[...] = value
-                else:
-                    self.sums[k - 1] = value
-                    self.copy(k).start()
-            return
-        if number == 2:
-            value = self.acc[...]
-            for j in range(self.plane - 1):
-                value = value + self.two[j]
-            self.acc[...] = value
-        if number == 3:
-            value = self.rows(self.acc, self.z_row, chunk)[...]
-            for k in range(1, Z_SIZE):
-                value = value + self.three[k - 1]
-            self.rows(self.out, self.own, chunk)[...] = value
-        if number < 6:
+        if 0 < number <= stages:
+            start, size, others = self.block[number - 1]
+            value = self.rows(self.x, start, size)[...]
+            for k in range(others):
+                value = value + self.landed[number - 1][k]
+            self.rows(self.out if number == stages else self.x, start, size)[...] = value
+        if number < 2 * stages:
             for k in self.stage[number]:
                 self.copy(k).start()
         else:
@@ -182,22 +169,15 @@
 
 
 def reduce_scratch(plane, total):
-    part = total // 2 // plane
-    chunk = part // Z_SIZE
-    v = pltpu.VMEM
-    count = 2 + 2 * (plane - 1) + 2 * (Z_SIZE - 1)
-    return [
-        v((total // 2, 128), F32),
-        v((plane - 1, part, 128), F32),
-        v((plane - 1, part, 128), F32),
-        v((Z_SIZE - 1, chunk, 128), F32),
-        v((part, 128), F32),
-        pltpu.SemaphoreType.DMA((count,)),
-        pltpu.SemaphoreType.DMA((count,)),
-    ]
-
-
-REDUCE_REFS = 7
+    scratch, size, moves = [], total, 0
+    for count in (2, plane, Z_SIZE):
+        size = size // count
+        moves += 2 * (count - 1)
+        scratch.append(pltpu.VMEM((count - 1, size, 128), F32))
+    return scratch + [pltpu.SemaphoreType.DMA((moves,)), pltpu.SemaphoreType.DMA((moves,))]
+
+
+REDUCE_REFS = 5
 SCRATCH = (
     "b_fwd", "b_bwd", "wo_d", "from_d", "to_d", "up_d", "pix_d", "down_b", "book_a", "book_b", "sel", "hot",
     "near", "near_t", "quant_t", "patches", "stem", "xs", "xs_top", "wide", "res", "act", "act_t", "low",
@@ -295,7 +275,8 @@
     plane = devices // Z_SIZE
     at, groups, _ = row_layout(devices)
     packed = r.packed
-    section, _, _, _, _, _, partners = partners_of(plane)
+    section = lax.axis_index("section")
+    partners = [to for _, members in exchange_stages(plane) for to in members]
     device = lax.axis_index("dp")
     part, image = lax.rem(device, 2), lax.div(device, 2)
     share = r.pix.shape[0]
@@ -356,7 +337,7 @@
 
     def begin(group):
         start, size = groups[group]
-        used = sum(size for _, size in GROUPS[group])
+        used = sum(size for _, size in groups_of(devices)[group])
         if size > used:
             packed[start + used : start + size, :] = jnp.zeros((size - used, 128), F32)
         reductions[group].step(0)
@@ -813,10 +794,17 @@
     pack_pixel(0)
     put("down", r.acc_down[...])
     begin(3)
-    steps(
-        (1, 4), (3, 1), (2, 2), (1, 5), (3, 2), (2, 3), (1, 6),
-        (3, 3), (2, 4), (3, 4), (2, 5), (3, 5), (2, 6), (3, 6),
-    )
+    if len(groups) > 4:
+        begin(4)
+        steps(
+            (1, 4), (3, 1), (4, 1), (2, 2), (3, 2), (1, 5), (4, 2), (2, 3), (3, 3), (1, 6), (4, 3), (2, 4),
+            (3, 4), (4, 4), (2, 5), (3, 5), (4, 5), (2, 6), (3, 6), (4, 6),
+        )
+    else:
+        steps(
+            (1, 4), (3, 1), (2, 2), (1, 5), (3, 2), (2, 3), (1, 6),
+            (3, 3), (2, 4), (3, 4), (2, 5), (3, 5), (2, 6), (3, 6),
+        )
 
 
 def compute(devices, valid_rows, dead_source, pixels, ct, cb, weights, book):
@@ -848,8 +836,7 @@
     book_o, count_o, sum_o = refs[46:49]
     at, groups, _ = row_layout(devices)
     squares = jnp.zeros((8, 128), F32)
-    for group in (0, 2, 3):
-        start, size = groups[group]
+    for start, size in groups[:1] + groups[2:]:
         grads = total[start : start + size, :]
         squares = squares + jnp.sum((grads * grads).reshape(size // 8, 8, 128), axis=0)
     squares = jnp.sum(squares)

time: 84.1 us -> 83.1 us (0.988)
  Pallas kernels: 83.1 us -> 82.1 us
    pallas_call x1, Pallas kernels: 76.4 us -> 75.5 us  [compute(): pl.pallas_call(functools.partial(compute_kernel, devices), in_specs=[anyw...]
where the time goes in v5:
time: 83.1 us; the launch traced here: 83 us
  Pallas kernels  82.1 us (99%)
  between operations  0.86 us (1%)
    pallas_call x1, Pallas kernels, compute(): pl.pallas_call(functools.partial(compute_kernel, devices), in_specs=[anyw...  75.5 us
    pallas_call x1, Pallas kernels, update(): pl.pallas_call(functools.partial(update_kernel, devices), out_shape=shape...  6.6 us

profile of v5, /device:TPU:0, one launch (start us, length us, event | category | flops | bytes accessed | tf_op | source)
XLA Modules:
  0.0 83.0 jit_solution(5109017491812690870)
XLA Ops:
  0.7 75.5 %step_compute.1.total = f32[3840,128]{1,0:T(8,128)} custom-call(s32[8,8]{1,0:T(8,128)} %valid_v.1, s32[2,8]{1,0:T(2,128)} %dead_rows.1, bf16[8,128,768]{2,1,0:T(8,128)(2,1)} %pixels.1, s32[8,16,32]{2,1,0:T(8,128)} %codes_top.1, s32[8,32,64]{2,1,0:T(8,128)} %codes_bottom.1, f32[3,64,1152]{2,1,0:T(8,128)} %bitcast.19, f32[3,64,128]{2,1,0:T(8,128)} %refs_1_.3, ...), custom_call_target="tpu_custom_call" | custom-call | tf_op jit(solution)/shard_map/step_compute/pallas_call | solution.py:816
  76.2 6.6 %step_update.1 = (f32[1]{0:T(128)}, f32[2]{0:T(128)}, f32[3,64,1152]{2,1,0:T(8,128)}, f32[3,64,128]{2,1,0:T(8,128)}, f32[5,64,128]{2,1,0:T(8,128)}, /*index=5*/f...) custom-call(s32[2,8]{1,0:T(2,128)} %dead_codes.1, ...), custom_call_target="tpu_custom_call" | custom-call | tf_op jit(solution)/shard_map/step_update/pallas_call | solution.py:910
